TPU v7x, 32 devices: a whole 2x2x4 slice. The times are simulated.
32 devices in a mesh: seq: 32 (over z, y, x, core).
Axes of the slice: x: 2, y: 2, z: 4, core: 2. Of those that a mesh axis runs over, the one named last changes fastest.
Arguments:
- hidden_in: bfloat16 [2, 4096, 768], P(None, 'seq'), may hold values from -6 to 6
- norm_gain: float32 [2, 768], replicated, may hold values from 0.1 to 1.9
- in_weight: bfloat16 [2, 768, 3072], replicated, may hold values from -0.21875 to 0.21875
- conv_weight: float32 [2, 1536, 4], replicated, may hold values from -3 to 3
- conv_bias: float32 [2, 1536], replicated, may hold values from -3 to 3
- xproj_weight: bfloat16 [2, 1536, 80], replicated, may hold values from -0.15625 to 0.15625
- dtproj_weight: bfloat16 [2, 48, 1536], replicated, may hold values from -0.875 to 0.875
- dt_bias: float32 [2, 1536], replicated, may hold values from -4.5 to -2.5
- a_log: float32 [2, 1536, 16], replicated, as said below
- skip_gain: float32 [2, 1536], replicated, may hold values from 0.5 to 1.5
- out_weight: bfloat16 [2, 1536, 768], replicated, may hold values from -0.15625 to 0.15625
- hidden_grad: bfloat16 [2, 4096, 768], P(None, 'seq'), may hold values from -6 to 6
Outputs:
- hidden_out: bfloat16 [2, 4096, 768], P(None, 'seq')
- input_grad: bfloat16 [2, 4096, 768], P(None, 'seq')
- grad_norm_gain: float32 [2, 768], replicated
- grad_in_weight: float32 [2, 768, 3072], replicated
- grad_conv_weight: float32 [2, 1536, 4], replicated
- grad_conv_bias: float32 [2, 1536], replicated
- grad_xproj_weight: float32 [2, 1536, 80], replicated
- grad_dtproj_weight: float32 [2, 48, 1536], replicated
- grad_dt_bias: float32 [2, 1536], replicated
- grad_a_log: float32 [2, 1536, 16], replicated
- grad_skip_gain: float32 [2, 1536], replicated
- grad_out_weight: float32 [2, 1536, 768], replicated
Inputs may be any that keep to these rules, and one draw needn't show every extreme that they name: `a_log`: logarithms of positive decay rates.
All inputs are finite; a program needn't handle non-finite values.
Results may differ from a plain program's by a relative error of at most 0.018.
The roundings to bfloat16 on the way count: a program that leaves them out, or rounds other values in their place, can miss the bound.
Values may be sent and summed in bfloat16 or wider, within the bound.
No kernel may reach another device: no remote copies, remote signals or barrier semaphores. Data moves between devices by JAX's collectives and lax.ppermute only.
A program may use at most 320 MiB of HBM per device.

v0:
```python
import functools
import math

import jax
import jax.numpy as jnp
from jax import lax
from jax.experimental import pallas as pl
from jax.experimental.pallas import tpu as pltpu
from jax.sharding import PartitionSpec as P

BF16 = jnp.bfloat16
F32 = jnp.float32
LOG2E = 1.4426950408889634
LN2 = 0.6931471805599453
AXIS = "seq"
XD = 128
EXTRA = 256
CHUNK = 256
UNROLL = 8
HALO = 8


def full(array):
    nd = len(array.shape)
    return pl.BlockSpec(array.shape, lambda i, nd=nd: (0,) * nd)


def part(shape, index):
    return pl.BlockSpec(shape, lambda i, index=index: index)


def run(kernel, outs, ins, scratch=(), flops=0, moved=None):
    arrays, specs = [], []
    for item in ins:
        if isinstance(item, tuple):
            arrays.append(item[0])
            specs.append(item[1])
        else:
            arrays.append(item)
            specs.append(full(item))
    if moved is None:
        moved = sum(math.prod(o.shape) * o.dtype.itemsize for o in outs) * 2
    return pl.pallas_call(
        kernel,
        grid=(1,),
        in_specs=specs,
        out_specs=[full(o) for o in outs],
        out_shape=outs,
        scratch_shapes=list(scratch),
        compiler_params=pltpu.CompilerParams(vmem_limit_bytes=58 * 1024 * 1024),
        cost_estimate=pl.CostEstimate(flops=flops, bytes_accessed=moved, transcendentals=0),
    )(*arrays)


def shape(dims, dtype):
    return jax.ShapeDtypeStruct(dims, dtype)


def dot(a, b):
    return jnp.dot(a, b, preferred_element_type=F32)


def dot_t(a, b):
    return lax.dot_general(a, b, (((1,), (1,)), ((), ())), preferred_element_type=F32)


def dot_rows(a, b):
    return lax.dot_general(a, b, (((0,), (0,)), ((), ())), preferred_element_type=F32)


def sigmoid(v):
    return 1.0 / (1.0 + jnp.exp(-v))


def softplus(v):
    return jnp.maximum(v, 0.0) + jnp.log1p(jnp.exp(-jnp.abs(v)))


def slope(v):
    s = sigmoid(v)
    return s * (1.0 + v * (1.0 - s))


def wide(block, lanes):
    return jnp.concatenate([block] * (lanes // block.shape[1]), axis=1)


def rows_of_sums(parts):
    row = lax.broadcasted_iota(jnp.int32, parts[0].shape, 0)
    m4, m2, m1 = row < 4, (row & 2) == 0, (row & 1) == 0
    q = []
    for i in range(4):
        first = jnp.where(m4, parts[i], parts[i + 4])
        other = jnp.where(m4, parts[i + 4], parts[i])
        q.append(first + pltpu.roll(other, 4, 0))
    s = []
    for i in range(2):
        s.append(
            jnp.where(
                m2, q[i] + pltpu.roll(q[i], 6, 0), q[i + 2] + pltpu.roll(q[i + 2], 2, 0)
            )
        )
    return jnp.where(m1, s[0] + pltpu.roll(s[0], 7, 0), s[1] + pltpu.roll(s[1], 1, 0))


def fold(block):
    out = block[0:8]
    for k in range(8, block.shape[0], 8):
        out = out + block[k : k + 8]
    return out


def fold_lanes(block):
    out = block[:, 0:128]
    for k in range(128, block.shape[1], 128):
        out = out + block[:, k : k + 128]
    return out


def normed_of(x, gain):
    rinv = lax.rsqrt(jnp.mean(x * x, axis=-1, keepdims=True) + 1e-05)
    return (x * rinv * gain).astype(BF16)


def fill_table(xdf_ref, lhs_ref, bc_ref, rank, states):
    rows = xdf_ref.shape[0]
    n_i = lax.broadcasted_iota(jnp.int32, (states, XD), 0)
    lane = lax.broadcasted_iota(jnp.int32, (states, XD), 1)
    mask = ((lane == rank + n_i) | (lane == rank + states + n_i)).astype(F32)

    def body(i, carry):
        for j in range(UNROLL):
            t = i * UNROLL + j
            line = xdf_ref[pl.ds(t, 1), :]
            lhs_ref[pl.ds(pl.multiple_of(t * states, states), states), :] = (
                line * mask
            ).astype(BF16)
        return carry

    lax.fori_loop(0, rows // UNROLL, body, 0)
    k_i = lax.broadcasted_iota(jnp.int32, (XD, 256), 0)
    c_i = lax.broadcasted_iota(jnp.int32, (XD, 256), 1)
    low = rank + jnp.where(c_i >= 128, states, 0)
    pick = ((k_i >= low) & (k_i < low + states)).astype(BF16)
    bc_ref[...] = dot(lhs_ref[...], pick)


def state_rows(t, states):
    return pl.ds(pl.multiple_of(t * states, states), states)


def scan_ends(dt_ref, dtu_ref, bc_ref, a2_ref, end_ref):
    rows, inner = dt_ref.shape
    states = a2_ref.shape[0]

    def chunk(c, carry):
        lanes = pl.ds(pl.multiple_of(c * CHUNK, CHUNK), CHUNK)
        a2 = a2_ref[:, lanes]

        def body(i, h):
            for j in range(UNROLL):
                t = i * UNROLL + j
                a = jnp.exp2(dt_ref[pl.ds(t, 1), lanes] * a2)
                b = wide(bc_ref[state_rows(t, states), 0:128], CHUNK)
                h = a * h + dtu_ref[pl.ds(t, 1), lanes] * b
            return h

        end_ref[:, lanes] = lax.fori_loop(
            0, rows // UNROLL, body, jnp.zeros((states, CHUNK), F32)
        )
        return carry

    lax.fori_loop(0, inner // CHUNK, chunk, 0)


def scan_back_ends(dt_ref, dy_ref, bc_ref, a2_ref, end_ref):
    rows, inner = dt_ref.shape
    states = a2_ref.shape[0]

    def chunk(c, carry):
        lanes = pl.ds(pl.multiple_of(c * CHUNK, CHUNK), CHUNK)
        a2 = a2_ref[:, lanes]

        def body(i, back):
            for j in range(UNROLL):
                t = rows - 1 - (i * UNROLL + j)
                a = jnp.exp2(dt_ref[pl.ds(t, 1), lanes] * a2)
                c_row = wide(bc_ref[state_rows(t, states), 128:256], CHUNK)
                back = a * (dy_ref[pl.ds(t, 1), lanes] * c_row + back)
            return back

        end_ref[:, lanes] = lax.fori_loop(
            0, rows // UNROLL, body, jnp.zeros((states, CHUNK), F32)
        )
        return carry

    lax.fori_loop(0, inner // CHUNK, chunk, 0)


def scan_forward(dt_ref, dtu_ref, bc_ref, a2_ref, h_in_ref, y_ref):
    rows, inner = dt_ref.shape
    states = a2_ref.shape[0]

    def chunk(c, carry):
        lanes = pl.ds(pl.multiple_of(c * CHUNK, CHUNK), CHUNK)
        a2 = a2_ref[:, lanes]

        def body(i, h):
            parts = []
            for j in range(UNROLL):
                t = i * UNROLL + j
                a = jnp.exp2(dt_ref[pl.ds(t, 1), lanes] * a2)
                both = bc_ref[state_rows(t, states), :]
                h = a * h + dtu_ref[pl.ds(t, 1), lanes] * wide(both[:, 0:128], CHUNK)
                parts.append(fold(h * wide(both[:, 128:256], CHUNK)))
            y_ref[pl.ds(pl.multiple_of(i * UNROLL, UNROLL), UNROLL), lanes] = rows_of_sums(
                parts
            )
            return h

        lax.fori_loop(0, rows // UNROLL, body, h_in_ref[:, lanes])
        return carry

    lax.fori_loop(0, inner // CHUNK, chunk, 0)


def scan_both(
    dt_ref,
    dtu_ref,
    dy_ref,
    bc_ref,
    a2_ref,
    h_in_ref,
    g_in_ref,
    y_ref,
    sgb_ref,
    sqa_ref,
    rate_ref,
    db_ref,
    dc_ref,
    a_s,
    ah_s,
):
    rows, inner = dt_ref.shape
    states = a2_ref.shape[0]
    db_ref[...] = jnp.zeros(db_ref.shape, F32)
    dc_ref[...] = jnp.zeros(dc_ref.shape, F32)

    def chunk(c, carry):
        lanes = pl.ds(pl.multiple_of(c * CHUNK, CHUNK), CHUNK)
        a2 = a2_ref[:, lanes]

        def ahead(i, h):
            parts = []
            for j in range(UNROLL):
                t = i * UNROLL + j
                at = state_rows(t, states)
                a = jnp.exp2(dt_ref[pl.ds(t, 1), lanes] * a2)
                both = bc_ref[at, :]
                ah = a * h
                a_s[at, :] = a
                ah_s[at, :] = ah
                h = ah + dtu_ref[pl.ds(t, 1), lanes] * wide(both[:, 0:128], CHUNK)
                dc_ref[at, :] += fold_lanes(h * dy_ref[pl.ds(t, 1), lanes])
                if y_ref is not None:
                    parts.append(fold(h * wide(both[:, 128:256], CHUNK)))
            if y_ref is not None:
                y_ref[pl.ds(pl.multiple_of(i * UNROLL, UNROLL), UNROLL), lanes] = (
                    rows_of_sums(parts)
                )
            return h

        lax.fori_loop(0, rows // UNROLL, ahead, h_in_ref[:, lanes])

        def retreat(i, carried):
            back, rate = carried
            block = rows // UNROLL - 1 - i
            gbs, qas = [None] * UNROLL, [None] * UNROLL
            for j in reversed(range(UNROLL)):
                t = block * UNROLL + j
                at = state_rows(t, states)
                both = bc_ref[at, :]
                g = dy_ref[pl.ds(t, 1), lanes] * wide(both[:, 128:256], CHUNK) + back
                q = g * ah_s[at, :]
                gbs[j] = fold(g * wide(both[:, 0:128], CHUNK))
                qas[j] = fold(q * a2)
                rate = rate + q * dt_ref[pl.ds(t, 1), lanes]
                db_ref[at, :] += fold_lanes(g * dtu_ref[pl.ds(t, 1), lanes])
                back = a_s[at, :] * g
            here = pl.ds(pl.multiple_of(block * UNROLL, UNROLL), UNROLL)
            sgb_ref[here, lanes] = rows_of_sums(gbs)
            sqa_ref[here, lanes] = rows_of_sums(qas)
            return back, rate

        _, rate = lax.fori_loop(
            0,
            rows // UNROLL,
            retreat,
            (g_in_ref[:, lanes], jnp.zeros((states, CHUNK), F32)),
        )
        rate_ref[:, lanes] = rate
        return carry

    lax.fori_loop(0, inner // CHUNK, chunk, 0)


def packed(state, total, wide_s):
    inner = total.shape[1]
    high = total.astype(BF16).astype(F32)
    rest = total - high
    wide_s[:, 0:inner] = state
    wide_s[:, inner:] = jnp.zeros((state.shape[0], EXTRA), F32)
    for k in range(inner // 128):
        wide_s[k : k + 1, inner : inner + 128] = high[:, k * 128 : (k + 1) * 128]
        wide_s[k : k + 1, inner + 128 : inner + 256] = rest[:, k * 128 : (k + 1) * 128]
    return wide_s[...].astype(BF16)


def unpack_total(wide_ref, m, total_ref, inner):
    for k in range(inner // 128):
        total_ref[m, 0:1, k * 128 : (k + 1) * 128] = (
            wide_ref[m, k : k + 1, inner : inner + 128]
            + wide_ref[m, k : k + 1, inner + 128 : inner + 256]
        )


def join_runs(states_ref, totals_ref, a2, digit, group, backward):
    inner = a2.shape[1]
    before = jnp.zeros(a2.shape, F32)
    entire = jnp.zeros(a2.shape, F32)
    sum_before = jnp.zeros((1, inner), F32)
    sum_entire = jnp.zeros((1, inner), F32)
    order = reversed(range(group)) if backward else range(group)
    for p in order:
        m = jnp.bitwise_xor(digit, p)
        state = states_ref[m, :, 0:inner]
        total = totals_ref[m, 0:1, :]
        through = jnp.exp2(total * a2)
        counts = (p > digit) if backward else (p < digit)
        before = jnp.where(counts, through * before + state, before)
        sum_before = jnp.where(counts, sum_before + total, sum_before)
        entire = through * entire + state
        sum_entire = sum_entire + total
    return before, sum_before, entire, sum_entire


def k_in(x_ref, g_ref, w_ref, n_ref, xc_ref, tail_ref):
    normed = normed_of(x_ref[...], g_ref[...])
    n_ref[...] = normed
    xc = dot(normed, w_ref[...]).astype(BF16)
    xc_ref[...] = xc
    tail_ref[...] = xc.astype(F32)[xc.shape[0] - HALO :, :]


def k_gate(n_ref, w_ref, z_ref):
    z_ref[...] = dot(n_ref[...], w_ref[...]).astype(BF16)


def k_dgated(e_ref, w_ref, out_ref):
    out_ref[...] = dot_t(e_ref[...], w_ref[...])


def conv_of(ext_s, halo_ref, xc_ref, cw_ref, cb_ref):
    rows = xc_ref.shape[0]
    taps = cw_ref.shape[0]
    ext_s[0:HALO, :] = halo_ref[...]
    ext_s[HALO:, :] = xc_ref[...].astype(F32)
    out = cb_ref[...]
    for k in range(taps):
        first = HALO - (taps - 1) + k
        out = out + cw_ref[k : k + 1, :] * ext_s[first : first + rows, :]
    return out


def k_local(
    rank, both, *refs
):
    refs = list(refs)
    halo, xc, cw, cb, xw, dw, db, a2 = refs[:8]
    refs = refs[8:]
    if both:
        dgated, z = refs[:2]
        refs = refs[2:]
    u_ref, xd_ref, v_ref, pay_ref = refs[:4]
    refs = refs[4:]
    if both:
        dy_ref = refs[0]
        refs = refs[1:]
    ext_s, dt_s, dtu_s, xdf_s, lhs_s, bc_s, end_s, wide_s = refs
    states = a2.shape[0]
    conv = conv_of(ext_s, halo, xc, cw, cb)
    u = (conv * sigmoid(conv)).astype(BF16)
    u_ref[...] = u
    xd = dot(u, xw[...]).astype(BF16)
    xd_ref[...] = xd
    xdf_s[...] = xd.astype(F32)
    v = dot(xd, dw[...]) + db[...]
    v_ref[...] = v
    dt = softplus(v)
    dt_s[...] = dt
    dtu_s[...] = dt * u.astype(F32)
    total = jnp.sum(dt, axis=0, keepdims=True)
    fill_table(xdf_s, lhs_s, bc_s, rank, states)
    scan_ends(dt_s, dtu_s, bc_s, a2, end_s)
    pay_ref[0:states, :] = packed(end_s[...], total, wide_s)
    if both:
        zf = z[...].astype(F32)
        dy_ref[...] = dgated[...] * (zf * sigmoid(zf))
        scan_back_ends(dt_s, dy_ref, bc_s, a2, end_s)
        pay_ref[states:, :] = packed(end_s[...], total, wide_s)


def k_join(group, nextgroup, mode, digits, *refs):
    refs = list(refs)
    received, refs = refs[:group], refs[group:]
    a2_ref, refs = refs[0], refs[1:]
    kinds = list(mode)
    n_pay = (nextgroup - 1) if (len(kinds) == 2 and nextgroup) else 1
    pays, refs = refs[:n_pay], refs[n_pay:]
    befores, refs = refs[: len(kinds)], refs[len(kinds) :]
    sums, refs = refs[: len(kinds)], refs[len(kinds) :]
    states_s, totals_s, wide_s = refs
    states, inner = a2_ref.shape
    digit = digits[0]
    nextdigit = digits[1]
    out = []
    for i in range(len(kinds)):
        for m in range(group):
            states_s[m] = received[m][i * states : (i + 1) * states, :].astype(F32)
            if i == 0:
                unpack_total(states_s, m, totals_s, inner)
        before, sum_before, entire, sum_entire = join_runs(
            states_s, totals_s, a2_ref[...], digit, group, kinds[i] == "b"
        )
        befores[i][...] = before
        sums[i][...] = sum_before
        out.append(packed(entire, sum_entire, wide_s))
    if len(kinds) == 2 and nextgroup:
        for m in range(1, nextgroup):
            ahead = jnp.bitwise_xor(nextdigit, m) > nextdigit
            pays[m - 1][...] = jnp.where(ahead, out[0].astype(F32), out[1].astype(F32)).astype(
                BF16
            )
    else:
        for i in range(len(kinds)):
            pays[0][i * states : (i + 1) * states, :] = out[i]


def entering(received, a2_ref, digit, befores, sums, states_s, totals_s, backward):
    states, inner = a2_ref.shape
    group = len(received) + 1
    states_s[0] = jnp.zeros(states_s.shape[1:], F32)
    for m in range(group):
        if m:
            states_s[m] = received[m - 1][...].astype(F32)
        unpack_total(states_s, m, totals_s, inner)
    value, _, _, _ = join_runs(states_s, totals_s, a2_ref[...], digit, group, backward)
    for before, total in reversed(list(zip(befores, sums))):
        value = jnp.exp2(total[...] * a2_ref[...]) * value + before[...]
    return value


def k_mix(rank, n_recv, n_low, digits, *refs):
    refs = list(refs)
    received, refs = refs[:n_recv], refs[n_recv:]
    befores, refs = refs[:n_low], refs[n_low:]
    sums, refs = refs[:n_low], refs[n_low:]
    a2, u_ref, v_ref, xd_ref, z_ref, x_ref, sk_ref, ow_ref, g_ref, iw_ref = refs[:10]
    refs = refs[10:]
    y_ref, gated_ref, x1_ref, n_ref, xc_ref, tail_ref, h_in_ref = refs[:7]
    dt_s, dtu_s, xdf_s, lhs_s, bc_s, states_s, totals_s = refs[7:]
    states = a2.shape[0]
    h_in_ref[...] = entering(received, a2, digits[0], befores, sums, states_s, totals_s, False)
    uf = u_ref[...].astype(F32)
    dt = softplus(v_ref[...])
    dt_s[...] = dt
    dtu_s[...] = dt * uf
    xdf_s[...] = xd_ref[...].astype(F32)
    fill_table(xdf_s, lhs_s, bc_s, rank, states)
    scan_forward(dt_s, dtu_s, bc_s, a2, h_in_ref, y_ref)
    y = y_ref[...] + sk_ref[...] * u_ref[...].astype(F32)
    y_ref[...] = y
    zf = z_ref[...].astype(F32)
    gated = (y * (zf * sigmoid(zf))).astype(BF16)
    gated_ref[...] = gated
    x1 = x_ref[...] + dot(gated, ow_ref[...])
    x1_ref[...] = x1
    normed = normed_of(x1, g_ref[...])
    n_ref[...] = normed
    xc = dot(normed, iw_ref[...]).astype(BF16)
    xc_ref[...] = xc
    tail_ref[...] = xc.astype(F32)[xc.shape[0] - HALO :, :]


def k_back(rank, n_recv, n_low, last, digits, *refs):
    refs = list(refs)
    received, refs = refs[:n_recv], refs[n_recv:]
    kinds = 2 if last else 1
    befores, refs = refs[: n_low * kinds], refs[n_low * kinds :]
    sums, refs = refs[: n_low * kinds], refs[n_low * kinds :]
    a2, u_ref, v_ref, xd_ref, dy_ref, halo, xc, cw, cb, xw, dw, sk_ref = refs[:12]
    refs = refs[12:]
    if last:
        y_ref = refs[0]
        refs = refs[1:]
    else:
        h_in_ref = refs[0]
        refs = refs[1:]
        y_ref = None
    dconv_ref, head_ref, small_ref = refs[:3]
    refs = refs[3:]
    (
        dt_s,
        dtu_s,
        xdf_s,
        lhs_s,
        bc_s,
        states_s,
        totals_s,
        ext_s,
        sgb_s,
        sqa_s,
        rate_s,
        db_s,
        dc_s,
        a_s,
        ah_s,
        g_s,
        h_s,
    ) = refs
    states = a2.shape[0]
    rows, inner = u_ref.shape
    low_f, low_b = befores[:n_low], befores[-n_low:]
    sum_f, sum_b = sums[:n_low], sums[-n_low:]
    if last:
        h_s[...] = entering(received, a2, digits[0], low_f, sum_f, states_s, totals_s, False)
        h_in_ref = h_s
    g_s[...] = entering(received, a2, digits[0], low_b, sum_b, states_s, totals_s, True)
    dt = softplus(v_ref[...])
    dt_s[...] = dt
    dtu_s[...] = dt * u_ref[...].astype(F32)
    xdf_s[...] = xd_ref[...].astype(F32)
    fill_table(xdf_s, lhs_s, bc_s, rank, states)
    scan_both(
        dt_s,
        dtu_s,
        dy_ref,
        bc_s,
        a2,
        h_in_ref,
        g_s,
        y_ref,
        sgb_s,
        sqa_s,
        rate_s,
        db_s,
        dc_s,
        a_s,
        ah_s,
    )
    u = u_ref[...]
    uf = u.astype(F32)
    dy = dy_ref[...]
    if last:
        y_ref[...] += sk_ref[...] * uf
    sgb = sgb_s[...]
    dpre = (LN2 * sqa_s[...] + uf * sgb) * sigmoid(v_ref[...])
    dpl = dpre.astype(BF16)

    ones = jnp.ones((128, 128), BF16)

    def lane_sums(block):
        high = block.astype(BF16)
        rest = (block - high.astype(F32)).astype(BF16)
        return dot(high, ones) + dot(rest, ones)

    n_i = lax.broadcasted_iota(jnp.int32, (states, XD), 0)
    lane = lax.broadcasted_iota(jnp.int32, (states, XD), 1)
    mask_b = (lane == rank + n_i).astype(F32)
    mask_c = (lane == rank + states + n_i).astype(F32)
    db_s[...] = lane_sums(db_s[...])
    dc_s[...] = lane_sums(dc_s[...])

    def gather(i, carry):
        parts = []
        for j in range(UNROLL):
            at = state_rows(i * UNROLL + j, states)
            parts.append(fold(db_s[at, :] * mask_b + dc_s[at, :] * mask_c))
        xdf_s[pl.ds(pl.multiple_of(i * UNROLL, UNROLL), UNROLL), :] = rows_of_sums(parts)
        return carry

    lax.fori_loop(0, rows // UNROLL, gather, 0)
    dxd = (dot_t(dpl, dw[...]) + xdf_s[...]).astype(BF16)
    du = dt_s[...] * sgb + sk_ref[...] * dy + dot_t(dxd, xw[...])
    conv = conv_of(ext_s, halo, xc, cw, cb)
    dconv = du * slope(conv)
    dconv_ref[...] = dconv
    head_ref[...] = dconv[0:HALO, :]
    taps = cw.shape[0]
    width = rank + 2 * states
    g_x = dot_rows(dxd, u)
    g_dt = dot_rows(xd_ref[...], dpl)
    at = 0
    small_ref[at : at + width, :] = g_x[0:width]
    at += width
    small_ref[at : at + rank, :] = g_dt[0:rank]
    at += rank
    small_ref[at : at + states, :] = rate_s[...] * (a2[...] * LN2)
    at += states
    for k in range(taps):
        first = HALO - (taps - 1) + k
        small_ref[at : at + 1, :] = jnp.sum(
            dconv * ext_s[first : first + rows, :], axis=0, keepdims=True
        )
        at += 1
    small_ref[at : at + 1, :] = jnp.sum(dconv, axis=0, keepdims=True)
    small_ref[at + 1 : at + 2, :] = jnp.sum(dpre, axis=0, keepdims=True)
    small_ref[at + 2 : at + 3, :] = jnp.sum(dy * uf, axis=0, keepdims=True)
    small_ref[at + 3 : at + 4, :] = jnp.zeros((1, inner), F32)


def k_out(x_ref, y_ref, z_ref, dgated_ref, ow_ref, iw_ref, hid_ref, gated_ref, dz_ref, dnz_ref):
    zf = z_ref[...].astype(F32)
    s = sigmoid(zf)
    y = y_ref[...]
    gated = (y * (zf * s)).astype(BF16)
    gated_ref[...] = gated
    dz = (dgated_ref[...] * y * (s * (1.0 + zf * (1.0 - s)))).astype(BF16)
    dz_ref[...] = dz
    dnz_ref[...] = dot_t(dz, iw_ref[...])
    hid_ref[...] = (x_ref[...] + dot(gated, ow_ref[...])).astype(BF16)


def conv_back(dce_s, dconv_ref, next_ref, cw_ref):
    rows = dconv_ref.shape[0]
    taps = cw_ref.shape[0]
    dce_s[0:rows, :] = dconv_ref[...]
    dce_s[rows:, :] = next_ref[...]
    out = cw_ref[taps - 1 : taps, :] * dce_s[0:rows, :]
    for k in range(taps - 1):
        first = taps - 1 - k
        out = out + cw_ref[k : k + 1, :] * dce_s[first : first + rows, :]
    return out.astype(BF16)


def norm_back(x, gain, e, dn):
    rinv = lax.rsqrt(jnp.mean(x * x, axis=-1, keepdims=True) + 1e-05)
    xhat = x * rinv
    dhat = dn * gain
    g_norm = jnp.sum(dn * xhat, axis=0, keepdims=True)
    return e + rinv * (dhat - xhat * jnp.mean(dhat * xhat, axis=-1, keepdims=True)), g_norm


def k_turn(
    rank,
    dconv_ref,
    next_ref,
    cw_ref,
    dnz_ref,
    iw_ref,
    x_ref,
    g_ref,
    e_ref,
    ow_ref,
    y_ref,
    z_ref,
    v_ref,
    xd_ref,
    a2,
    dxc_ref,
    gn_ref,
    e1_ref,
    de_ref,
    dy_ref,
    dz_ref,
    pay_ref,
    dce_s,
    dt_s,
    xdf_s,
    lhs_s,
    bc_s,
    end_s,
    wide_s,
):
    dxc = conv_back(dce_s, dconv_ref, next_ref, cw_ref)
    dxc_ref[...] = dxc
    dn = dnz_ref[...] + dot_t(dxc, iw_ref[...])
    e1, g_norm = norm_back(x_ref[...], g_ref[...], e_ref[...].astype(F32), dn)
    gn_ref[...] = g_norm
    e1_ref[...] = e1
    de = e1.astype(BF16)
    de_ref[...] = de
    dgated = dot_t(de, ow_ref[...])
    zf = z_ref[...].astype(F32)
    s = sigmoid(zf)
    dy_ref[...] = dgated * (zf * s)
    dz_ref[...] = (dgated * y_ref[...] * (s * (1.0 + zf * (1.0 - s)))).astype(BF16)
    states = a2.shape[0]
    dt = softplus(v_ref[...])
    dt_s[...] = dt
    total = jnp.sum(dt, axis=0, keepdims=True)
    xdf_s[...] = xd_ref[...].astype(F32)
    fill_table(xdf_s, lhs_s, bc_s, rank, states)
    scan_back_ends(dt_s, dy_ref, bc_s, a2, end_s)
    pay_ref[...] = packed(end_s[...], total, wide_s)


def k_end(
    dconv_ref, next_ref, cw_ref, dnz_ref, iw_ref, x_ref, g_ref, e_ref, dxc_ref, gn_ref, e0_ref, dce_s
):
    dxc = conv_back(dce_s, dconv_ref, next_ref, cw_ref)
    dxc_ref[...] = dxc
    dn = dnz_ref[...] + dot_t(dxc, iw_ref[...])
    e0, g_norm = norm_back(x_ref[...], g_ref[...], e_ref[...], dn)
    gn_ref[...] = g_norm
    e0_ref[...] = e0.astype(BF16)


def k_dnz(dz_ref, iw_ref, out_ref):
    out_ref[...] = dot_t(dz_ref[...], iw_ref[...])


def k_wgrad(a_ref, b_ref, out_ref):
    out_ref[...] = dot_rows(a_ref[...], b_ref[...]).astype(out_ref.dtype)


def shards(
    hidden_in,
    norm_gain,
    in_weight,
    conv_weight,
    conv_bias,
    xproj_weight,
    dtproj_weight,
    dt_bias,
    a_log,
    skip_gain,
    out_weight,
    hidden_grad,
):
    layers, width, _ = in_weight.shape
    inner, states = a_log.shape[1], a_log.shape[2]
    rank = dtproj_weight.shape[1]
    taps = conv_weight.shape[2]
    seqs, own, _ = hidden_in.shape
    ndev = lax.axis_size(AXIS)
    me = lax.axis_index(AXIS)
    core = me % 2
    chip = me // 2
    rows = seqs * own
    assert layers == 2 and seqs == 2 and ndev % 2 == 0
    assert inner % CHUNK == 0 and inner // 128 <= states and rank + 2 * states <= XD

    pairs = [(i, i ^ 1) for i in range(ndev)]

    def to_runs(block):
        mine = lax.dynamic_index_in_dim(block, core, 0, keepdims=False)
        other = lax.dynamic_index_in_dim(block, 1 - core, 0, keepdims=False)
        came = lax.ppermute(other, AXIS, pairs)
        first = jnp.where(core == 0, mine, came)
        second = jnp.where(core == 0, came, mine)
        return jnp.concatenate([first, second], axis=0)

    def from_runs(run_block):
        halves = run_block.reshape((2, own) + run_block.shape[1:])
        mine = lax.dynamic_index_in_dim(halves, core, 0, keepdims=False)
        other = lax.dynamic_index_in_dim(halves, 1 - core, 0, keepdims=False)
        came = lax.ppermute(other, AXIS, pairs)
        first = jnp.where(core == 0, mine, came)
        second = jnp.where(core == 0, came, mine)
        return jnp.stack([first, second], axis=0)

    def from_before(block):
        return lax.ppermute(block, AXIS, [(i, i + 2) for i in range(ndev - 2)])

    def from_after(block):
        return lax.ppermute(block, AXIS, [(i + 2, i) for i in range(ndev - 2)])

    bits = (ndev // 2).bit_length() - 1
    assert 2 << bits == ndev and bits > 2
    rounds = []
    low = 0
    while low < bits:
        n = 2 if bits - low >= 2 else 1
        rounds.append((low, 1 << n))
        low += n

    def digit_of(r):
        low, group = rounds[r]
        return (chip >> low) & (group - 1)

    def digits_of(r):
        nxt = digit_of(r + 1) if r + 1 < len(rounds) else jnp.zeros_like(chip)
        return jnp.stack([digit_of(r), nxt]).astype(jnp.int32)

    def send(block, r, m, which):
        low, group = rounds[r]
        flip = (m << low) << 1
        route = [(i, i ^ flip) for i in range(ndev)]
        if which == "up":
            route = [(i, j) for i, j in route if j > i]
        if which == "down":
            route = [(i, j) for i, j in route if j < i]
        return lax.ppermute(block, AXIS, route)

    smem = pl.BlockSpec(memory_space=pltpu.SMEM)
    pay = shape((states, inner + EXTRA), BF16)

    def exchange(payload, a2, mode):
        befores = [[] for _ in mode]
        sums = [[] for _ in mode]
        for r, (low, group) in enumerate(rounds[:-1]):
            received = [payload] + [send(payload, r, m, "all") for m in range(1, group)]
            final = r + 2 == len(rounds)
            split = len(mode) == 2 and final
            nextgroup = rounds[r + 1][1] if split else 0
            pays = (
                [pay] * (nextgroup - 1)
                if split
                else [shape((states * len(mode), inner + EXTRA), BF16)]
            )
            outs = run(
                functools.partial(k_join, group, nextgroup, mode),
                pays
                + [shape((states, inner), F32)] * len(mode)
                + [shape((1, inner), F32)] * len(mode),
                [(digits_of(r), smem)] + received + [a2],
                [
                    pltpu.VMEM((group, states, inner + EXTRA), F32),
                    pltpu.VMEM((group, 8, inner), F32),
                    pltpu.VMEM((states, inner + EXTRA), F32),
                ],
                flops=10**6,
            )
            sent, outs = outs[: len(pays)], outs[len(pays) :]
            for i in range(len(mode)):
                befores[i].append(outs[i])
                sums[i].append(outs[len(mode) + i])
            payload = sent if split else sent[0]
        r = len(rounds) - 1
        if len(mode) == 2:
            last = [send(payload[m - 1], r, m, "all") for m in range(1, rounds[r][1])]
        else:
            way = "up" if mode == "f" else "down"
            last = [send(payload, r, m, way) for m in range(1, rounds[r][1])]
        return last, sum(befores, []), sum(sums, []), digits_of(r)

    a2_all = -jnp.exp(jnp.swapaxes(a_log, 1, 2)) * LOG2E
    cw_all = jnp.swapaxes(conv_weight, 1, 2)
    xw_all = jnp.pad(xproj_weight, ((0, 0), (0, 0), (0, XD - xproj_weight.shape[2])))
    dw_all = jnp.pad(dtproj_weight, ((0, 0), (0, XD - rank), (0, 0)))

    def row(array, l):
        return array[l : l + 1, :]

    def w_in(l, half):
        return in_weight, part((None, width, inner), (l, 0, half))

    def w_out(l):
        return out_weight, part((None, inner, width), (l, 0, 0))

    def table_scratch():
        return [
            pltpu.VMEM((rows, XD), F32),
            pltpu.VMEM((rows * states, XD), BF16),
            pltpu.VMEM((rows * states, 256), F32),
        ]

    act = shape((rows, inner), F32)
    act_b = shape((rows, inner), BF16)
    res = shape((rows, width), F32)
    res_b = shape((rows, width), BF16)
    edge = shape((HALO, inner), F32)
    mm = 2 * rows * width * inner

    grad_out = to_runs(hidden_grad)
    x0 = to_runs(hidden_in).astype(F32)

    normed = [None, None]
    xc = [None, None]
    halo = [None, None]
    z = [None, None]
    u = [None, None]
    xd = [None, None]
    v = [None, None]

    normed[0], xc[0], tail = run(
        k_in, [res_b, act_b, edge], [x0, row(norm_gain, 0), w_in(0, 0)], flops=mm
    )

    def before_scan(l, tail, dgated=None):
        halo[l] = from_before(tail)
        (z[l],) = run(k_gate, [act_b], [normed[l], w_in(l, 1)], flops=mm)
        both = dgated is not None
        outs = run(
            functools.partial(k_local, rank, both),
            [
                act_b,
                shape((rows, XD), BF16),
                act,
                shape((states * (2 if both else 1), inner + EXTRA), BF16),
            ]
            + ([act] if both else []),
            [
                halo[l],
                xc[l],
                cw_all[l],
                row(conv_bias, l),
                xw_all[l],
                dw_all[l],
                row(dt_bias, l),
                a2_all[l],
            ]
            + ([dgated, z[l]] if both else []),
            [pltpu.VMEM((rows + HALO, inner), F32)]
            + [pltpu.VMEM((rows, inner), F32)] * 2
            + table_scratch()
            + [pltpu.VMEM((states, inner), F32), pltpu.VMEM((states, inner + EXTRA), F32)],
            flops=10**9,
        )
        u[l], xd[l], v[l] = outs[:3]
        return outs[3:]

    (dgated1,) = run(k_dgated, [act], [grad_out, w_out(1)], flops=mm)

    def join_scratch():
        group = rounds[-1][1]
        return [
            pltpu.VMEM((group, states, inner + EXTRA), F32),
            pltpu.VMEM((group, 8, inner), F32),
        ]

    (payload,) = before_scan(0, tail)
    last, befores, sums, digits = exchange(payload, a2_all[0], "f")
    y0, gated0, x1, normed[1], xc[1], tail, h0 = run(
        functools.partial(k_mix, rank, len(last), len(befores)),
        [act, act_b, res, res_b, act_b, edge, shape((states, inner), F32)],
        [(digits, smem)]
        + last
        + befores
        + sums
        + [
            a2_all[0],
            u[0],
            v[0],
            xd[0],
            z[0],
            x0,
            row(skip_gain, 0),
            w_out(0),
            row(norm_gain, 1),
            w_in(1, 0),
        ],
        [pltpu.VMEM((rows, inner), F32)] * 2 + table_scratch() + join_scratch(),
        flops=10**9,
    )
    payload, dy1 = before_scan(1, tail, dgated1)
    last, befores, sums, digits = exchange(payload, a2_all[1], "fb")

    small = shape((rank + 2 * states + rank + states + taps + 4, inner), F32)

    def backward(l, dy, last, befores, sums, digits, h_in):
        final = h_in is None
        n_low = len(rounds) - 1
        outs = run(
            functools.partial(k_back, rank, len(last), n_low, final),
            ([act] if final else []) + [act, edge, small],
            [(digits, smem)]
            + last
            + befores
            + sums
            + [
                a2_all[l],
                u[l],
                v[l],
                xd[l],
                dy,
                halo[l],
                xc[l],
                cw_all[l],
                row(conv_bias, l),
                xw_all[l],
                dw_all[l],
                row(skip_gain, l),
            ]
            + ([] if final else [h_in]),
            [pltpu.VMEM((rows, inner), F32)] * 2
            + table_scratch()
            + join_scratch()
            + [pltpu.VMEM((rows + HALO, inner), F32)]
            + [pltpu.VMEM((rows, inner), F32)] * 2
            + [pltpu.VMEM((states, inner), F32)]
            + [pltpu.VMEM((rows * states, 128), F32)] * 2
            + [pltpu.VMEM((rows * states, CHUNK), F32)] * 2
            + [pltpu.VMEM((states, inner), F32)] * 2,
            flops=2 * 10**9,
        )
        return outs

    y1, dconv1, head1, small1 = backward(1, dy1, last, befores, sums, digits, None)
    after1 = from_after(head1)
    hidden_out, gated1, dz1, dnz1 = run(
        k_out,
        [res_b, act_b, act_b, res],
        [x1, y1, z[1], dgated1, w_out(1), w_in(1, 1)],
        flops=2 * mm,
    )

    def wgrad(a, b):
        (out,) = run(
            k_wgrad, [shape((a.shape[1], b.shape[1]), F32)], [a, b], flops=mm
        )
        return out

    dxc1, gn1, e1, de0, dy0, dz0, payload = run(
        functools.partial(k_turn, rank),
        [act_b, shape((1, width), F32), res, res_b, act, act_b, pay],
        [
            dconv1,
            after1,
            cw_all[1],
            dnz1,
            w_in(1, 0),
            x1,
            row(norm_gain, 1),
            grad_out,
            w_out(0),
            y0,
            z[0],
            v[0],
            xd[0],
            a2_all[0],
        ],
        [pltpu.VMEM((rows + HALO, inner), F32), pltpu.VMEM((rows, inner), F32)]
        + table_scratch()
        + [pltpu.VMEM((states, inner), F32), pltpu.VMEM((states, inner + EXTRA), F32)],
        flops=10**9,
    )
    g_out1 = wgrad(gated1, grad_out)
    g_inz1 = wgrad(normed[1], dz1)
    last, befores, sums, digits = exchange(payload, a2_all[0], "b")
    g_inx1 = wgrad(normed[1], dxc1)
    layer1 = lax.psum((g_out1, g_inz1, g_inx1, small1, gn1), AXIS)
    (dnz0,) = run(k_dnz, [res], [dz0, w_in(0, 1)], flops=mm)
    g_out0 = wgrad(gated0, de0)
    g_inz0 = wgrad(normed[0], dz0)
    dconv0, head0, small0 = backward(0, dy0, last, befores, sums, digits, h0)
    after0 = from_after(head0)
    dxc0, gn0, e0 = run(
        k_end,
        [act_b, shape((1, width), F32), res_b],
        [dconv0, after0, cw_all[0], dnz0, w_in(0, 0), x0, row(norm_gain, 0), e1],
        [pltpu.VMEM((rows + HALO, inner), F32)],
        flops=mm,
    )
    g_inx0 = wgrad(normed[0], dxc0)
    layer0 = lax.psum((g_out0, g_inz0, g_inx0, small0, gn0), AXIS)

    def stacked(i):
        return jnp.stack([layer0[i], layer1[i]])

    g_in = jnp.concatenate([stacked(1), stacked(2)][::-1], axis=2)
    smalls = stacked(3)
    at = 0
    n_x = rank + 2 * states
    g_xw = jnp.swapaxes(smalls[:, 0:n_x], 1, 2)
    g_dw = smalls[:, n_x : n_x + rank]
    at = n_x + rank
    g_al = jnp.swapaxes(smalls[:, at : at + states], 1, 2)
    at += states
    g_cw = jnp.swapaxes(smalls[:, at : at + taps], 1, 2)
    at += taps
    return (
        from_runs(hidden_out),
        from_runs(e0),
        stacked(4)[:, 0],
        g_in,
        g_cw,
        smalls[:, at],
        g_xw,
        g_dw,
        smalls[:, at + 1],
        g_al,
        smalls[:, at + 2],
        stacked(0),
    )


def solution(mesh):
    split = P(None, AXIS, None)
    return jax.shard_map(
        shards,
        mesh=mesh,
        in_specs=(split,) + (P(),) * 10 + (split,),
        out_specs=(split, split) + (P(),) * 10,
        check_vma=False,
    )
```

profile of v0, /device:TPU:0, one launch (start us, length us, event | category | flops | bytes accessed | tf_op | source)
XLA Modules:
  0.0 799.4 jit_solution(1013757729236428181)
XLA Ops:
  21.2 3.7 shard_map.211
  24.9 4.8 collective-permute-start.1
  32.4 14.3 %shard_map.212 = (bf16[256,1536]{1,0:T(8,128)(2,1)}, bf16[256,128]{1,0:T(8,128)(2,1)}, f32[256,1536]{1,0:T(8,128)}, bf16[16,1792]{1,0:T(8,128)(2,1)}) custom-call(f32[8,1536]{1,0:T(8,128)} %copy-done.32, bf16[256,1536]{1,0:T(8,128)(2,1)} %get-tuple-element.66.refs_1_.refs_11_, f32[4,1536]{1,0:T(4,128)} %get-tuple-element.146.refs_2_.refs_12_.cw_ref, ...), custom_call_target="tpu_custom_call" | custom-call | flops 1000000000 | bytes 4964352 | tf_op jit(solution)/shard_map/pallas_call | solution.py:43
  57.3 6.1 collective-permute-start.7
  70.7 3.8 shard_map.216.refs_8_.dgated_ref
  75.1 19.6 %shard_map.215 = (f32[256,1536]{1,0:T(8,128)}, bf16[256,1536]{1,0:T(8,128)(2,1)}, f32[256,768]{1,0:T(8,128)}, bf16[256,768]{1,0:T(8,128)(2,1)}, bf16[256,1536]{1...) custom-call(s32[2]{0:T(128)} %pad_add_fusion.digits, bf16[16,1792]{1,0:T(8,128)(2,1)} %copy-done.11, ...), custom_call_target="tpu_custom_call" | custom-call | flops 1000000000 | bytes 8945664 | tf_op jit(solution)/shard_map/pallas_call | solution.py:43
  94.8 4.0 collective-permute-start.8
  102.9 23.7 %shard_map.218 = (bf16[256,1536]{1,0:T(8,128)(2,1)}, bf16[256,128]{1,0:T(8,128)(2,1)}, f32[256,1536]{1,0:T(8,128)}, bf16[32,1792]{1,0:T(8,128)(2,1)}, f32[256,1536]{1,0:T(8,128)}) custom-call(f32[8,1536]{1,0:T(8,128)} %copy-done.18, bf16[256,1536]{1,0:T(8,128)(2,1)} %get-tuple-element.77.refs_1_.refs_13_, ...), custom_call_target="tpu_custom_call" | custom-call | flops 1000000000 | bytes 8224768 | tf_op jit(solution)/shard_map/pallas_call | solution.py:43
  137.0 4.1 collective-permute-start.15
  144.7 41.7 %shard_map.220 = (f32[256,1536]{1,0:T(8,128)}, f32[256,1536]{1,0:T(8,128)}, f32[8,1536]{1,0:T(8,128)}, f32[152,1536]{1,0:T(8,128)}) custom-call(s32[2]{0:T(128)} %pad_add_fusion.digits, bf16[16,1792]{1,0:T(8,128)(2,1)} %copy-done.26, bf16[16,1792]{1,0:T(8,128)(2,1)} %copy-done.28, bf16[16,1792]{1,0:T(8,128)(2,1)} %copy-done.30, ...), custom_call_target="tpu_custom_call" | custom-call | flops 2000000000 | bytes 8257536 | tf_op jit(solution)/shard_map/pallas_call | solution.py:43
  187.9 6.5 shard_map.221
  194.4 4.3 shard_map.232
  199.3 19.0 %shard_map.222 = (bf16[256,1536]{1,0:T(8,128)(2,1)}, f32[1,768]{1,0:T(1,128)}, f32[256,768]{1,0:T(8,128)}, bf16[256,768]{1,0:T(8,128)(2,1)}, f32[256,1536]{1,0:T...) custom-call(f32[256,1536]{1,0:T(8,128)} %get-tuple-element.93.dconv_ref, f32[8,1536]{1,0:T(8,128)} %copy-done.20, ...), custom_call_target="tpu_custom_call" | custom-call | flops 1000000000 | bytes 8771584 | tf_op jit(solution)/shard_map/pallas_call | solution.py:43
  222.9 4.2 shard_map.230
  238.0 4.2 shard_map.229
  242.2 4.3 shard_map.228
  247.2 38.1 %shard_map.224 = (f32[256,1536]{1,0:T(8,128)}, f32[8,1536]{1,0:T(8,128)}, f32[152,1536]{1,0:T(8,128)}) custom-call(s32[2]{0:T(128)} %pad_add_fusion.digits, bf16[16,1792]{1,0:T(8,128)(2,1)} %copy-done.31, bf16[16,1792]{1,0:T(8,128)(2,1)} %copy-done.29, bf16[16,1792]{1,0:T(8,128)(2,1)} %copy-done.27, f32[16,1536]{1,0:T(8,128)} %get-tuple-element.99.refs_3_, ...), custom_call_target="tpu_custom_call" | custom-call | flops 2000000000 | bytes 5111808 | tf_op jit(solution)/shard_map/pallas_call | solution.py:43
  286.8 4.3 shard_map.231
  292.1 5.1 shard_map.226
  297.2 4.2 shard_map.227
  305.0 45.3 %all-reduce.2 = (f32[1,1,768]{2,0,1:T(1,128)S(1)}, f32[1,1,768]{2,0,1:T(1,128)S(1)}) all-reduce(f32[1,1,768]{2,0,1:T(1,128)S(1)} %bitcast.108, f32[1,1,768]{2,0,1:T(1,128)S(1)} %bitcast.109), channel_id=1, replica_groups=mesh['seq'=32] {'seq'}, use_global_device_ids=true, to_apply=%region_1.2 | all-reduce | flops 1536 | bytes 12288 | tf_op jit(solution)/shard_map/psum | solution.py:1043
  351.7 416.9 %all-reduce.6.cloned.1.call-done = (f32[1,768,1536]{2,1,0:T(8,128)}, f32[1,768,1536]{2,1,0:T(8,128)}, f32[1,768,1536]{2,1,0:T(8,128)}, f32[1,768,1536]{2,1,0:T(8...) async-done(((f32[1,768,1536]{2,1,0:T(8,128)}, f32[1,768,1536]{2,1,0:T(8,128)}, ...) | async-done | bytes 30179344 | tf_op jit(solution)/shard_map/psum | solution.py:1043
  776.2 8.9 %pad_maximum_fusion = f32[2,1536,768]{2,1,0:T(8,128)} fusion(f32[1,1536,768]{2,1,0:T(8,128)} %get-tuple-element.126, f32[1,1536,768]{2,1,0:T(8,128)} %get-tuple-element.127), kind=kLoop, calls=%fused_computation.1 | loop fusion | flops 2359296 | bytes 18874368 | tf_op jit(solution)/shard_map/stack | solution.py:1060
  785.2 6.9 maximum_maximum_fusion
  (171 shorter events, 86.5 us)
Async XLA Ops:
  7.2 761.4 %all-reduce.6.cloned.1.call-start = ((), (), s32[]{:S(2)}) async-start(), calls=%async_computation | async-start | bytes 60358656 | tf_op jit(solution)/shard_map/psum | solution.py:1043
  8.3 21.4 %collective-permute-start.9 = (bf16[128,768]{1,0:T(8,128)(2,1)S(1)}, bf16[128,768]{1,0:T(8,128)(2,1)S(1)}, u32[]{:S(2)}, u32[]{:S(2)}) collective-permute-start(bf16[128,768]{1,0:T(8,128)(2,1)S(1)} %dynamic-slice_bitcast_fusion.2), channel_id=1, source_target_pairs={{0,1},{1,0},{2,3},{3,2},{4,5},{5,4},{6,7},{7,6},{8,9},{9,8},{10,11... | collective-permute-start | bytes 589832 | tf_op jit(solution)/shard_map/ppermute | solution.py:759
  9.8 10.4 %collective-permute-start = (bf16[128,768]{1,0:T(8,128)(2,1)S(1)}, bf16[128,768]{1,0:T(8,128)(2,1)S(1)}, u32[]{:S(2)}, u32[]{:S(2)}) collective-permute-start(bf16[128,768]{1,0:T(8,128)(2,1)S(1)} %dynamic-slice_bitcast_fusion.3), channel_id=1, source_target_pairs={{0,1},{1,0},{2,3},{3,2},{4,5},{5,4},{6,7},{7,6},{8,9},{9,8},{10,11... | collective-permute-start | bytes 589832 | tf_op jit(solution)/shard_map/ppermute | solution.py:759
  24.9 6.9 collective-permute-start.1
  46.7 5.7 collective-permute-start.4
  57.3 17.1 %collective-permute-start.7 = (bf16[16,1792]{1,0:T(8,128)(2,1)}, bf16[16,1792]{1,0:T(8,128)(2,1)S(1)}, u32[]{:S(2)}, u32[]{:S(2)}) collective-permute-start(bf16[16,1792]{1,0:T(8,128)(2,1)} %get-tuple-element.68), channel_id=1, source_target_pairs={{0,24},{1,25},{2,26},{3,27},{4,28},{5,29},{6,30},{7,31},{8,16},{9,... | collective-permute-start | bytes 172040 | tf_op jit(solution)/shard_map/ppermute | solution.py:804
  63.4 11.0 %collective-permute-start.6 = (bf16[16,1792]{1,0:T(8,128)(2,1)}, bf16[16,1792]{1,0:T(8,128)(2,1)S(1)}, u32[]{:S(2)}, u32[]{:S(2)}) collective-permute-start(bf16[16,1792]{1,0:T(8,128)(2,1)} %get-tuple-element.68), channel_id=1, source_target_pairs={{0,16},{1,17},{2,18},{3,19},{4,20},{5,21},{6,22},{7,23},{8,24},{9,... | collective-permute-start | bytes 172040 | tf_op jit(solution)/shard_map/ppermute | solution.py:804
  64.7 9.7 %collective-permute-start.5 = (bf16[16,1792]{1,0:T(8,128)(2,1)}, bf16[16,1792]{1,0:T(8,128)(2,1)S(1)}, u32[]{:S(2)}, u32[]{:S(2)}) collective-permute-start(bf16[16,1792]{1,0:T(8,128)(2,1)} %get-tuple-element.68), channel_id=1, source_target_pairs={{0,8},{1,9},{2,10},{3,11},{4,12},{5,13},{6,14},{7,15},{16,24},{17,... | collective-permute-start | bytes 172040 | tf_op jit(solution)/shard_map/ppermute | solution.py:804
  94.8 7.5 collective-permute-start.8
  126.6 6.0 collective-permute-start.12
  127.0 6.2 collective-permute-start.11
  128.7 5.0 collective-permute-start.10
  136.7 4.4 collective-permute-start.13
  137.0 5.3 collective-permute-start.14
  137.0 7.1 collective-permute-start.15
  186.4 12.2 %collective-permute-start.17 = (f32[8,1536]{1,0:T(8,128)}, f32[8,1536]{1,0:T(8,128)S(1)}, u32[]{:S(2)}, u32[]{:S(2)}) collective-permute-start(f32[8,1536]{1,0:T(8,128)} %get-tuple-element.94), channel_id=1, source_target_pairs={{2,0},{3,1},{4,2},{5,3},{6,4},{7,5},{8,6},{9,7},{10,8},{11,9},{12,... | collective-permute-start | bytes 147464 | tf_op jit(solution)/shard_map/ppermute | solution.py:777
  218.2 12.5 %collective-permute-start.20 = (bf16[16,1792]{1,0:T(8,128)(2,1)}, bf16[16,1792]{1,0:T(8,128)(2,1)S(1)}, u32[]{:S(2)}, u32[]{:S(2)}) collective-permute-start(bf16[16,1792]{1,0:T(8,128)(2,1)} %get-tuple-element.97.refs_0_), channel_id=1, source_target_pairs={{0,6},{1,7},{2,4},{3,5},{4,2},{5,3},{6,0},{7,1},{8,14},{9,15},{10,... | collective-permute-start | bytes 172040 | tf_op jit(solution)/shard_map/ppermute | solution.py:804
  221.4 9.4 %collective-permute-start.19 = (bf16[16,1792]{1,0:T(8,128)(2,1)}, bf16[16,1792]{1,0:T(8,128)(2,1)S(1)}, u32[]{:S(2)}, u32[]{:S(2)}) collective-permute-start(bf16[16,1792]{1,0:T(8,128)(2,1)} %get-tuple-element.97.refs_0_), channel_id=1, source_target_pairs={{0,4},{1,5},{2,6},{3,7},{4,0},{5,1},{6,2},{7,3},{8,12},{9,13},{10,... | collective-permute-start | bytes 172040 | tf_op jit(solution)/shard_map/ppermute | solution.py:804
  222.3 8.5 %collective-permute-start.18 = (bf16[16,1792]{1,0:T(8,128)(2,1)}, bf16[16,1792]{1,0:T(8,128)(2,1)S(1)}, u32[]{:S(2)}, u32[]{:S(2)}) collective-permute-start(bf16[16,1792]{1,0:T(8,128)(2,1)} %get-tuple-element.97.refs_0_), channel_id=1, source_target_pairs={{0,2},{1,3},{2,0},{3,1},{4,6},{5,7},{6,4},{7,5},{8,10},{9,11},{10,... | collective-permute-start | bytes 172040 | tf_op jit(solution)/shard_map/ppermute | solution.py:804
  233.9 12.6 %collective-permute-start.23 = (bf16[16,1792]{1,0:T(8,128)(2,1)}, bf16[16,1792]{1,0:T(8,128)(2,1)S(1)}, u32[]{:S(2)}, u32[]{:S(2)}) collective-permute-start(bf16[16,1792]{1,0:T(8,128)(2,1)} %get-tuple-element.98), channel_id=1, source_target_pairs={{16,8},{17,9},{18,10},{19,11},{20,12},{21,13},{22,14},{23,15},{24,... | collective-permute-start | bytes 172040 | tf_op jit(solution)/shard_map/ppermute | solution.py:804
  235.2 11.3 %collective-permute-start.22 = (bf16[16,1792]{1,0:T(8,128)(2,1)}, bf16[16,1792]{1,0:T(8,128)(2,1)S(1)}, u32[]{:S(2)}, u32[]{:S(2)}) collective-permute-start(bf16[16,1792]{1,0:T(8,128)(2,1)} %get-tuple-element.98), channel_id=1, source_target_pairs={{16,0},{17,1},{18,2},{19,3},{20,4},{21,5},{22,6},{23,7},{24,8},{25... | collective-permute-start | bytes 172040 | tf_op jit(solution)/shard_map/ppermute | solution.py:804
  236.5 10.1 %collective-permute-start.21 = (bf16[16,1792]{1,0:T(8,128)(2,1)}, bf16[16,1792]{1,0:T(8,128)(2,1)S(1)}, u32[]{:S(2)}, u32[]{:S(2)}) collective-permute-start(bf16[16,1792]{1,0:T(8,128)(2,1)} %get-tuple-element.98), channel_id=1, source_target_pairs={{8,0},{9,1},{10,2},{11,3},{12,4},{13,5},{14,6},{15,7},{24,16},{25,... | collective-permute-start | bytes 172040 | tf_op jit(solution)/shard_map/ppermute | solution.py:804
  285.3 6.2 collective-permute-start.24
  304.0 46.9 %collective-permute-start.25 = (bf16[128,768]{1,0:T(8,128)(2,1)S(1)}, bf16[128,768]{1,0:T(8,128)(2,1)S(1)}, u32[]{:S(2)}, u32[]{:S(2)}) collective-permute-start(bf16[128,768]{1,0:T(8,128)(2,1)S(1)} %dynamic-slice_bitcast_fusion), channel_id=1, source_target_pairs={{0,1},{1,0},{2,3},{3,2},{4,5},{5,4},{6,7},{7,6},{8,9},{9,8},{10,11... | collective-permute-start | bytes 589832 | tf_op jit(solution)/shard_map/ppermute | solution.py:768
  (42 other events, 180.3 us)
Sparse Core Ops, SparseCore 0:
  301.5 467.0 all-reduce.5
where the time goes:
time: 809 us; the launch traced here: 799 us
  waiting for transfers between devices  430 us (53%)
  Pallas kernels  217 us (27%)
  blocking collectives  45.3 us (6%)
  starting transfers between devices  43.9 us (5%)
  local copies, waits for them, and re-layouts  25.7 us (3%)
  other arithmetic  22.1 us (3%)
  between operations  14.9 us (2%)
    psum x1, waiting for transfers between devices, shards(): layer1 = lax.psum((g_out1, g_inz1, g_inx1, small1, gn1), AXIS)  417 us
    pallas_call x22, Pallas kernels, run(): pl.pallas_call(kernel, grid=(1,), in_specs=specs, out_specs=[full(o) for...  217 us
    psum x1, blocking collectives, shards(): layer1 = lax.psum((g_out1, g_inz1, g_inx1, small1, gn1), AXIS)  45.3 us
    ppermute x18, starting transfers between devices, send(): return lax.ppermute(block, AXIS, route)  31.1 us
  transfers between devices with their start and end apart: 27, of which 12 were waited for; matrix products, arithmetic and copies ran while one was open for 2% of the time, Pallas kernels for 6%

commit v1 on v0

--- a/solution.py
+++ b/solution.py
@@ -18,6 +18,9 @@
 CHUNK = 256
 UNROLL = 8
 HALO = 8
+COST = pl.CostEstimate(flops=1, bytes_accessed=1, transcendentals=0)
+LONG = pl.CostEstimate(flops=1, bytes_accessed=10**8, transcendentals=0)
+BLOCKS = 16
 
 
 def full(array):
@@ -29,7 +32,9 @@
     return pl.BlockSpec(shape, lambda i, index=index: index)
 
 
-def run(kernel, outs, ins, scratch=(), flops=0, moved=None):
+def run(kernel, outs, ins, scratch=(), turn=None, cost=COST):
+    out_specs = [o[1] if isinstance(o, tuple) else full(o) for o in outs]
+    outs = [o[0] if isinstance(o, tuple) else o for o in outs]
     arrays, specs = [], []
     for item in ins:
         if isinstance(item, tuple):
@@ -38,18 +43,28 @@
         else:
             arrays.append(item)
             specs.append(full(item))
-    if moved is None:
-        moved = sum(math.prod(o.shape) * o.dtype.itemsize for o in outs) * 2
-    return pl.pallas_call(
-        kernel,
+    body = kernel
+    if turn:
+        n = len(arrays)
+        arrays.append(turn[0])
+        specs.append(pl.BlockSpec(memory_space=pl.ANY))
+
+        def body(*refs):
+            kernel(*refs[:n], *refs[n + 1 :])
+
+    results = pl.pallas_call(
+        body,
         grid=(1,),
         in_specs=specs,
-        out_specs=[full(o) for o in outs],
+        out_specs=out_specs,
         out_shape=outs,
         scratch_shapes=list(scratch),
         compiler_params=pltpu.CompilerParams(vmem_limit_bytes=58 * 1024 * 1024),
-        cost_estimate=pl.CostEstimate(flops=flops, bytes_accessed=moved, transcendentals=0),
+        cost_estimate=cost,
     )(*arrays)
+    if turn is not None:
+        turn[:] = [results[-1]]
+    return results
 
 
 def shape(dims, dtype):
@@ -232,7 +247,6 @@
     a2_ref,
     h_in_ref,
     g_in_ref,
-    y_ref,
     sgb_ref,
     sqa_ref,
     rate_ref,
@@ -251,23 +265,16 @@
         a2 = a2_ref[:, lanes]
 
         def ahead(i, h):
-            parts = []
             for j in range(UNROLL):
                 t = i * UNROLL + j
                 at = state_rows(t, states)
                 a = jnp.exp2(dt_ref[pl.ds(t, 1), lanes] * a2)
-                both = bc_ref[at, :]
+                b_row = wide(bc_ref[at, 0:128], CHUNK)
                 ah = a * h
                 a_s[at, :] = a
                 ah_s[at, :] = ah
-                h = ah + dtu_ref[pl.ds(t, 1), lanes] * wide(both[:, 0:128], CHUNK)
+                h = ah + dtu_ref[pl.ds(t, 1), lanes] * b_row
                 dc_ref[at, :] += fold_lanes(h * dy_ref[pl.ds(t, 1), lanes])
-                if y_ref is not None:
-                    parts.append(fold(h * wide(both[:, 128:256], CHUNK)))
-            if y_ref is not None:
-                y_ref[pl.ds(pl.multiple_of(i * UNROLL, UNROLL), UNROLL), lanes] = (
-                    rows_of_sums(parts)
-                )
             return h
 
         lax.fori_loop(0, rows // UNROLL, ahead, h_in_ref[:, lanes])
@@ -446,126 +453,95 @@
             pays[0][i * states : (i + 1) * states, :] = out[i]
 
 
-def entering(received, a2_ref, digit, befores, sums, states_s, totals_s, backward):
-    states, inner = a2_ref.shape
+def entering(received, a2_ref, digit, befores, sums, states_s, totals_s, backward, lane0=0):
+    lanes = a2_ref.shape[1]
+    inner = received[0].shape[1] - EXTRA
+    here = slice(lane0, lane0 + lanes)
     group = len(received) + 1
     states_s[0] = jnp.zeros(states_s.shape[1:], F32)
-    for m in range(group):
-        if m:
-            states_s[m] = received[m - 1][...].astype(F32)
-        unpack_total(states_s, m, totals_s, inner)
+    totals_s[0] = jnp.zeros(totals_s.shape[1:], F32)
+    for m in range(1, group):
+        states_s[m] = received[m - 1][:, here].astype(F32)
+        sums_m = received[m - 1][:, inner:].astype(F32)
+        for k in range(lanes // 128):
+            row = lane0 // 128 + k
+            totals_s[m, 0:1, k * 128 : (k + 1) * 128] = (
+                sums_m[row : row + 1, 0:128] + sums_m[row : row + 1, 128:256]
+            )
     value, _, _, _ = join_runs(states_s, totals_s, a2_ref[...], digit, group, backward)
     for before, total in reversed(list(zip(befores, sums))):
-        value = jnp.exp2(total[...] * a2_ref[...]) * value + before[...]
+        value = jnp.exp2(total[:, here] * a2_ref[...]) * value + before[:, here]
     return value
 
 
-def k_mix(rank, n_recv, n_low, digits, *refs):
+def k_mix(rank, last, n_recv, n_low, digits, core, *refs):
     refs = list(refs)
     received, refs = refs[:n_recv], refs[n_recv:]
     befores, refs = refs[:n_low], refs[n_low:]
     sums, refs = refs[:n_low], refs[n_low:]
-    a2, u_ref, v_ref, xd_ref, z_ref, x_ref, sk_ref, ow_ref, g_ref, iw_ref = refs[:10]
-    refs = refs[10:]
-    y_ref, gated_ref, x1_ref, n_ref, xc_ref, tail_ref, h_in_ref = refs[:7]
-    dt_s, dtu_s, xdf_s, lhs_s, bc_s, states_s, totals_s = refs[7:]
-    states = a2.shape[0]
+    a2, u_ref, v_ref, xd_ref, z_ref, x_ref, sk_ref, ow_ref = refs[:8]
+    refs = refs[8:]
+    if last:
+        dgated_ref, hid_ref, dz_ref, dz_keep, dz_send, gated_keep, gated_send, h_in_ref = refs[:8]
+        y_ref, refs = refs[8], refs[9:]
+    else:
+        g_ref, iw_ref, y_ref, x1_ref, n_ref, xc_ref, tail_ref = refs[:7]
+        gated_keep, gated_send, h_in_ref = refs[7:10]
+        refs = refs[10:]
+    gated_s, dt_s, dtu_s, xdf_s, lhs_s, bc_s, states_s, totals_s = refs
     h_in_ref[...] = entering(received, a2, digits[0], befores, sums, states_s, totals_s, False)
     uf = u_ref[...].astype(F32)
     dt = softplus(v_ref[...])
     dt_s[...] = dt
     dtu_s[...] = dt * uf
     xdf_s[...] = xd_ref[...].astype(F32)
-    fill_table(xdf_s, lhs_s, bc_s, rank, states)
+    fill_table(xdf_s, lhs_s, bc_s, rank, a2.shape[0])
     scan_forward(dt_s, dtu_s, bc_s, a2, h_in_ref, y_ref)
     y = y_ref[...] + sk_ref[...] * u_ref[...].astype(F32)
-    y_ref[...] = y
     zf = z_ref[...].astype(F32)
-    gated = (y * (zf * sigmoid(zf))).astype(BF16)
-    gated_ref[...] = gated
+    s = sigmoid(zf)
+    gated = (y * (zf * s)).astype(BF16)
+    gated_s[...] = gated
+    gated_keep[...] = lane_half(gated_s, core[0])
+    gated_send[...] = lane_half(gated_s, 1 - core[0])
     x1 = x_ref[...] + dot(gated, ow_ref[...])
-    x1_ref[...] = x1
-    normed = normed_of(x1, g_ref[...])
-    n_ref[...] = normed
-    xc = dot(normed, iw_ref[...]).astype(BF16)
-    xc_ref[...] = xc
-    tail_ref[...] = xc.astype(F32)[xc.shape[0] - HALO :, :]
-
-
-def k_back(rank, n_recv, n_low, last, digits, *refs):
+    if last:
+        dz_ref[...] = (dgated_ref[...] * y * (s * (1.0 + zf * (1.0 - s)))).astype(BF16)
+        dz_keep[...] = lane_half(dz_ref, core[0])
+        dz_send[...] = lane_half(dz_ref, 1 - core[0])
+        hid_ref[...] = x1.astype(BF16)
+    else:
+        y_ref[...] = y
+        x1_ref[...] = x1
+        normed = normed_of(x1, g_ref[...])
+        n_ref[...] = normed
+        xc = dot(normed, iw_ref[...]).astype(BF16)
+        xc_ref[...] = xc
+        tail_ref[...] = xc.astype(F32)[xc.shape[0] - HALO :, :]
+
+
+def k_scan(rank, lane0, n_recv, n_low, digits, *refs):
     refs = list(refs)
     received, refs = refs[:n_recv], refs[n_recv:]
-    kinds = 2 if last else 1
-    befores, refs = refs[: n_low * kinds], refs[n_low * kinds :]
-    sums, refs = refs[: n_low * kinds], refs[n_low * kinds :]
-    a2, u_ref, v_ref, xd_ref, dy_ref, halo, xc, cw, cb, xw, dw, sk_ref = refs[:12]
-    refs = refs[12:]
-    if last:
-        y_ref = refs[0]
-        refs = refs[1:]
-    else:
-        h_in_ref = refs[0]
-        refs = refs[1:]
-        y_ref = None
-    dconv_ref, head_ref, small_ref = refs[:3]
-    refs = refs[3:]
-    (
-        dt_s,
-        dtu_s,
-        xdf_s,
-        lhs_s,
-        bc_s,
-        states_s,
-        totals_s,
-        ext_s,
-        sgb_s,
-        sqa_s,
-        rate_s,
-        db_s,
-        dc_s,
-        a_s,
-        ah_s,
-        g_s,
-        h_s,
-    ) = refs
+    befores, refs = refs[:n_low], refs[n_low:]
+    sums, refs = refs[:n_low], refs[n_low:]
+    a2, u_ref, v_ref, dy_ref, h_in_ref, xd_ref = refs[:6]
+    sgb_ref, sqa_ref, rate_ref, dbc_ref = refs[6:10]
+    dt_s, dtu_s, xdf_s, lhs_s, bc_s, states_s, totals_s, db_s, dc_s, a_s, ah_s, g_s = refs[10:]
     states = a2.shape[0]
-    rows, inner = u_ref.shape
-    low_f, low_b = befores[:n_low], befores[-n_low:]
-    sum_f, sum_b = sums[:n_low], sums[-n_low:]
-    if last:
-        h_s[...] = entering(received, a2, digits[0], low_f, sum_f, states_s, totals_s, False)
-        h_in_ref = h_s
-    g_s[...] = entering(received, a2, digits[0], low_b, sum_b, states_s, totals_s, True)
+    rows = u_ref.shape[0]
+    g_s[...] = entering(
+        received, a2, digits[0], befores, sums, states_s, totals_s, True, lane0
+    )
     dt = softplus(v_ref[...])
     dt_s[...] = dt
     dtu_s[...] = dt * u_ref[...].astype(F32)
     xdf_s[...] = xd_ref[...].astype(F32)
     fill_table(xdf_s, lhs_s, bc_s, rank, states)
     scan_both(
-        dt_s,
-        dtu_s,
-        dy_ref,
-        bc_s,
-        a2,
-        h_in_ref,
-        g_s,
-        y_ref,
-        sgb_s,
-        sqa_s,
-        rate_s,
-        db_s,
-        dc_s,
-        a_s,
-        ah_s,
+        dt_s, dtu_s, dy_ref, bc_s, a2, h_in_ref, g_s, sgb_ref, sqa_ref, rate_ref, db_s, dc_s, a_s, ah_s
     )
-    u = u_ref[...]
-    uf = u.astype(F32)
-    dy = dy_ref[...]
-    if last:
-        y_ref[...] += sk_ref[...] * uf
-    sgb = sgb_s[...]
-    dpre = (LN2 * sqa_s[...] + uf * sgb) * sigmoid(v_ref[...])
-    dpl = dpre.astype(BF16)
+    rate_ref[...] = rate_ref[...] * (a2[...] * LN2)
 
     ones = jnp.ones((128, 128), BF16)
 
@@ -586,12 +562,35 @@
         for j in range(UNROLL):
             at = state_rows(i * UNROLL + j, states)
             parts.append(fold(db_s[at, :] * mask_b + dc_s[at, :] * mask_c))
-        xdf_s[pl.ds(pl.multiple_of(i * UNROLL, UNROLL), UNROLL), :] = rows_of_sums(parts)
+        dbc_ref[pl.ds(pl.multiple_of(i * UNROLL, UNROLL), UNROLL), :] = rows_of_sums(parts)
         return carry
 
     lax.fori_loop(0, rows // UNROLL, gather, 0)
-    dxd = (dot_t(dpl, dw[...]) + xdf_s[...]).astype(BF16)
-    du = dt_s[...] * sgb + sk_ref[...] * dy + dot_t(dxd, xw[...])
+
+
+def k_post(rank, n_parts, *refs):
+    refs = list(refs)
+    sgbs, refs = refs[:n_parts], refs[n_parts:]
+    sqas, refs = refs[:n_parts], refs[n_parts:]
+    rates, refs = refs[:n_parts], refs[n_parts:]
+    dbcs, refs = refs[:n_parts], refs[n_parts:]
+    u_ref, v_ref, xd_ref, dy_ref, halo, xc, cw, cb, xw, dw, sk_ref = refs[:11]
+    dconv_ref, head_ref, small_ref, ext_s = refs[11:]
+    states = rates[0].shape[0]
+    rows, inner = u_ref.shape
+    sgb = jnp.concatenate([ref[...] for ref in sgbs], axis=1)
+    sqa = jnp.concatenate([ref[...] for ref in sqas], axis=1)
+    dbc = dbcs[0][...]
+    for ref in dbcs[1:]:
+        dbc = dbc + ref[...]
+    u = u_ref[...]
+    uf = u.astype(F32)
+    dy = dy_ref[...]
+    v = v_ref[...]
+    dpre = (LN2 * sqa + uf * sgb) * sigmoid(v)
+    dpl = dpre.astype(BF16)
+    dxd = (dot_t(dpl, dw[...]) + dbc).astype(BF16)
+    du = softplus(v) * sgb + sk_ref[...] * dy + dot_t(dxd, xw[...])
     conv = conv_of(ext_s, halo, xc, cw, cb)
     dconv = du * slope(conv)
     dconv_ref[...] = dconv
@@ -605,7 +604,7 @@
     at += width
     small_ref[at : at + rank, :] = g_dt[0:rank]
     at += rank
-    small_ref[at : at + states, :] = rate_s[...] * (a2[...] * LN2)
+    small_ref[at : at + states, :] = jnp.concatenate([ref[...] for ref in rates], axis=1)
     at += states
     for k in range(taps):
         first = HALO - (taps - 1) + k
@@ -619,16 +618,9 @@
     small_ref[at + 3 : at + 4, :] = jnp.zeros((1, inner), F32)
 
 
-def k_out(x_ref, y_ref, z_ref, dgated_ref, ow_ref, iw_ref, hid_ref, gated_ref, dz_ref, dnz_ref):
-    zf = z_ref[...].astype(F32)
-    s = sigmoid(zf)
-    y = y_ref[...]
-    gated = (y * (zf * s)).astype(BF16)
-    gated_ref[...] = gated
-    dz = (dgated_ref[...] * y * (s * (1.0 + zf * (1.0 - s)))).astype(BF16)
-    dz_ref[...] = dz
-    dnz_ref[...] = dot_t(dz, iw_ref[...])
-    hid_ref[...] = (x_ref[...] + dot(gated, ow_ref[...])).astype(BF16)
+def lane_half(ref, which):
+    half = ref.shape[1] // 2
+    return ref[:, pl.ds(pl.multiple_of(which * half, 128), half)]
 
 
 def conv_back(dce_s, dconv_ref, next_ref, cw_ref):
@@ -651,8 +643,19 @@
     return e + rinv * (dhat - xhat * jnp.mean(dhat * xhat, axis=-1, keepdims=True)), g_norm
 
 
+def small_out(core, small_ref, g_norm, keep_ref, send_ref):
+    rows, inner = small_ref.shape
+    width = g_norm.shape[1]
+    small_ref[rows - 1 : rows, 0:width] = g_norm
+    for which, ref in ((core[0], keep_ref), (1 - core[0], send_ref)):
+        ref[0:rows, :] = lane_half(small_ref, which)
+        ref[rows:, :] = jnp.zeros((ref.shape[0] - rows, ref.shape[1]), F32)
+
+
 def k_turn(
     rank,
+    core,
+    small_ref,
     dconv_ref,
     next_ref,
     cw_ref,
@@ -667,13 +670,19 @@
     v_ref,
     xd_ref,
     a2,
-    dxc_ref,
-    gn_ref,
+    dxc_keep,
+    dxc_send,
+    small_keep,
+    small_send,
     e1_ref,
     de_ref,
     dy_ref,
     dz_ref,
+    dz_keep,
+    dz_send,
     pay_ref,
+    small_s,
+    dxc_s,
     dce_s,
     dt_s,
     xdf_s,
@@ -683,10 +692,13 @@
     wide_s,
 ):
     dxc = conv_back(dce_s, dconv_ref, next_ref, cw_ref)
-    dxc_ref[...] = dxc
+    dxc_s[...] = dxc
+    dxc_keep[...] = lane_half(dxc_s, core[0])
+    dxc_send[...] = lane_half(dxc_s, 1 - core[0])
     dn = dnz_ref[...] + dot_t(dxc, iw_ref[...])
     e1, g_norm = norm_back(x_ref[...], g_ref[...], e_ref[...].astype(F32), dn)
-    gn_ref[...] = g_norm
+    small_s[...] = small_ref[...]
+    small_out(core, small_s, g_norm, small_keep, small_send)
     e1_ref[...] = e1
     de = e1.astype(BF16)
     de_ref[...] = de
@@ -695,6 +707,8 @@
     s = sigmoid(zf)
     dy_ref[...] = dgated * (zf * s)
     dz_ref[...] = (dgated * y_ref[...] * (s * (1.0 + zf * (1.0 - s)))).astype(BF16)
+    dz_keep[...] = lane_half(dz_ref, core[0])
+    dz_send[...] = lane_half(dz_ref, 1 - core[0])
     states = a2.shape[0]
     dt = softplus(v_ref[...])
     dt_s[...] = dt
@@ -706,13 +720,33 @@
 
 
 def k_end(
-    dconv_ref, next_ref, cw_ref, dnz_ref, iw_ref, x_ref, g_ref, e_ref, dxc_ref, gn_ref, e0_ref, dce_s
+    core,
+    small_ref,
+    dconv_ref,
+    next_ref,
+    cw_ref,
+    dnz_ref,
+    iw_ref,
+    x_ref,
+    g_ref,
+    e_ref,
+    dxc_keep,
+    dxc_send,
+    small_keep,
+    small_send,
+    e0_ref,
+    small_s,
+    dxc_s,
+    dce_s,
 ):
     dxc = conv_back(dce_s, dconv_ref, next_ref, cw_ref)
-    dxc_ref[...] = dxc
+    dxc_s[...] = dxc
+    dxc_keep[...] = lane_half(dxc_s, core[0])
+    dxc_send[...] = lane_half(dxc_s, 1 - core[0])
     dn = dnz_ref[...] + dot_t(dxc, iw_ref[...])
     e0, g_norm = norm_back(x_ref[...], g_ref[...], e_ref[...], dn)
-    gn_ref[...] = g_norm
+    small_s[...] = small_ref[...]
+    small_out(core, small_s, g_norm, small_keep, small_send)
     e0_ref[...] = e0.astype(BF16)
 
 
@@ -720,8 +754,114 @@
     out_ref[...] = dot_t(dz_ref[...], iw_ref[...])
 
 
-def k_wgrad(a_ref, b_ref, out_ref):
-    out_ref[...] = dot_rows(a_ref[...], b_ref[...]).astype(out_ref.dtype)
+def k_chip_sum(n_pairs, has_small, *refs):
+    refs = list(refs)
+    pairs, refs = [refs[4 * i : 4 * i + 4] for i in range(n_pairs)], refs[4 * n_pairs :]
+    if has_small:
+        (small_a, small_b), refs = refs[:2], refs[2:]
+    (s_ref,) = refs
+    blocks = s_ref.shape[0]
+    rows = pairs[0][0].shape[1] // blocks
+    for i, (a, a_came, b, b_came) in enumerate(pairs):
+        total = dot_rows(
+            jnp.concatenate([a[...], a_came[...]], axis=0),
+            jnp.concatenate([b[...], b_came[...]], axis=0),
+        )
+        s_ref[:, i * rows : (i + 1) * rows, :] = total.reshape(blocks, rows, total.shape[1])
+    if has_small:
+        n = small_a.shape[0] // blocks
+        top = n_pairs * rows
+        s_ref[:, top:, :] = jnp.zeros((blocks, s_ref.shape[1] - top, s_ref.shape[2]), F32)
+        for k in range(blocks):
+            here = slice(k * n, (k + 1) * n)
+            s_ref[k, top : top + n, :] = small_a[here, :] + small_b[here, :]
+
+
+def k_first(n_pairs, has_small, place, *refs):
+    keep_a, keep_b, send_a, send_b, s_ref = refs[-5:]
+    k_chip_sum(n_pairs, has_small, *refs[:-5], s_ref)
+    blocks = s_ref.shape[0]
+    half = s_ref.shape[2] // 2
+    x, y = place[0] & 1, (place[0] >> 1) & 1
+    for i in range(blocks // 2):
+        at = (i >> 1) * 4 + (i & 1) * 2
+        keep_a[i] = s_ref[at + x, :, 0:half]
+        send_a[i] = s_ref[at + 1 - x, :, 0:half].astype(BF16)
+        at = (i >> 1) * 4 + (i & 1)
+        keep_b[i] = s_ref[at + 2 * y, :, half:]
+        send_b[i] = s_ref[at + 2 * (1 - y), :, half:].astype(BF16)
+
+
+def k_second(place, keep_a, keep_b, came_a, came_b, stay_a, stay_b, send_a, send_b):
+    x, y = place[0] & 1, (place[0] >> 1) & 1
+    for i in range(stay_a.shape[0]):
+        for keep, came, stay, send, bit in (
+            (keep_a, came_a, stay_a, send_a, y),
+            (keep_b, came_b, stay_b, send_b, x),
+        ):
+            at = 2 * i + bit
+            stay[i] = keep[at] + came[at].astype(F32)
+            at = 2 * i + 1 - bit
+            send[i] = (keep[at] + came[at].astype(F32)).astype(BF16)
+
+
+def k_third(place, stay_a, stay_b, came_a, came_b, keep, send1, send2, send3):
+    z = (place[0] >> 2) & 3
+    half = stay_a.shape[2]
+    for m, ref in enumerate((keep, send1, send2, send3)):
+        at = jnp.bitwise_xor(z, m)
+        ref[:, 0:half] = (stay_a[at] + came_a[at].astype(F32)).astype(ref.dtype)
+        ref[:, half:] = (stay_b[at] + came_b[at].astype(F32)).astype(ref.dtype)
+
+
+def k_fourth(keep, came1, came2, came3, out):
+    out[...] = (
+        keep[...] + came1[...].astype(F32) + came2[...].astype(F32) + came3[...].astype(F32)
+    ).astype(BF16)
+
+
+def k_stack(mine, came1, came2, came3, out_a, out_b):
+    half = out_a.shape[2]
+    for m, ref in enumerate((mine, came1, came2, came3)):
+        out_a[m] = ref[:, 0:half]
+        out_b[m] = ref[:, half:]
+
+
+def k_chip(place, *refs):
+    left, right, out = refs[0:4], refs[4:8], refs[8]
+    half = left[0].shape[2]
+    xy, z = place[0] & 3, (place[0] >> 2) & 3
+    for d in range(4):
+        for m in range(4):
+            at = jnp.bitwise_xor(z, m) * 4 + jnp.bitwise_xor(xy, d)
+            out[at, :, 0:half] = left[d][m]
+            out[at, :, half:] = right[d][m]
+
+
+def k_place(split_rows, core, mine, came, *refs):
+    out, done = refs[-2:]
+    done[...] = jnp.zeros(done.shape, F32)
+    blocks, rows, lanes = mine.shape
+    own = core[0] == 0
+    a = mine[...].astype(F32).reshape(blocks * rows, lanes)
+    b = came[...].astype(F32).reshape(blocks * rows, lanes)
+    low, high = jnp.where(own, a, b), jnp.where(own, b, a)
+    if split_rows:
+        out[0], out[1] = low, high
+    else:
+        out[:, 0:lanes] = low
+        out[:, lanes:] = high
+
+
+def k_place_small(row0, core, mine, came, out):
+    blocks, _, lanes = mine.shape
+    n = out.shape[0] // blocks
+    first = jnp.where(core[0] == 0, 0, 1)
+    for src, half in ((mine, first), (came, 1 - first)):
+        for k in range(blocks):
+            out[k * n : (k + 1) * n, pl.ds(pl.multiple_of(half * lanes, 128), lanes)] = src[
+                k, row0 : row0 + 16, :
+            ].astype(F32)[0:n]
 
 
 def shards(
@@ -752,6 +892,8 @@
     assert inner % CHUNK == 0 and inner // 128 <= states and rank + 2 * states <= XD
 
     pairs = [(i, i ^ 1) for i in range(ndev)]
+    turn = []
+    call = functools.partial(run, turn=turn)
 
     def to_runs(block):
         mine = lax.dynamic_index_in_dim(block, core, 0, keepdims=False)
@@ -804,13 +946,21 @@
         return lax.ppermute(block, AXIS, route)
 
     smem = pl.BlockSpec(memory_space=pltpu.SMEM)
+    core_s = (core[None].astype(jnp.int32), smem)
+
+    def swap(block):
+        return lax.ppermute(block, AXIS, pairs)
+
     pay = shape((states, inner + EXTRA), BF16)
 
-    def exchange(payload, a2, mode):
+    def exchange(payload, a2, mode, meanwhile=()):
+        meanwhile = dict(enumerate(meanwhile))
         befores = [[] for _ in mode]
         sums = [[] for _ in mode]
         for r, (low, group) in enumerate(rounds[:-1]):
             received = [payload] + [send(payload, r, m, "all") for m in range(1, group)]
+            if r in meanwhile:
+                meanwhile[r]()
             final = r + 2 == len(rounds)
             split = len(mode) == 2 and final
             nextgroup = rounds[r + 1][1] if split else 0
@@ -819,7 +969,7 @@
                 if split
                 else [shape((states * len(mode), inner + EXTRA), BF16)]
             )
-            outs = run(
+            outs = call(
                 functools.partial(k_join, group, nextgroup, mode),
                 pays
                 + [shape((states, inner), F32)] * len(mode)
@@ -830,7 +980,6 @@
                     pltpu.VMEM((group, 8, inner), F32),
                     pltpu.VMEM((states, inner + EXTRA), F32),
                 ],
-                flops=10**6,
             )
             sent, outs = outs[: len(pays)], outs[len(pays) :]
             for i in range(len(mode)):
@@ -843,6 +992,9 @@
         else:
             way = "up" if mode == "f" else "down"
             last = [send(payload, r, m, way) for m in range(1, rounds[r][1])]
+        for step in sorted(meanwhile):
+            if step >= r:
+                meanwhile[step]()
         return last, sum(befores, []), sum(sums, []), digits_of(r)
 
     a2_all = -jnp.exp(jnp.swapaxes(a_log, 1, 2)) * LOG2E
@@ -884,15 +1036,17 @@
     xd = [None, None]
     v = [None, None]
 
-    normed[0], xc[0], tail = run(
-        k_in, [res_b, act_b, edge], [x0, row(norm_gain, 0), w_in(0, 0)], flops=mm
+    normed[0], xc[0], tail = call(
+        k_in, [res_b, act_b, edge], [x0, row(norm_gain, 0), w_in(0, 0)]
     )
 
     def before_scan(l, tail, dgated=None):
         halo[l] = from_before(tail)
-        (z[l],) = run(k_gate, [act_b], [normed[l], w_in(l, 1)], flops=mm)
+        (z[l],) = call(k_gate, [act_b], [normed[l], w_in(l, 1)])
+        if l == 0:
+            (dgated1,) = call(k_dgated, [act], [grad_out, w_out(1)])
         both = dgated is not None
-        outs = run(
+        outs = call(
             functools.partial(k_local, rank, both),
             [
                 act_b,
@@ -916,61 +1070,93 @@
             + [pltpu.VMEM((rows, inner), F32)] * 2
             + table_scratch()
             + [pltpu.VMEM((states, inner), F32), pltpu.VMEM((states, inner + EXTRA), F32)],
-            flops=10**9,
+            cost=LONG,
         )
         u[l], xd[l], v[l] = outs[:3]
-        return outs[3:]
-
-    (dgated1,) = run(k_dgated, [act], [grad_out, w_out(1)], flops=mm)
+        return (outs[3], dgated1) if l == 0 else outs[3:]
 
     def join_scratch():
         group = rounds[-1][1]
         return [
-            pltpu.VMEM((group, states, inner + EXTRA), F32),
+            pltpu.VMEM((group, states, inner), F32),
             pltpu.VMEM((group, 8, inner), F32),
         ]
 
-    (payload,) = before_scan(0, tail)
-    last, befores, sums, digits = exchange(payload, a2_all[0], "f")
-    y0, gated0, x1, normed[1], xc[1], tail, h0 = run(
-        functools.partial(k_mix, rank, len(last), len(befores)),
-        [act, act_b, res, res_b, act_b, edge, shape((states, inner), F32)],
-        [(digits, smem)]
-        + last
-        + befores
-        + sums
-        + [
-            a2_all[0],
-            u[0],
-            v[0],
-            xd[0],
-            z[0],
-            x0,
-            row(skip_gain, 0),
-            w_out(0),
-            row(norm_gain, 1),
-            w_in(1, 0),
-        ],
-        [pltpu.VMEM((rows, inner), F32)] * 2 + table_scratch() + join_scratch(),
-        flops=10**9,
-    )
-    payload, dy1 = before_scan(1, tail, dgated1)
-    last, befores, sums, digits = exchange(payload, a2_all[1], "fb")
-
-    small = shape((rank + 2 * states + rank + states + taps + 4, inner), F32)
-
-    def backward(l, dy, last, befores, sums, digits, h_in):
-        final = h_in is None
-        n_low = len(rounds) - 1
-        outs = run(
-            functools.partial(k_back, rank, len(last), n_low, final),
-            ([act] if final else []) + [act, edge, small],
-            [(digits, smem)]
+    def mix(l, parts, extra, outs):
+        final = l == layers - 1
+        last, befores, sums, digits = parts
+        befores, sums = befores[: len(rounds) - 1], sums[: len(rounds) - 1]
+        return call(
+            functools.partial(k_mix, rank, final, len(last), len(befores)),
+            outs,
+            [(digits, smem), core_s]
             + last
             + befores
             + sums
+            + [a2_all[l], u[l], v[l], xd[l], z[l], residual[l], row(skip_gain, l), w_out(l)]
+            + extra,
+            ([act_scratch] if final else [])
+            + [pltpu.VMEM((rows, inner), BF16)]
+            + [act_scratch] * 2
+            + table_scratch()
+            + join_scratch(),
+            cost=LONG,
+        )
+
+    half_b = shape((rows, width), BF16)
+    entry = shape((states, inner), F32)
+    act_scratch = pltpu.VMEM((rows, inner), F32)
+    residual = [x0, None]
+    payload, dgated1 = before_scan(0, tail)
+    parts = exchange(payload, a2_all[0], "f")
+    y0, x1, normed[1], xc[1], tail, gated_keep, gated_send, h0 = mix(
+        0,
+        parts,
+        [row(norm_gain, 1), w_in(1, 0)],
+        [act, res, res_b, act_b, edge, half_b, half_b, entry],
+    )
+    residual[1] = x1
+    gated0_pair = (gated_keep, swap(gated_send))
+    payload, dy1 = before_scan(1, tail, dgated1)
+    parts = exchange(payload, a2_all[1], "fb")
+    n_small = rank + 2 * states + rank + states + taps + 4
+    small = shape((n_small, inner), F32)
+    small_pad = -(-n_small // (BLOCKS * 2)) * BLOCKS * 2 if n_small % BLOCKS else n_small
+
+    n_parts = 2
+    lanes = inner // n_parts
+
+    def scan(l, i, dy, parts, h_in):
+        last, befores, sums, digits = parts
+        n_low = len(rounds) - 1
+        cut = part((rows, lanes), (0, i))
+        cut_s = part((states, lanes), (0, i))
+        return call(
+            functools.partial(k_scan, rank, i * lanes, len(last), n_low),
+            [shape((rows, lanes), F32)] * 2 + [shape((states, lanes), F32), shape((rows, XD), F32)],
+            [(digits, smem)]
+            + last
+            + befores[-n_low:]
+            + sums[-n_low:]
+            + [(a2_all[l], cut_s), (u[l], cut), (v[l], cut), (dy, cut), (h_in, cut_s), xd[l]],
+            [pltpu.VMEM((rows, lanes), F32)] * 2
+            + table_scratch()
             + [
-                a2_all[l],
+                pltpu.VMEM((rounds[-1][1], states, lanes), F32),
+                pltpu.VMEM((rounds[-1][1], 8, lanes), F32),
+            ]
+            + [pltpu.VMEM((rows * states, 128), F32)] * 2
+            + [pltpu.VMEM((rows * states, CHUNK), F32)] * 2
+            + [pltpu.VMEM((states, lanes), F32)],
+            cost=LONG,
+        )
+
+    def post(l, scans, dy):
+        return call(
+            functools.partial(k_post, rank, n_parts),
+            [act, edge, small],
+            [outs[k] for k in range(4) for outs in scans]
+            + [
                 u[l],
                 v[l],
                 xd[l],
@@ -982,40 +1168,164 @@
                 xw_all[l],
                 dw_all[l],
                 row(skip_gain, l),
-            ]
-            + ([] if final else [h_in]),
-            [pltpu.VMEM((rows, inner), F32)] * 2
-            + table_scratch()
-            + join_scratch()
-            + [pltpu.VMEM((rows + HALO, inner), F32)]
-            + [pltpu.VMEM((rows, inner), F32)] * 2
-            + [pltpu.VMEM((states, inner), F32)]
-            + [pltpu.VMEM((rows * states, 128), F32)] * 2
-            + [pltpu.VMEM((rows * states, CHUNK), F32)] * 2
-            + [pltpu.VMEM((states, inner), F32)] * 2,
-            flops=2 * 10**9,
-        )
-        return outs
-
-    y1, dconv1, head1, small1 = backward(1, dy1, last, befores, sums, digits, None)
+            ],
+            [pltpu.VMEM((rows + HALO, inner), F32)],
+            cost=LONG,
+        )
+
+
+    def over(block, flip):
+        return lax.ppermute(block, AXIS, [(i, i ^ (flip << 1)) for i in range(ndev)])
+
+    place_s = (chip[None].astype(jnp.int32), smem)
+
+    def summed(matrices, smalls):
+        ins = []
+        each = width // BLOCKS
+        for (a, a_came), (b, b_came) in matrices:
+            ins += [a, a_came, b, b_came]
+        r = each * len(matrices)
+        if smalls is not None:
+            ins += list(smalls)
+            r += 16
+        has_small = smalls is not None
+        half = width // 2
+        if ndev != 2 * BLOCKS:
+            (mine,) = call(
+                functools.partial(k_chip_sum, len(matrices), has_small),
+                [shape((BLOCKS, r, width), F32)],
+                ins,
+            )
+            empty = jnp.zeros((2,) + mine.shape, F32)
+            total = lax.psum(lax.dynamic_update_index_in_dim(empty, mine, core, 0), AXIS)
+            total = total.astype(BF16)
+            for _ in range(5):
+                yield None
+            yield (
+                lax.dynamic_index_in_dim(total, core, 0, keepdims=False),
+                lax.dynamic_index_in_dim(total, 1 - core, 0, keepdims=False),
+            )
+            return
+        n = BLOCKS // 2
+        keep_a, keep_b, send_a, send_b = call(
+            functools.partial(k_first, len(matrices), has_small),
+            [shape((n, r, half), F32)] * 2 + [shape((n, r, half), BF16)] * 2,
+            [place_s] + ins,
+            [pltpu.VMEM((BLOCKS, r, width), F32)],
+        )
+        came_a, came_b = over(send_a, 1), over(send_b, 2)
+        yield None
+        n = BLOCKS // 4
+        stay_a, stay_b, send_a, send_b = call(
+            k_second,
+            [shape((n, r, half), F32)] * 2 + [shape((n, r, half), BF16)] * 2,
+            [place_s, keep_a, keep_b, came_a, came_b],
+        )
+        came_a, came_b = over(send_a, 2), over(send_b, 1)
+        yield None
+        keep, *sends = call(
+            k_third,
+            [shape((r, width), F32)] + [shape((r, width), BF16)] * 3,
+            [place_s, stay_a, stay_b, came_a, came_b],
+        )
+        came = [over(send_m, 4 * (m + 1)) for m, send_m in enumerate(sends)]
+        yield None
+        (done,) = call(k_fourth, [shape((r, width), BF16)], [keep] + came)
+        came = [over(done, 4 * m) for m in (1, 2, 3)]
+        yield None
+        left, right = call(k_stack, [shape((4, r, half), BF16)] * 2, [done] + came)
+        left_y, right_x = over(left, 2), over(right, 1)
+        lefts = [left, over(left, 1), left_y, over(left_y, 1)]
+        rights = [right, right_x, over(right, 2), over(right_x, 2)]
+        yield None
+        (mine,) = call(
+            k_chip, [shape((BLOCKS, r, width), BF16)], [place_s] + lefts + rights
+        )
+        yield mine, swap(mine)
+
+    def placed(halves, i, whole, block, index, split_rows, before):
+        each = width // BLOCKS
+        steps = 4
+        per = BLOCKS // steps
+        source = pl.BlockSpec((per, each, width), lambda g: (g, i, 0))
+        anywhere = pl.BlockSpec(memory_space=pl.ANY)
+        ins = [core_s[0], halves[0], halves[1], turn[0]]
+        specs = [smem, source, source, anywhere]
+        aliases = {}
+        if before is not None:
+            ins.append(before)
+            specs.append(anywhere)
+            aliases = {4: 0}
+        out, turn[0] = pl.pallas_call(
+            functools.partial(k_place, split_rows),
+            grid=(steps,),
+            in_specs=specs,
+            out_specs=[pl.BlockSpec(block, index), pl.BlockSpec((8, 128), lambda g: (0, 0))],
+            out_shape=[whole, shape((8, 128), F32)],
+            input_output_aliases=aliases,
+            compiler_params=pltpu.CompilerParams(vmem_limit_bytes=58 * 1024 * 1024),
+            cost_estimate=COST,
+        )(*ins)
+        return out
+
+    g_out_shape = shape((layers, 2, width, width), F32)
+    g_in_shape = shape((layers, width, 2 * inner), F32)
+    quarter = width // 4
+    out_block = (None, 2, quarter, width)
+    in_block = (None, quarter, inner)
+
+    def out_at(l):
+        return lambda g: (l, 0, g, 0)
+
+    def in_at(l, half):
+        return lambda g: (l, g, half)
+
+    def placed_small(halves, i):
+        each = width // BLOCKS
+        (out,) = call(
+            functools.partial(k_place_small, i * each),
+            [shape((small_pad, inner), F32)],
+            [core_s, halves[0], halves[1]],
+        )
+        return out
+
+    half_small = shape((small_pad, width), F32)
+    n1_pair = (normed[1], swap(normed[1]))
+    n0_pair = (normed[0], swap(normed[0]))
+    e1_pair = (grad_out, swap(grad_out))
+
+    hidden_out, dz1, dz_keep, dz_send, gated_keep, gated_send, h1 = mix(
+        1, parts, [dgated1], [res_b, act_b] + [half_b] * 4 + [entry]
+    )
+    a_sum = summed(
+        [((gated_keep, swap(gated_send)), e1_pair), (n1_pair, (dz_keep, swap(dz_send)))], None
+    )
+    scans = [scan(1, 0, dy1, parts, h1)]
+    next(a_sum)
+    scans.append(scan(1, 1, dy1, parts, h1))
+    next(a_sum)
+    dconv1, head1, small1 = post(1, scans, dy1)
     after1 = from_after(head1)
-    hidden_out, gated1, dz1, dnz1 = run(
-        k_out,
-        [res_b, act_b, act_b, res],
-        [x1, y1, z[1], dgated1, w_out(1), w_in(1, 1)],
-        flops=2 * mm,
-    )
-
-    def wgrad(a, b):
-        (out,) = run(
-            k_wgrad, [shape((a.shape[1], b.shape[1]), F32)], [a, b], flops=mm
-        )
-        return out
-
-    dxc1, gn1, e1, de0, dy0, dz0, payload = run(
+    (dnz1,) = call(k_dnz, [res], [dz1, w_in(1, 1)])
+    next(a_sum)
+    (
+        dxc_keep,
+        dxc_send,
+        small_keep,
+        small_send,
+        e1,
+        de0,
+        dy0,
+        dz0,
+        dz_keep,
+        dz_send,
+        payload,
+    ) = call(
         functools.partial(k_turn, rank),
-        [act_b, shape((1, width), F32), res, res_b, act, act_b, pay],
+        [half_b, half_b, half_small, half_small, res, res_b, act, act_b, half_b, half_b, pay],
         [
+            core_s,
+            small1,
             dconv1,
             after1,
             cw_all[1],
@@ -1031,37 +1341,74 @@
             xd[0],
             a2_all[0],
         ],
-        [pltpu.VMEM((rows + HALO, inner), F32), pltpu.VMEM((rows, inner), F32)]
+        [
+            pltpu.VMEM((n_small, inner), F32),
+            pltpu.VMEM((rows, inner), BF16),
+            pltpu.VMEM((rows + HALO, inner), F32),
+            pltpu.VMEM((rows, inner), F32),
+        ]
         + table_scratch()
         + [pltpu.VMEM((states, inner), F32), pltpu.VMEM((states, inner + EXTRA), F32)],
-        flops=10**9,
+        cost=LONG,
     )
-    g_out1 = wgrad(gated1, grad_out)
-    g_inz1 = wgrad(normed[1], dz1)
-    last, befores, sums, digits = exchange(payload, a2_all[0], "b")
-    g_inx1 = wgrad(normed[1], dxc1)
-    layer1 = lax.psum((g_out1, g_inz1, g_inx1, small1, gn1), AXIS)
-    (dnz0,) = run(k_dnz, [res], [dz0, w_in(0, 1)], flops=mm)
-    g_out0 = wgrad(gated0, de0)
-    g_inz0 = wgrad(normed[0], dz0)
-    dconv0, head0, small0 = backward(0, dy0, last, befores, sums, digits, h0)
+    b_sum = summed(
+        [
+            (n1_pair, (dxc_keep, swap(dxc_send))),
+            (gated0_pair, (de0, swap(de0))),
+            (n0_pair, (dz_keep, swap(dz_send))),
+        ],
+        (small_keep, swap(small_send)),
+    )
+    kept = {}
+
+    def first_shadow():
+        (kept["dnz0"],) = call(k_dnz, [res], [dz0, w_in(0, 1)])
+
+    def second_shadow():
+        next(b_sum)
+
+    parts = exchange(payload, a2_all[0], "b", (first_shadow, second_shadow))
+    dnz0 = kept["dnz0"]
+    next(a_sum)
+    scans = [scan(0, 0, dy0, parts, h0)]
+    next(a_sum)
+    next(b_sum)
+    scans.append(scan(0, 1, dy0, parts, h0))
+    next(b_sum)
+    dconv0, head0, small0 = post(0, scans, dy0)
     after0 = from_after(head0)
-    dxc0, gn0, e0 = run(
+    sum_a1 = next(a_sum)
+    dxc_keep, dxc_send, small_keep, small_send, e0 = call(
         k_end,
-        [act_b, shape((1, width), F32), res_b],
-        [dconv0, after0, cw_all[0], dnz0, w_in(0, 0), x0, row(norm_gain, 0), e1],
-        [pltpu.VMEM((rows + HALO, inner), F32)],
-        flops=mm,
+        [half_b, half_b, half_small, half_small, res_b],
+        [core_s, small0, dconv0, after0, cw_all[0], dnz0, w_in(0, 0), x0, row(norm_gain, 0), e1],
+        [
+            pltpu.VMEM((n_small, inner), F32),
+            pltpu.VMEM((rows, inner), BF16),
+            pltpu.VMEM((rows + HALO, inner), F32),
+        ],
+        cost=LONG,
     )
-    g_inx0 = wgrad(normed[0], dxc0)
-    layer0 = lax.psum((g_out0, g_inz0, g_inx0, small0, gn0), AXIS)
-
-    def stacked(i):
-        return jnp.stack([layer0[i], layer1[i]])
-
-    g_in = jnp.concatenate([stacked(1), stacked(2)][::-1], axis=2)
-    smalls = stacked(3)
-    at = 0
+    c_sum = summed([(n0_pair, (dxc_keep, swap(dxc_send)))], (small_keep, swap(small_send)))
+    next(c_sum)
+    g_out = placed(sum_a1, 0, g_out_shape, out_block, out_at(1), True, None)
+    next(b_sum)
+    next(c_sum)
+    g_in = placed(sum_a1, 1, g_in_shape, in_block, in_at(1, 1), False, None)
+    next(c_sum)
+    next(b_sum)
+    next(c_sum)
+    next(c_sum)
+    sum_b = next(b_sum)
+    small1 = placed_small(sum_b, 3)
+    g_in = placed(sum_b, 0, g_in_shape, in_block, in_at(1, 0), False, g_in)
+    g_out = placed(sum_b, 1, g_out_shape, out_block, out_at(0), True, g_out)
+    sum_c = next(c_sum)
+    g_in = placed(sum_b, 2, g_in_shape, in_block, in_at(0, 1), False, g_in)
+    g_in = placed(sum_c, 0, g_in_shape, in_block, in_at(0, 0), False, g_in)
+    small0 = placed_small(sum_c, 1)
+
+    smalls = jnp.stack([small0, small1])
     n_x = rank + 2 * states
     g_xw = jnp.swapaxes(smalls[:, 0:n_x], 1, 2)
     g_dw = smalls[:, n_x : n_x + rank]
@@ -1073,7 +1420,7 @@
     return (
         from_runs(hidden_out),
         from_runs(e0),
-        stacked(4)[:, 0],
+        smalls[:, n_small - 1, 0:width],
         g_in,
         g_cw,
         smalls[:, at],
@@ -1082,7 +1429,7 @@
         smalls[:, at + 1],
         g_al,
         smalls[:, at + 2],
-        stacked(0),
+        g_out.reshape(layers, inner, width),
     )
 
 

time: 809 us -> 581 us (0.72)
  waiting for transfers between devices: 430 us -> 96.3 us
  Pallas kernels: 217 us -> 320 us
  starting transfers between devices: 43.9 us -> 107 us
  blocking collectives: 45.3 us -> 0 us
  between operations: 14.9 us -> 2.03 us
  other arithmetic: 22.1 us -> 9.58 us
  local copies, waits for them, and re-layouts: 25.7 us -> 35.8 us
    psum x1 -> x0, waiting for transfers between devices: 417 us -> none  [shards(): layer1 = lax.psum((g_out1, g_inz1, g_inx1, small1, gn1), AXIS)]
    pallas_call x22 -> x47, Pallas kernels: 217 us -> 320 us  [the longest x41 293 us: run(): pl.pallas_call(body, grid=(1,), in_specs=specs, out_specs=out_specs, out_...]
    ppermute x0 -> x63, waiting for transfers between devices: none -> 72.9 us  [the longest x48 70.7 us: over(): return lax.ppermute(block, AXIS, [(i, i ^ flip << 1) for i in range(ndev)])]
    ppermute x0 -> x63, starting transfers between devices: none -> 64.4 us  [the longest x48 62.6 us: over(): return lax.ppermute(block, AXIS, [(i, i ^ flip << 1) for i in range(ndev)])]
    psum x1 -> x0, blocking collectives: 45.3 us -> none  [shards(): layer1 = lax.psum((g_out1, g_inz1, g_inx1, small1, gn1), AXIS)]
    unnamed x83 -> x229, local copies, waits for them, and re-layouts: 12.6 us -> 27.2 us
  transfers between devices with their start and end apart: 27 -> 89, of which waited for: 12 -> 30; matrix products, arithmetic and copies ran while one was open for 2% -> 2% of each run, Pallas kernels for 6% -> 38%
where the time goes in v1:
time: 581 us; the launch traced here: 571 us
  Pallas kernels  320 us (55%)
  starting transfers between devices  107 us (18%)
  waiting for transfers between devices  96.3 us (17%)
  local copies, waits for them, and re-layouts  35.8 us (6%)
  other arithmetic  9.58 us (2%)
    pallas_call x41, Pallas kernels, run(): pl.pallas_call(body, grid=(1,), in_specs=specs, out_specs=out_specs, out_...  293 us
    ppermute x48, waiting for transfers between devices, over(): return lax.ppermute(block, AXIS, [(i, i ^ flip << 1) for i in range(ndev)])  70.7 us
    ppermute x48, starting transfers between devices, over(): return lax.ppermute(block, AXIS, [(i, i ^ flip << 1) for i in range(ndev)])  62.6 us
    ppermute x18, starting transfers between devices, send(): return lax.ppermute(block, AXIS, route)  30.8 us
    unnamed x229, local copies, waits for them, and re-layouts  27.2 us
    pallas_call x6, Pallas kernels, placed(): pl.pallas_call(functools.partial(k_place, split_rows), grid=(steps,), in_...  26.8 us
    ppermute x18, waiting for transfers between devices, send(): return lax.ppermute(block, AXIS, route)  16.3 us
  transfers between devices with their start and end apart: 89, of which 30 were waited for; matrix products, arithmetic and copies ran while one was open for 2% of the time, Pallas kernels for 38%

profile of v1, /device:TPU:0, one launch (start us, length us, event | category | flops | bytes accessed | tf_op | source)
XLA Modules:
  0.0 571.1 jit_solution(8770065267464193630)
XLA Ops:
  16.0 4.8 collective-permute-start.1
  29.6 14.3 %shard_map.214 = (bf16[256,1536]{1,0:T(8,128)(2,1)}, bf16[256,128]{1,0:T(8,128)(2,1)}, f32[256,1536]{1,0:T(8,128)}, bf16[16,1792]{1,0:T(8,128)(2,1)}) custom-call(f32[8,1536]{1,0:T(8,128)} %copy-done.65, bf16[256,1536]{1,0:T(8,128)(2,1)} %get-tuple-element.145.refs_1_.refs_13_, f32[4,1536]{1,0:T(4,128)} %get-tuple-element.294.refs_2_.refs_14_.refs_4_, ...), custom_call_target="tpu_custom_call" | custom-call | flops 1 | bytes 100000000 | tf_op jit(solution)/shard_map/pallas_call | solution.py:55
  53.8 5.4 collective-permute-start.8
  65.7 19.9 %shard_map.216 = (f32[256,1536]{1,0:T(8,128)}, f32[256,768]{1,0:T(8,128)}, bf16[256,768]{1,0:T(8,128)(2,1)}, bf16[256,1536]{1,0:T(8,128)(2,1)}, f32[8,1536]{1,0:...) custom-call(s32[2]{0:T(128)} %pad_add_fusion.refs_0_, ...), custom_call_target="tpu_custom_call" | custom-call | flops 1 | bytes 100000000 | tf_op jit(solution)/shard_map/pallas_call | solution.py:55
  92.7 23.8 %shard_map.218 = (bf16[256,1536]{1,0:T(8,128)(2,1)}, bf16[256,128]{1,0:T(8,128)(2,1)}, f32[256,1536]{1,0:T(8,128)}, bf16[32,1792]{1,0:T(8,128)(2,1)}, f32[256,1536]{1,0:T(8,128)}) custom-call(f32[8,1536]{1,0:T(8,128)} %copy-done.64, bf16[256,1536]{1,0:T(8,128)(2,1)} %get-tuple-element.155.refs_1_.refs_13_, ...), custom_call_target="tpu_custom_call" | custom-call | flops 1 | bytes 100000000 | tf_op jit(solution)/shard_map/pallas_call | solution.py:55
  136.7 19.2 %shard_map.220 = (bf16[256,768]{1,0:T(8,128)(2,1)}, bf16[256,1536]{1,0:T(8,128)(2,1)}, bf16[256,768]{1,0:T(8,128)(2,1)}, bf16[256,768]{1,0:T(8,128)(2,1)}, bf16[...) custom-call(s32[2]{0:T(128)} %pad_add_fusion.refs_0_, s32[1]{0:T(128)} %bitcast.1.refs_1_.refs_0_.core, ...), custom_call_target="tpu_custom_call" | custom-call | flops 1 | bytes 100000000 | tf_op jit(solution)/shard_map/pallas_call | solution.py:55
  156.4 19.0 %shard_map.221 = (f32[256,768]{1,0:T(8,128)}, f32[256,768]{1,0:T(8,128)}, f32[16,768]{1,0:T(8,128)}, f32[256,128]{1,0:T(8,128)}) custom-call(s32[2]{0:T(128)} %pad_add_fusion.refs_0_, bf16[16,1792]{1,0:T(8,128)(2,1)} %copy-done.17, bf16[16,1792]{1,0:T(8,128)(2,1)} %copy-done.18, bf16[16,1792]{1,0:T(8,128)(2,1)} %copy-done.19, ...), custom_call_target="tpu_custom_call" | custom-call | flops 1 | bytes 100000000 | tf_op jit(solution)/shard_map/pallas_call | solution.py:55
  176.6 5.7 shard_map.222
  184.4 19.0 %shard_map.223 = (f32[256,768]{1,0:T(8,128)}, f32[256,768]{1,0:T(8,128)}, f32[16,768]{1,0:T(8,128)}, f32[256,128]{1,0:T(8,128)}) custom-call(s32[2]{0:T(128)} %pad_add_fusion.refs_0_, bf16[16,1792]{1,0:T(8,128)(2,1)} %copy-done.17, bf16[16,1792]{1,0:T(8,128)(2,1)} %copy-done.18, bf16[16,1792]{1,0:T(8,128)(2,1)} %copy-done.19, ...), custom_call_target="tpu_custom_call" | custom-call | flops 1 | bytes 100000000 | tf_op jit(solution)/shard_map/pallas_call | solution.py:55
  209.7 9.5 %shard_map.225 = (f32[256,1536]{1,0:T(8,128)}, f32[8,1536]{1,0:T(8,128)}, f32[152,1536]{1,0:T(8,128)}) custom-call(f32[256,768]{1,0:T(8,128)} %get-tuple-element.173.refs_0_, f32[256,768]{1,0:T(8,128)} %get-tuple-element.180.refs_1_, f32[256,768]{1,0:T(8,128)} %get-tuple-element.181.refs_2_, f32[256,768]{1,0:T(8,128)} %get-tuple-element.182.refs_3_, ...), custom_call_target="tpu_custom_call" | custom-call | flops 1 | bytes 100000000 | tf_op jit(solution)/shard_map/pallas_call | solution.py:55
  228.1 20.9 %shard_map.228 = (bf16[256,768]{1,0:T(8,128)(2,1)}, bf16[256,768]{1,0:T(8,128)(2,1)}, f32[160,768]{1,0:T(8,128)}, f32[160,768]{1,0:T(8,128)}, f32[256,768]{1,0:T...) custom-call(s32[1]{0:T(128)} %bitcast.1.refs_1_.refs_0_.core, ...), custom_call_target="tpu_custom_call" | custom-call | flops 1 | bytes 100000000 | tf_op jit(solution)/shard_map/pallas_call | solution.py:55
  265.0 8.6 %shard_map.231 = (f32[8,160,384]{2,1,0:T(8,128)}, f32[8,160,384]{2,1,0:T(8,128)}, bf16[8,160,384]{2,1,0:T(8,128)(2,1)}, bf16[8,160,384]{2,1,0:T(8,128)(2,1)}) custom-call(s32[1]{0:T(128)} %bitcast.22.refs_0_, bf16[256,768]{1,0:T(8,128)(2,1)} %get-tuple-element.156.refs_0_.refs_5_.refs_1_, bf16[256,768]{1,0:T(8,128)(2,1)} %copy-done.10, ...), custom_call_target="tpu_custom_call" | custom-call | flops 1 | bytes 1 | tf_op jit(solution)/shard_map/pallas_call | solution.py:55
  285.7 7.5 %collective-permute-done.33.refs_2_ = bf16[96,768]{1,0:T(8,128)(2,1)S(1)} collective-permute-done((bf16[96,768]{1,0:T(8,128)(2,1)S(1)}, bf16[96,768]{1,0:T(8,128)(2,1)S(1)}, u32[]{:S(2)}, u32[]{:S(2)}) %collective-permute-start.33) | collective-permute-done | bytes 147488 | tf_op jit(solution)/shard_map/ppermute | solution.py:1178
  297.7 5.6 collective-permute-start.45
  304.4 19.3 %shard_map.233 = (f32[256,768]{1,0:T(8,128)}, f32[256,768]{1,0:T(8,128)}, f32[16,768]{1,0:T(8,128)}, f32[256,128]{1,0:T(8,128)}) custom-call(s32[2]{0:T(128)} %pad_add_fusion.refs_0_, bf16[16,1792]{1,0:T(8,128)(2,1)} %copy-done.63, bf16[16,1792]{1,0:T(8,128)(2,1)} %copy-done.62, bf16[16,1792]{1,0:T(8,128)(2,1)} %copy-done.61, ...), custom_call_target="tpu_custom_call" | custom-call | flops 1 | bytes 100000000 | tf_op jit(solution)/shard_map/pallas_call | solution.py:55
  337.1 13.3 %collective-permute-done.50.refs_3_ = bf16[4,96,384]{2,1,0:T(8,128)(2,1)S(1)} collective-permute-done((bf16[4,96,384]{2,1,0:T(8,128)(2,1)S(1)}, bf16[4,96,384]{2,1,0:T(8,128)(2,1)S(1)}, u32[]{:S(2)}, u32[]{:S(2)}) %collective-permute-start.50) | collective-permute-done | bytes 294944 | tf_op jit(solution)/shard_map/ppermute | solution.py:1178
  353.0 18.9 %shard_map.236 = (f32[256,768]{1,0:T(8,128)}, f32[256,768]{1,0:T(8,128)}, f32[16,768]{1,0:T(8,128)}, f32[256,128]{1,0:T(8,128)}) custom-call(s32[2]{0:T(128)} %pad_add_fusion.refs_0_, bf16[16,1792]{1,0:T(8,128)(2,1)} %copy-done.63, bf16[16,1792]{1,0:T(8,128)(2,1)} %copy-done.62, bf16[16,1792]{1,0:T(8,128)(2,1)} %copy-done.61, ...), custom_call_target="tpu_custom_call" | custom-call | flops 1 | bytes 100000000 | tf_op jit(solution)/shard_map/pallas_call | solution.py:55
  375.7 9.5 %shard_map.238 = (f32[256,1536]{1,0:T(8,128)}, f32[8,1536]{1,0:T(8,128)}, f32[152,1536]{1,0:T(8,128)}) custom-call(f32[256,768]{1,0:T(8,128)} %get-tuple-element.218.refs_0_, f32[256,768]{1,0:T(8,128)} %get-tuple-element.225.refs_1_, f32[256,768]{1,0:T(8,128)} %get-tuple-element.226.refs_2_, f32[256,768]{1,0:T(8,128)} %get-tuple-element.227.refs_3_, ...), custom_call_target="tpu_custom_call" | custom-call | flops 1 | bytes 100000000 | tf_op jit(solution)/shard_map/pallas_call | solution.py:55
  396.1 6.1 %shard_map.240 = (bf16[256,768]{1,0:T(8,128)(2,1)}, bf16[256,768]{1,0:T(8,128)(2,1)}, f32[160,768]{1,0:T(8,128)}, f32[160,768]{1,0:T(8,128)}, bf16[256,768]{1,0:T(8,128)(2,1)}) custom-call(s32[1]{0:T(128)} %bitcast.1.refs_1_.refs_0_.core, f32[152,1536]{1,0:T(8,128)} %get-tuple-element.235.refs_9_.refs_1_, f32[256,1536]{1,0:T(8,128)} %get-tuple-element.236.refs_2_, ...), custom_call_target="tpu_custom_call" | custom-call | flops 1 | bytes 100000000 | tf_op jit(solution)/shard_map/pallas_call | solution.py:55
  426.2 9.8 %collective-permute-done.61.refs_2_ = bf16[160,768]{1,0:T(8,128)(2,1)S(1)} collective-permute-done((bf16[160,768]{1,0:T(8,128)(2,1)S(1)}, bf16[160,768]{1,0:T(8,128)(2,1)S(1)}, u32[]{:S(2)}, u32[]{:S(2)}) %collective-permute-start.61) | collective-permute-done | bytes 245792 | tf_op jit(solution)/shard_map/ppermute | solution.py:1178
  441.8 5.2 collective-permute-start.70
  473.8 6.0 %collective-permute-done.82.refs_3_ = bf16[4,160,384]{2,1,0:T(8,128)(2,1)S(1)} collective-permute-done((bf16[4,160,384]{2,1,0:T(8,128)(2,1)}, bf16[4,160,384]{2,1,0:T(8,128)(2,1)S(1)}, u32[]{:S(2)}, u32[]{:S(2)}) %collective-permute-start.82) | collective-permute-done | bytes 491552 | tf_op jit(solution)/shard_map/ppermute | solution.py:1178
  497.5 6.4 %collective-permute-done.73.refs_2_ = bf16[64,768]{1,0:T(8,128)(2,1)S(1)} collective-permute-done((bf16[64,768]{1,0:T(8,128)(2,1)}, bf16[64,768]{1,0:T(8,128)(2,1)S(1)}, u32[]{:S(2)}, u32[]{:S(2)}) %collective-permute-start.73) | collective-permute-done | bytes 98336 | tf_op jit(solution)/shard_map/ppermute | solution.py:1178
  503.9 4.8 collective-permute-done.72.refs_1_
  (458 shorter events, 286.5 us)
Async XLA Ops:
  132.5 42.9 %collective-permute-start.18 = (bf16[256,768]{1,0:T(8,128)(2,1)S(1)}, bf16[256,768]{1,0:T(8,128)(2,1)S(1)}, u32[]{:S(2)}, u32[]{:S(2)}) collective-permute-start(bf16[256,768]{1,0:T(8,128)(2,1)S(1)} %copy-done.4), channel_id=1, source_target_pairs={{0,1},{1,0},{2,3},{3,2},{4,5},{5,4},{6,7},{7,6},{8,9},{9,8},{10,11... | collective-permute-start | bytes 1179656 | tf_op jit(solution)/shard_map/ppermute | solution.py:952
  132.5 43.0 %collective-permute-start.19 = (bf16[256,768]{1,0:T(8,128)(2,1)S(1)}, bf16[256,768]{1,0:T(8,128)(2,1)S(1)}, u32[]{:S(2)}, u32[]{:S(2)}) collective-permute-start(bf16[256,768]{1,0:T(8,128)(2,1)S(1)} %copy-done.7), channel_id=1, source_target_pairs={{0,1},{1,0},{2,3},{3,2},{4,5},{5,4},{6,7},{7,6},{8,9},{9,8},{10,11... | collective-permute-start | bytes 1179656 | tf_op jit(solution)/shard_map/ppermute | solution.py:952
  182.3 21.1 %collective-permute-start.21 = (bf16[8,96,384]{2,1,0:T(8,128)(2,1)}, bf16[8,96,384]{2,1,0:T(8,128)(2,1)S(1)}, u32[]{:S(2)}, u32[]{:S(2)}) collective-permute-start(bf16[8,96,384]{2,1,0:T(8,128)(2,1)} %get-tuple-element.188), channel_id=1, source_target_pairs={{0,2},{1,3},{2,0},{3,1},{4,6},{5,7},{6,4},{7,5},{8,10},{9,11},{10,... | collective-permute-start | bytes 1769480 | tf_op jit(solution)/shard_map/ppermute | solution.py:1178
  184.4 70.1 %collective-permute-start.38 = (bf16[256,768]{1,0:T(8,128)(2,1)S(1)}, bf16[256,768]{1,0:T(8,128)(2,1)S(1)}, u32[]{:S(2)}, u32[]{:S(2)}) collective-permute-start(bf16[256,768]{1,0:T(8,128)(2,1)S(1)} %copy-done.6), channel_id=1, source_target_pairs={{0,1},{1,0},{2,3},{3,2},{4,5},{5,4},{6,7},{7,6},{8,9},{9,8},{10,11... | collective-permute-start | bytes 1179656 | tf_op jit(solution)/shard_map/ppermute | solution.py:952
  273.7 52.8 %collective-permute-start.41 = (bf16[8,160,384]{2,1,0:T(8,128)(2,1)}, bf16[8,160,384]{2,1,0:T(8,128)(2,1)S(1)}, u32[]{:S(2)}, u32[]{:S(2)}) collective-permute-start(bf16[8,160,384]{2,1,0:T(8,128)(2,1)} %get-tuple-element.221), channel_id=1, source_target_pairs={{0,2},{1,3},{2,0},{3,1},{4,6},{5,7},{6,4},{7,5},{8,10},{9,11},{10,... | collective-permute-start | bytes 2949128 | tf_op jit(solution)/shard_map/ppermute | solution.py:1178
  274.9 51.6 %collective-permute-start.42 = (bf16[8,160,384]{2,1,0:T(8,128)(2,1)}, bf16[8,160,384]{2,1,0:T(8,128)(2,1)S(1)}, u32[]{:S(2)}, u32[]{:S(2)}) collective-permute-start(bf16[8,160,384]{2,1,0:T(8,128)(2,1)} %get-tuple-element.217.refs_4_), channel_id=1, source_target_pairs={{0,4},{1,5},{2,6},{3,7},{4,0},{5,1},{6,2},{7,3},{8,12},{9,13},{10,... | collective-permute-start | bytes 2949128 | tf_op jit(solution)/shard_map/ppermute | solution.py:1178
  297.7 26.0 %collective-permute-start.45 = (bf16[96,768]{1,0:T(8,128)(2,1)}, bf16[96,768]{1,0:T(8,128)(2,1)S(1)}, u32[]{:S(2)}, u32[]{:S(2)}) collective-permute-start(bf16[96,768]{1,0:T(8,128)(2,1)} %shard_map.232.refs_12_.refs_0_), channel_id=1, source_target_pairs={{0,24},{1,25},{2,26},{3,27},{4,28},{5,29},{6,30},{7,31},{8,16},{9,... | collective-permute-start | bytes 442376 | tf_op jit(solution)/shard_map/ppermute | solution.py:1178
  335.0 36.9 %collective-permute-start.47 = (bf16[4,160,384]{2,1,0:T(8,128)(2,1)}, bf16[4,160,384]{2,1,0:T(8,128)(2,1)S(1)}, u32[]{:S(2)}, u32[]{:S(2)}) collective-permute-start(bf16[4,160,384]{2,1,0:T(8,128)(2,1)} %get-tuple-element.224.refs_12_), channel_id=1, source_target_pairs={{0,2},{1,3},{2,0},{3,1},{4,6},{5,7},{6,4},{7,5},{8,10},{9,11},{10,... | collective-permute-start | bytes 1474568 | tf_op jit(solution)/shard_map/ppermute | solution.py:1178
  336.5 48.7 %collective-permute-start.49 = (bf16[4,96,384]{2,1,0:T(8,128)(2,1)S(1)}, bf16[4,96,384]{2,1,0:T(8,128)(2,1)S(1)}, u32[]{:S(2)}, u32[]{:S(2)}) collective-permute-start(bf16[4,96,384]{2,1,0:T(8,128)(2,1)S(1)} %copy-done.44), channel_id=1, source_target_pairs={{0,2},{1,3},{2,0},{3,1},{4,6},{5,7},{6,4},{7,5},{8,10},{9,11},{10,... | collective-permute-start | bytes 884744 | tf_op jit(solution)/shard_map/ppermute | solution.py:1178
  350.3 34.9 %collective-permute-start.53 = (bf16[4,96,384]{2,1,0:T(8,128)(2,1)S(1)}, bf16[4,96,384]{2,1,0:T(8,128)(2,1)S(1)}, u32[]{:S(2)}, u32[]{:S(2)}) collective-permute-start(bf16[4,96,384]{2,1,0:T(8,128)(2,1)S(1)} %copy-done.11), channel_id=1, source_target_pairs={{0,4},{1,5},{2,6},{3,7},{4,0},{5,1},{6,2},{7,3},{8,12},{9,13},{10,... | collective-permute-start | bytes 884744 | tf_op jit(solution)/shard_map/ppermute | solution.py:1178
  351.1 34.1 %collective-permute-start.51 = (bf16[4,96,384]{2,1,0:T(8,128)(2,1)S(1)}, bf16[4,96,384]{2,1,0:T(8,128)(2,1)S(1)}, u32[]{:S(2)}, u32[]{:S(2)}) collective-permute-start(bf16[4,96,384]{2,1,0:T(8,128)(2,1)S(1)} %collective-permute-done.50.refs_3_), channel_id=1, source_target_pairs={{0,2},{1,3},{2,0},{3,1},{4,6},{5,7},{6,4},{7,5},{8,10},{9,11},{10,... | collective-permute-start | bytes 884744 | tf_op jit(solution)/shard_map/ppermute | solution.py:1178
  351.7 33.6 %collective-permute-start.54 = (bf16[4,96,384]{2,1,0:T(8,128)(2,1)S(1)}, bf16[4,96,384]{2,1,0:T(8,128)(2,1)S(1)}, u32[]{:S(2)}, u32[]{:S(2)}) collective-permute-start(bf16[4,96,384]{2,1,0:T(8,128)(2,1)S(1)} %collective-permute-done.52.refs_6_), channel_id=1, source_target_pairs={{0,4},{1,5},{2,6},{3,7},{4,0},{5,1},{6,2},{7,3},{8,12},{9,13},{10,... | collective-permute-start | bytes 884744 | tf_op jit(solution)/shard_map/ppermute | solution.py:1178
  389.4 27.7 %collective-permute-start.63 = (bf16[16,96,768]{2,1,0:T(8,128)(2,1)}, bf16[16,96,768]{2,1,0:T(8,128)(2,1)S(1)}, u32[]{:S(2)}, u32[]{:S(2)}) collective-permute-start(bf16[16,96,768]{2,1,0:T(8,128)(2,1)} %shard_map.239.refs_10_.mine), channel_id=1, source_target_pairs={{0,1},{1,0},{2,3},{3,2},{4,5},{5,4},{6,7},{7,6},{8,9},{9,8},{10,11... | collective-permute-start | bytes 7077896 | tf_op jit(solution)/shard_map/ppermute | solution.py:952
  410.2 37.4 %collective-permute-start.58 = (bf16[8,64,384]{2,1,0:T(8,128)(2,1)}, bf16[8,64,384]{2,1,0:T(8,128)(2,1)S(1)}, u32[]{:S(2)}, u32[]{:S(2)}) collective-permute-start(bf16[8,64,384]{2,1,0:T(8,128)(2,1)} %get-tuple-element.247), channel_id=1, source_target_pairs={{0,2},{1,3},{2,0},{3,1},{4,6},{5,7},{6,4},{7,5},{8,10},{9,11},{10,... | collective-permute-start | bytes 1179656 | tf_op jit(solution)/shard_map/ppermute | solution.py:1178
  412.5 35.0 %collective-permute-start.59 = (bf16[8,64,384]{2,1,0:T(8,128)(2,1)}, bf16[8,64,384]{2,1,0:T(8,128)(2,1)S(1)}, u32[]{:S(2)}, u32[]{:S(2)}) collective-permute-start(bf16[8,64,384]{2,1,0:T(8,128)(2,1)} %get-tuple-element.248.refs_0_), channel_id=1, source_target_pairs={{0,4},{1,5},{2,6},{3,7},{4,0},{5,1},{6,2},{7,3},{8,12},{9,13},{10,... | collective-permute-start | bytes 1179656 | tf_op jit(solution)/shard_map/ppermute | solution.py:1178
  415.7 20.3 %collective-permute-start.61 = (bf16[160,768]{1,0:T(8,128)(2,1)S(1)}, bf16[160,768]{1,0:T(8,128)(2,1)S(1)}, u32[]{:S(2)}, u32[]{:S(2)}) collective-permute-start(bf16[160,768]{1,0:T(8,128)(2,1)S(1)} %copy-done.106), channel_id=1, source_target_pairs={{0,16},{1,17},{2,18},{3,19},{4,20},{5,21},{6,22},{7,23},{8,24},{9,... | collective-permute-start | bytes 737288 | tf_op jit(solution)/shard_map/ppermute | solution.py:1178
  438.9 21.2 %collective-permute-start.71 = (bf16[160,768]{1,0:T(8,128)(2,1)}, bf16[160,768]{1,0:T(8,128)(2,1)S(1)}, u32[]{:S(2)}, u32[]{:S(2)}) collective-permute-start(bf16[160,768]{1,0:T(8,128)(2,1)} %shard_map.243.refs_5_.refs_0_), channel_id=1, source_target_pairs={{0,24},{1,25},{2,26},{3,27},{4,28},{5,29},{6,30},{7,31},{8,16},{9,... | collective-permute-start | bytes 737288 | tf_op jit(solution)/shard_map/ppermute | solution.py:1178
  441.8 20.5 %collective-permute-start.70 = (bf16[160,768]{1,0:T(8,128)(2,1)}, bf16[160,768]{1,0:T(8,128)(2,1)S(1)}, u32[]{:S(2)}, u32[]{:S(2)}) collective-permute-start(bf16[160,768]{1,0:T(8,128)(2,1)} %shard_map.243.refs_5_.refs_0_), channel_id=1, source_target_pairs={{0,16},{1,17},{2,18},{3,19},{4,20},{5,21},{6,22},{7,23},{8,24},{9,... | collective-permute-start | bytes 737288 | tf_op jit(solution)/shard_map/ppermute | solution.py:1178
  469.5 41.7 %collective-permute-start.81 = (bf16[4,160,384]{2,1,0:T(8,128)(2,1)}, bf16[4,160,384]{2,1,0:T(8,128)(2,1)S(1)}, u32[]{:S(2)}, u32[]{:S(2)}) collective-permute-start(bf16[4,160,384]{2,1,0:T(8,128)(2,1)} %get-tuple-element.265.refs_1_), channel_id=1, source_target_pairs={{0,2},{1,3},{2,0},{3,1},{4,6},{5,7},{6,4},{7,5},{8,10},{9,11},{10,... | collective-permute-start | bytes 1474568 | tf_op jit(solution)/shard_map/ppermute | solution.py:1178
  471.7 39.5 %collective-permute-start.85 = (bf16[4,160,384]{2,1,0:T(8,128)(2,1)}, bf16[4,160,384]{2,1,0:T(8,128)(2,1)S(1)}, u32[]{:S(2)}, u32[]{:S(2)}) collective-permute-start(bf16[4,160,384]{2,1,0:T(8,128)(2,1)} %get-tuple-element.262.refs_4_.refs_5_), channel_id=1, source_target_pairs={{0,4},{1,5},{2,6},{3,7},{4,0},{5,1},{6,2},{7,3},{8,12},{9,13},{10,... | collective-permute-start | bytes 1474568 | tf_op jit(solution)/shard_map/ppermute | solution.py:1178
  479.7 31.5 %collective-permute-start.83 = (bf16[4,160,384]{2,1,0:T(8,128)(2,1)S(1)}, bf16[4,160,384]{2,1,0:T(8,128)(2,1)S(1)}, u32[]{:S(2)}, u32[]{:S(2)}) collective-permute-start(bf16[4,160,384]{2,1,0:T(8,128)(2,1)S(1)} %collective-permute-done.82.refs_3_), channel_id=1, source_target_pairs={{0,2},{1,3},{2,0},{3,1},{4,6},{5,7},{6,4},{7,5},{8,10},{9,11},{10,... | collective-permute-start | bytes 1474568 | tf_op jit(solution)/shard_map/ppermute | solution.py:1178
  480.3 31.0 %collective-permute-start.86 = (bf16[4,160,384]{2,1,0:T(8,128)(2,1)S(1)}, bf16[4,160,384]{2,1,0:T(8,128)(2,1)S(1)}, u32[]{:S(2)}, u32[]{:S(2)}) collective-permute-start(bf16[4,160,384]{2,1,0:T(8,128)(2,1)S(1)} %collective-permute-done.84.refs_6_), channel_id=1, source_target_pairs={{0,4},{1,5},{2,6},{3,7},{4,0},{5,1},{6,2},{7,3},{8,12},{9,13},{10,... | collective-permute-start | bytes 1474568 | tf_op jit(solution)/shard_map/ppermute | solution.py:1178
  519.0 23.0 %collective-permute-start.75 = (bf16[4,64,384]{2,1,0:T(8,128)(2,1)S(1)}, bf16[4,64,384]{2,1,0:T(8,128)(2,1)S(1)}, u32[]{:S(2)}, u32[]{:S(2)}) collective-permute-start(bf16[4,64,384]{2,1,0:T(8,128)(2,1)S(1)} %copy-done.68), channel_id=1, source_target_pairs={{0,2},{1,3},{2,0},{3,1},{4,6},{5,7},{6,4},{7,5},{8,10},{9,11},{10,... | collective-permute-start | bytes 589832 | tf_op jit(solution)/shard_map/ppermute | solution.py:1178
  519.9 22.1 %collective-permute-start.79 = (bf16[4,64,384]{2,1,0:T(8,128)(2,1)S(1)}, bf16[4,64,384]{2,1,0:T(8,128)(2,1)S(1)}, u32[]{:S(2)}, u32[]{:S(2)}) collective-permute-start(bf16[4,64,384]{2,1,0:T(8,128)(2,1)S(1)} %copy-done.14), channel_id=1, source_target_pairs={{0,4},{1,5},{2,6},{3,7},{4,0},{5,1},{6,2},{7,3},{8,12},{9,13},{10,... | collective-permute-start | bytes 589832 | tf_op jit(solution)/shard_map/ppermute | solution.py:1178
  (177 other events, 1187.1 us)

commit v2 on v1

--- a/solution.py
+++ b/solution.py
@@ -15,7 +15,7 @@
 AXIS = "seq"
 XD = 128
 EXTRA = 256
-CHUNK = 256
+CHUNK = 512
 UNROLL = 8
 HALO = 8
 COST = pl.CostEstimate(flops=1, bytes_accessed=1, transcendentals=0)
@@ -32,25 +32,36 @@
     return pl.BlockSpec(shape, lambda i, index=index: index)
 
 
+class Row:
+    def __init__(self, array, index):
+        self.array, self.index = array, index
+
+
 def run(kernel, outs, ins, scratch=(), turn=None, cost=COST):
     out_specs = [o[1] if isinstance(o, tuple) else full(o) for o in outs]
     outs = [o[0] if isinstance(o, tuple) else o for o in outs]
-    arrays, specs = [], []
+    arrays, specs, picks = [], [], {}
     for item in ins:
+        if isinstance(item, Row):
+            picks[len(arrays)] = item.index
+            item = item.array
         if isinstance(item, tuple):
             arrays.append(item[0])
             specs.append(item[1])
         else:
             arrays.append(item)
             specs.append(full(item))
-    body = kernel
+    n = len(arrays)
     if turn:
-        n = len(arrays)
         arrays.append(turn[0])
         specs.append(pl.BlockSpec(memory_space=pl.ANY))
-
-        def body(*refs):
-            kernel(*refs[:n], *refs[n + 1 :])
+    after = len(arrays)
+
+    def body(*refs):
+        given = list(refs[:n])
+        for k, index in picks.items():
+            given[k] = given[k].at[index : index + 1, :]
+        kernel(*given, *refs[after:])
 
     results = pl.pallas_call(
         body,
@@ -482,11 +493,11 @@
     a2, u_ref, v_ref, xd_ref, z_ref, x_ref, sk_ref, ow_ref = refs[:8]
     refs = refs[8:]
     if last:
-        dgated_ref, hid_ref, dz_ref, dz_keep, dz_send, gated_keep, gated_send, h_in_ref = refs[:8]
-        y_ref, refs = refs[8], refs[9:]
+        dgated_ref, hid_mine, hid_other, dz_ref, dz_keep, gated_keep, sends, h_in_ref = refs[:8]
+        y_ref, hid_s, refs = refs[8], refs[9], refs[10:]
     else:
         g_ref, iw_ref, y_ref, x1_ref, n_ref, xc_ref, tail_ref = refs[:7]
-        gated_keep, gated_send, h_in_ref = refs[7:10]
+        gated_keep, sends, h_in_ref = refs[7:10]
         refs = refs[10:]
     gated_s, dt_s, dtu_s, xdf_s, lhs_s, bc_s, states_s, totals_s = refs
     h_in_ref[...] = entering(received, a2, digits[0], befores, sums, states_s, totals_s, False)
@@ -502,19 +513,23 @@
     s = sigmoid(zf)
     gated = (y * (zf * s)).astype(BF16)
     gated_s[...] = gated
+    rows = gated.shape[0]
     gated_keep[...] = lane_half(gated_s, core[0])
-    gated_send[...] = lane_half(gated_s, 1 - core[0])
+    sends[0:rows, :] = lane_half(gated_s, 1 - core[0])
     x1 = x_ref[...] + dot(gated, ow_ref[...])
     if last:
         dz_ref[...] = (dgated_ref[...] * y * (s * (1.0 + zf * (1.0 - s)))).astype(BF16)
         dz_keep[...] = lane_half(dz_ref, core[0])
-        dz_send[...] = lane_half(dz_ref, 1 - core[0])
-        hid_ref[...] = x1.astype(BF16)
+        sends[rows:, :] = lane_half(dz_ref, 1 - core[0])
+        hid_s[...] = x1
+        hid_mine[...] = row_half(hid_s, core[0]).astype(BF16)
+        hid_other[...] = row_half(hid_s, 1 - core[0]).astype(BF16)
     else:
         y_ref[...] = y
         x1_ref[...] = x1
         normed = normed_of(x1, g_ref[...])
         n_ref[...] = normed
+        sends[rows:, :] = normed
         xc = dot(normed, iw_ref[...]).astype(BF16)
         xc_ref[...] = xc
         tail_ref[...] = xc.astype(F32)[xc.shape[0] - HALO :, :]
@@ -618,6 +633,11 @@
     small_ref[at + 3 : at + 4, :] = jnp.zeros((1, inner), F32)
 
 
+def row_half(ref, which):
+    half = ref.shape[0] // 2
+    return ref[pl.ds(pl.multiple_of(which * half, 16), half), :]
+
+
 def lane_half(ref, which):
     half = ref.shape[1] // 2
     return ref[:, pl.ds(pl.multiple_of(which * half, 128), half)]
@@ -643,13 +663,16 @@
     return e + rinv * (dhat - xhat * jnp.mean(dhat * xhat, axis=-1, keepdims=True)), g_norm
 
 
-def small_out(core, small_ref, g_norm, keep_ref, send_ref):
+def small_out(core, small_ref, g_norm, keep_ref, sends, at):
     rows, inner = small_ref.shape
     width = g_norm.shape[1]
     small_ref[rows - 1 : rows, 0:width] = g_norm
-    for which, ref in ((core[0], keep_ref), (1 - core[0], send_ref)):
-        ref[0:rows, :] = lane_half(small_ref, which)
-        ref[rows:, :] = jnp.zeros((ref.shape[0] - rows, ref.shape[1]), F32)
+    pad = keep_ref.shape[0] - rows
+    for which, ref, first in ((core[0], keep_ref, 0), (1 - core[0], sends, at)):
+        block = lane_half(small_ref, which)
+        block = jnp.concatenate([block, jnp.zeros((pad, block.shape[1]), F32)], axis=0)
+        ref[first : first + rows + pad, :] = block.astype(ref.dtype)
+    sends[at + rows + pad :, :] = jnp.zeros((sends.shape[0] - at - rows - pad, inner // 2), BF16)
 
 
 def k_turn(
@@ -671,15 +694,13 @@
     xd_ref,
     a2,
     dxc_keep,
-    dxc_send,
     small_keep,
-    small_send,
     e1_ref,
     de_ref,
     dy_ref,
     dz_ref,
     dz_keep,
-    dz_send,
+    sends,
     pay_ref,
     small_s,
     dxc_s,
@@ -692,23 +713,25 @@
     wide_s,
 ):
     dxc = conv_back(dce_s, dconv_ref, next_ref, cw_ref)
+    rows = dxc.shape[0]
     dxc_s[...] = dxc
     dxc_keep[...] = lane_half(dxc_s, core[0])
-    dxc_send[...] = lane_half(dxc_s, 1 - core[0])
+    sends[0:rows, :] = lane_half(dxc_s, 1 - core[0])
     dn = dnz_ref[...] + dot_t(dxc, iw_ref[...])
     e1, g_norm = norm_back(x_ref[...], g_ref[...], e_ref[...].astype(F32), dn)
     small_s[...] = small_ref[...]
-    small_out(core, small_s, g_norm, small_keep, small_send)
+    small_out(core, small_s, g_norm, small_keep, sends, 3 * rows)
     e1_ref[...] = e1
     de = e1.astype(BF16)
     de_ref[...] = de
+    sends[2 * rows : 3 * rows, :] = de
     dgated = dot_t(de, ow_ref[...])
     zf = z_ref[...].astype(F32)
     s = sigmoid(zf)
     dy_ref[...] = dgated * (zf * s)
     dz_ref[...] = (dgated * y_ref[...] * (s * (1.0 + zf * (1.0 - s)))).astype(BF16)
     dz_keep[...] = lane_half(dz_ref, core[0])
-    dz_send[...] = lane_half(dz_ref, 1 - core[0])
+    sends[rows : 2 * rows, :] = lane_half(dz_ref, 1 - core[0])
     states = a2.shape[0]
     dt = softplus(v_ref[...])
     dt_s[...] = dt
@@ -731,23 +754,27 @@
     g_ref,
     e_ref,
     dxc_keep,
-    dxc_send,
     small_keep,
-    small_send,
-    e0_ref,
+    sends,
+    e0_mine,
+    e0_other,
     small_s,
     dxc_s,
     dce_s,
+    e0_s,
 ):
     dxc = conv_back(dce_s, dconv_ref, next_ref, cw_ref)
+    rows = dxc.shape[0]
     dxc_s[...] = dxc
     dxc_keep[...] = lane_half(dxc_s, core[0])
-    dxc_send[...] = lane_half(dxc_s, 1 - core[0])
+    sends[0:rows, :] = lane_half(dxc_s, 1 - core[0])
     dn = dnz_ref[...] + dot_t(dxc, iw_ref[...])
     e0, g_norm = norm_back(x_ref[...], g_ref[...], e_ref[...], dn)
     small_s[...] = small_ref[...]
-    small_out(core, small_s, g_norm, small_keep, small_send)
-    e0_ref[...] = e0.astype(BF16)
+    small_out(core, small_s, g_norm, small_keep, sends, rows)
+    e0_s[...] = e0
+    e0_mine[...] = row_half(e0_s, core[0]).astype(BF16)
+    e0_other[...] = row_half(e0_s, 1 - core[0]).astype(BF16)
 
 
 def k_dnz(dz_ref, iw_ref, out_ref):
@@ -772,9 +799,9 @@
         n = small_a.shape[0] // blocks
         top = n_pairs * rows
         s_ref[:, top:, :] = jnp.zeros((blocks, s_ref.shape[1] - top, s_ref.shape[2]), F32)
+        small = small_a[...] + small_b[...].astype(F32)[0 : small_a.shape[0]]
         for k in range(blocks):
-            here = slice(k * n, (k + 1) * n)
-            s_ref[k, top : top + n, :] = small_a[here, :] + small_b[here, :]
+            s_ref[k, top : top + n, :] = small[k * n : (k + 1) * n]
 
 
 def k_first(n_pairs, has_small, place, *refs):
@@ -838,14 +865,20 @@
             out[at, :, half:] = right[d][m]
 
 
-def k_place(split_rows, core, mine, came, *refs):
+def in_order(core, sources):
+    if len(sources) == 1:
+        return sources[0][:, 0].astype(F32), sources[0][:, 1].astype(F32)
+    own = core[0] == 0
+    a, b = sources[0][...].astype(F32), sources[1][...].astype(F32)
+    return jnp.where(own, a, b), jnp.where(own, b, a)
+
+
+def k_place(n_sources, split_rows, core, *refs):
     out, done = refs[-2:]
     done[...] = jnp.zeros(done.shape, F32)
-    blocks, rows, lanes = mine.shape
-    own = core[0] == 0
-    a = mine[...].astype(F32).reshape(blocks * rows, lanes)
-    b = came[...].astype(F32).reshape(blocks * rows, lanes)
-    low, high = jnp.where(own, a, b), jnp.where(own, b, a)
+    low, high = in_order(core, refs[:n_sources])
+    blocks, rows, lanes = low.shape
+    low, high = low.reshape(blocks * rows, lanes), high.reshape(blocks * rows, lanes)
     if split_rows:
         out[0], out[1] = low, high
     else:
@@ -853,15 +886,32 @@
         out[:, lanes:] = high
 
 
-def k_place_small(row0, core, mine, came, out):
-    blocks, _, lanes = mine.shape
-    n = out.shape[0] // blocks
-    first = jnp.where(core[0] == 0, 0, 1)
-    for src, half in ((mine, first), (came, 1 - first)):
+def k_place_small(rank, taps, counts, core, *refs):
+    refs = list(refs)
+    given, refs = refs[: sum(counts)], refs[sum(counts) :]
+    norm, cw, cb, xw, dw, db, al, sk, all_s = refs
+    states = al.shape[1]
+    n_x = rank + 2 * states
+    all_s[...] = jnp.zeros(all_s.shape, F32)
+    at = 0
+    for l, count in enumerate(counts):
+        low, high = in_order(core, given[at : at + count])
+        at += count
+        blocks, _, lanes = low.shape
+        n = -(-(n_x + rank + states + taps + 4) // blocks)
         for k in range(blocks):
-            out[k * n : (k + 1) * n, pl.ds(pl.multiple_of(half * lanes, 128), lanes)] = src[
-                k, row0 : row0 + 16, :
-            ].astype(F32)[0:n]
+            all_s[k * n : (k + 1) * n, 0:lanes] = low[k, 0:n]
+            all_s[k * n : (k + 1) * n, lanes:] = high[k, 0:n]
+        dw[l] = all_s[n_x : n_x + rank, :]
+        first = n_x + rank
+        xw[l] = all_s[0:n_x, :]
+        al[l] = all_s[first : first + states, :]
+        cw[l] = all_s[first + states : first + states + taps, :]
+        first += states + taps
+        cb[l : l + 1, :] = all_s[first : first + 1, :]
+        db[l : l + 1, :] = all_s[first + 1 : first + 2, :]
+        sk[l : l + 1, :] = all_s[first + 2 : first + 3, :]
+        norm[l : l + 1, :] = all_s[first + 3 : first + 4, 0 : norm.shape[1]]
 
 
 def shards(
@@ -903,14 +953,18 @@
         second = jnp.where(core == 0, came, mine)
         return jnp.concatenate([first, second], axis=0)
 
-    def from_runs(run_block):
-        halves = run_block.reshape((2, own) + run_block.shape[1:])
-        mine = lax.dynamic_index_in_dim(halves, core, 0, keepdims=False)
-        other = lax.dynamic_index_in_dim(halves, 1 - core, 0, keepdims=False)
+    def from_runs(mine, other):
         came = lax.ppermute(other, AXIS, pairs)
         first = jnp.where(core == 0, mine, came)
         second = jnp.where(core == 0, came, mine)
         return jnp.stack([first, second], axis=0)
+
+    def done_by_now(array):
+        array, turn[0] = lax.optimization_barrier((array, turn[0]))
+        return array
+
+    def not_before(*arrays):
+        return lax.optimization_barrier(arrays + (turn[0],))[:-1]
 
     def from_before(block):
         return lax.ppermute(block, AXIS, [(i, i + 2) for i in range(ndev - 2)])
@@ -952,6 +1006,8 @@
         return lax.ppermute(block, AXIS, pairs)
 
     pay = shape((states, inner + EXTRA), BF16)
+
+    kept = {}
 
     def exchange(payload, a2, mode, meanwhile=()):
         meanwhile = dict(enumerate(meanwhile))
@@ -992,18 +1048,17 @@
         else:
             way = "up" if mode == "f" else "down"
             last = [send(payload, r, m, way) for m in range(1, rounds[r][1])]
+        kept["last"] = last
         for step in sorted(meanwhile):
             if step >= r:
                 meanwhile[step]()
         return last, sum(befores, []), sum(sums, []), digits_of(r)
 
-    a2_all = -jnp.exp(jnp.swapaxes(a_log, 1, 2)) * LOG2E
-    cw_all = jnp.swapaxes(conv_weight, 1, 2)
-    xw_all = jnp.pad(xproj_weight, ((0, 0), (0, 0), (0, XD - xproj_weight.shape[2])))
-    dw_all = jnp.pad(dtproj_weight, ((0, 0), (0, XD - rank), (0, 0)))
-
     def row(array, l):
-        return array[l : l + 1, :]
+        return Row(array, l)
+
+    def layer_of(array, l):
+        return array, part((None,) + array.shape[1:], (l, 0, 0))
 
     def w_in(l, half):
         return in_weight, part((None, width, inner), (l, 0, half))
@@ -1025,7 +1080,6 @@
     edge = shape((HALO, inner), F32)
     mm = 2 * rows * width * inner
 
-    grad_out = to_runs(hidden_grad)
     x0 = to_runs(hidden_in).astype(F32)
 
     normed = [None, None]
@@ -1040,11 +1094,18 @@
         k_in, [res_b, act_b, edge], [x0, row(norm_gain, 0), w_in(0, 0)]
     )
 
+    a_log, conv_weight, xproj_weight, dtproj_weight, hidden_grad = not_before(
+        a_log, conv_weight, xproj_weight, dtproj_weight, hidden_grad
+    )
+    a2_all = -jnp.exp(jnp.swapaxes(a_log, 1, 2)) * LOG2E
+    cw_all = jnp.swapaxes(conv_weight, 1, 2)
+    xw_all = jnp.pad(xproj_weight, ((0, 0), (0, 0), (0, XD - xproj_weight.shape[2])))
+    dw_all = jnp.pad(dtproj_weight, ((0, 0), (0, XD - rank), (0, 0)))
+    grad_out = to_runs(hidden_grad)
+
     def before_scan(l, tail, dgated=None):
         halo[l] = from_before(tail)
-        (z[l],) = call(k_gate, [act_b], [normed[l], w_in(l, 1)])
-        if l == 0:
-            (dgated1,) = call(k_dgated, [act], [grad_out, w_out(1)])
+        (z[l],) = call(k_gate, [act_b], [normed[l], w_in(l, 1)], cost=LONG)
         both = dgated is not None
         outs = call(
             functools.partial(k_local, rank, both),
@@ -1058,12 +1119,12 @@
             [
                 halo[l],
                 xc[l],
-                cw_all[l],
+                layer_of(cw_all, l),
                 row(conv_bias, l),
-                xw_all[l],
-                dw_all[l],
+                layer_of(xw_all, l),
+                layer_of(dw_all, l),
                 row(dt_bias, l),
-                a2_all[l],
+                layer_of(a2_all, l),
             ]
             + ([dgated, z[l]] if both else []),
             [pltpu.VMEM((rows + HALO, inner), F32)]
@@ -1073,7 +1134,7 @@
             cost=LONG,
         )
         u[l], xd[l], v[l] = outs[:3]
-        return (outs[3], dgated1) if l == 0 else outs[3:]
+        return outs[3:]
 
     def join_scratch():
         group = rounds[-1][1]
@@ -1081,6 +1142,9 @@
             pltpu.VMEM((group, states, inner), F32),
             pltpu.VMEM((group, 8, inner), F32),
         ]
+
+    def piece(array, i):
+        return array, part((rows, array.shape[1]), (i, 0))
 
     def mix(l, parts, extra, outs):
         final = l == layers - 1
@@ -1093,9 +1157,9 @@
             + last
             + befores
             + sums
-            + [a2_all[l], u[l], v[l], xd[l], z[l], residual[l], row(skip_gain, l), w_out(l)]
+            + [layer_of(a2_all, l), u[l], v[l], xd[l], z[l], residual[l], row(skip_gain, l), w_out(l)]
             + extra,
-            ([act_scratch] if final else [])
+            ([act_scratch, pltpu.VMEM((rows, width), F32)] if final else [])
             + [pltpu.VMEM((rows, inner), BF16)]
             + [act_scratch] * 2
             + table_scratch()
@@ -1107,38 +1171,50 @@
     entry = shape((states, inner), F32)
     act_scratch = pltpu.VMEM((rows, inner), F32)
     residual = [x0, None]
-    payload, dgated1 = before_scan(0, tail)
-    parts = exchange(payload, a2_all[0], "f")
-    y0, x1, normed[1], xc[1], tail, gated_keep, gated_send, h0 = mix(
+    def shadow_0():
+        (kept["dgated1"],) = call(k_dgated, [act], [grad_out, w_out(1)], cost=LONG)
+
+    (payload,) = before_scan(0, tail)
+    parts = exchange(payload, layer_of(a2_all, 0), "f", (shadow_0,))
+    dgated1 = kept["dgated1"]
+    y0, x1, normed[1], xc[1], tail, gated_keep, sends, h0 = mix(
         0,
         parts,
         [row(norm_gain, 1), w_in(1, 0)],
-        [act, res, res_b, act_b, edge, half_b, half_b, entry],
+        [act, res, res_b, act_b, edge, half_b, shape((2 * rows, width), BF16), entry],
     )
     residual[1] = x1
-    gated0_pair = (gated_keep, swap(gated_send))
+    came = swap(sends)
+    n1_pair = (normed[1], piece(came, 1))
+    gated0_pair = (gated_keep, piece(came, 0))
+    n0_pair = (normed[0], swap(normed[0]))
+    e1_pair = (grad_out, swap(grad_out))
     payload, dy1 = before_scan(1, tail, dgated1)
-    parts = exchange(payload, a2_all[1], "fb")
+    parts = exchange(payload, layer_of(a2_all, 1), "fb")
     n_small = rank + 2 * states + rank + states + taps + 4
     small = shape((n_small, inner), F32)
     small_pad = -(-n_small // (BLOCKS * 2)) * BLOCKS * 2 if n_small % BLOCKS else n_small
 
-    n_parts = 2
-    lanes = inner // n_parts
+    n_chunks = inner // CHUNK
+    cuts = [(0, (n_chunks + 1) // 2 * CHUNK), ((n_chunks + 1) // 2 * CHUNK, n_chunks // 2 * CHUNK)]
+    n_parts = len(cuts)
+    assert all(first % lanes == 0 for first, lanes in cuts)
 
     def scan(l, i, dy, parts, h_in):
+        lane0, lanes = cuts[i]
         last, befores, sums, digits = parts
         n_low = len(rounds) - 1
-        cut = part((rows, lanes), (0, i))
-        cut_s = part((states, lanes), (0, i))
+        cut = part((rows, lanes), (0, lane0 // lanes))
+        cut_s = part((states, lanes), (0, lane0 // lanes))
+        cut_a = part((None, states, lanes), (l, 0, lane0 // lanes))
         return call(
-            functools.partial(k_scan, rank, i * lanes, len(last), n_low),
+            functools.partial(k_scan, rank, lane0, len(last), n_low),
             [shape((rows, lanes), F32)] * 2 + [shape((states, lanes), F32), shape((rows, XD), F32)],
             [(digits, smem)]
             + last
             + befores[-n_low:]
             + sums[-n_low:]
-            + [(a2_all[l], cut_s), (u[l], cut), (v[l], cut), (dy, cut), (h_in, cut_s), xd[l]],
+            + [(a2_all, cut_a), (u[l], cut), (v[l], cut), (dy, cut), (h_in, cut_s), xd[l]],
             [pltpu.VMEM((rows, lanes), F32)] * 2
             + table_scratch()
             + [
@@ -1163,10 +1239,10 @@
                 dy,
                 halo[l],
                 xc[l],
-                cw_all[l],
+                layer_of(cw_all, l),
                 row(conv_bias, l),
-                xw_all[l],
-                dw_all[l],
+                layer_of(xw_all, l),
+                layer_of(dw_all, l),
                 row(skip_gain, l),
             ],
             [pltpu.VMEM((rows + HALO, inner), F32)],
@@ -1179,7 +1255,12 @@
 
     place_s = (chip[None].astype(jnp.int32), smem)
 
-    def summed(matrices, smalls):
+    def held(arrays, gate):
+        if gate is None:
+            return arrays
+        return lax.optimization_barrier(tuple(arrays) + tuple(gate()))[: len(arrays)]
+
+    def summed(matrices, smalls, aside=False, gates=(None, None, None)):
         ins = []
         each = width // BLOCKS
         for (a, a_came), (b, b_came) in matrices:
@@ -1199,8 +1280,11 @@
             empty = jnp.zeros((2,) + mine.shape, F32)
             total = lax.psum(lax.dynamic_update_index_in_dim(empty, mine, core, 0), AXIS)
             total = total.astype(BF16)
-            for _ in range(5):
+            for _ in range(3 if aside else 5):
                 yield None
+            if aside:
+                yield jnp.swapaxes(total, 0, 1)
+                return
             yield (
                 lax.dynamic_index_in_dim(total, core, 0, keepdims=False),
                 lax.dynamic_index_in_dim(total, 1 - core, 0, keepdims=False),
@@ -1212,7 +1296,9 @@
             [shape((n, r, half), F32)] * 2 + [shape((n, r, half), BF16)] * 2,
             [place_s] + ins,
             [pltpu.VMEM((BLOCKS, r, width), F32)],
-        )
+            cost=LONG,
+        )
+        send_a, send_b = held([send_a, send_b], gates[0])
         came_a, came_b = over(send_a, 1), over(send_b, 2)
         yield None
         n = BLOCKS // 4
@@ -1221,6 +1307,7 @@
             [shape((n, r, half), F32)] * 2 + [shape((n, r, half), BF16)] * 2,
             [place_s, keep_a, keep_b, came_a, came_b],
         )
+        send_a, send_b = held([send_a, send_b], gates[1])
         came_a, came_b = over(send_a, 2), over(send_b, 1)
         yield None
         keep, *sends = call(
@@ -1228,9 +1315,14 @@
             [shape((r, width), F32)] + [shape((r, width), BF16)] * 3,
             [place_s, stay_a, stay_b, came_a, came_b],
         )
+        sends = held(sends, gates[2])
         came = [over(send_m, 4 * (m + 1)) for m, send_m in enumerate(sends)]
         yield None
         (done,) = call(k_fourth, [shape((r, width), BF16)], [keep] + came)
+        if aside:
+            every = lax.all_gather(done, AXIS)
+            yield every.reshape(BLOCKS, 2, r, width)
+            return
         came = [over(done, 4 * m) for m in (1, 2, 3)]
         yield None
         left, right = call(k_stack, [shape((4, r, half), BF16)] * 2, [done] + came)
@@ -1243,21 +1335,27 @@
         )
         yield mine, swap(mine)
 
+    def sources(halves, i, per, each, place):
+        if not isinstance(halves, tuple):
+            spec = pl.BlockSpec((per, 2, each, width), lambda g: (place(g), 0, i, 0))
+            return [halves], [spec]
+        spec = pl.BlockSpec((per, each, width), lambda g: (place(g), i, 0))
+        return list(halves), [spec, spec]
+
     def placed(halves, i, whole, block, index, split_rows, before):
         each = width // BLOCKS
         steps = 4
-        per = BLOCKS // steps
-        source = pl.BlockSpec((per, each, width), lambda g: (g, i, 0))
         anywhere = pl.BlockSpec(memory_space=pl.ANY)
-        ins = [core_s[0], halves[0], halves[1], turn[0]]
-        specs = [smem, source, source, anywhere]
+        arrays, specs = sources(halves, i, BLOCKS // steps, each, lambda g: g)
+        ins = [core_s[0]] + arrays + [turn[0]]
+        specs = [smem] + specs + [anywhere]
         aliases = {}
         if before is not None:
+            aliases = {len(ins): 0}
             ins.append(before)
             specs.append(anywhere)
-            aliases = {4: 0}
         out, turn[0] = pl.pallas_call(
-            functools.partial(k_place, split_rows),
+            functools.partial(k_place, len(arrays), split_rows),
             grid=(steps,),
             in_specs=specs,
             out_specs=[pl.BlockSpec(block, index), pl.BlockSpec((8, 128), lambda g: (0, 0))],
@@ -1280,55 +1378,66 @@
     def in_at(l, half):
         return lambda g: (l, g, half)
 
-    def placed_small(halves, i):
+    def placed_small(layer_sums):
         each = width // BLOCKS
-        (out,) = call(
-            functools.partial(k_place_small, i * each),
-            [shape((small_pad, inner), F32)],
-            [core_s, halves[0], halves[1]],
-        )
-        return out
+        ins, counts = [core_s], []
+        for halves, i in layer_sums:
+            arrays, specs = sources(halves, i * each // 16, BLOCKS, 16, lambda g: 0)
+            ins += list(zip(arrays, specs))
+            counts.append(len(arrays))
+        n_x = rank + 2 * states
+        return call(
+            functools.partial(k_place_small, rank, taps, tuple(counts)),
+            [
+                shape((layers, width), F32),
+                shape((layers, taps, inner), F32),
+                shape((layers, inner), F32),
+                shape((layers, n_x, inner), F32),
+                shape((layers, rank, inner), F32),
+                shape((layers, inner), F32),
+                shape((layers, states, inner), F32),
+                shape((layers, inner), F32),
+            ],
+            ins,
+            [pltpu.VMEM((small_pad, inner), F32)],
+        )
 
     half_small = shape((small_pad, width), F32)
-    n1_pair = (normed[1], swap(normed[1]))
-    n0_pair = (normed[0], swap(normed[0]))
-    e1_pair = (grad_out, swap(grad_out))
-
-    hidden_out, dz1, dz_keep, dz_send, gated_keep, gated_send, h1 = mix(
-        1, parts, [dgated1], [res_b, act_b] + [half_b] * 4 + [entry]
+
+    hid_mine, hid_other, dz1, dz_keep, gated_keep, sends, h1 = mix(
+        1,
+        parts,
+        [dgated1],
+        [shape((own, width), BF16)] * 2
+        + [act_b, half_b, half_b, shape((2 * rows, width), BF16), entry],
     )
+    came = swap(sends)
+    hidden_out = from_runs(hid_mine, hid_other)
     a_sum = summed(
-        [((gated_keep, swap(gated_send)), e1_pair), (n1_pair, (dz_keep, swap(dz_send)))], None
+        [((gated_keep, piece(came, 0)), e1_pair), (n1_pair, (dz_keep, piece(came, 1)))],
+        None,
+        True,
+        (None, None, lambda: [after1]),
     )
     scans = [scan(1, 0, dy1, parts, h1)]
     next(a_sum)
     scans.append(scan(1, 1, dy1, parts, h1))
+    hidden_out = done_by_now(hidden_out)
     next(a_sum)
     dconv1, head1, small1 = post(1, scans, dy1)
     after1 = from_after(head1)
-    (dnz1,) = call(k_dnz, [res], [dz1, w_in(1, 1)])
+    (dnz1,) = call(k_dnz, [res], [dz1, w_in(1, 1)], cost=LONG)
     next(a_sum)
-    (
-        dxc_keep,
-        dxc_send,
-        small_keep,
-        small_send,
-        e1,
-        de0,
-        dy0,
-        dz0,
-        dz_keep,
-        dz_send,
-        payload,
-    ) = call(
+    turn_back = functools.partial(
+        call,
         functools.partial(k_turn, rank),
-        [half_b, half_b, half_small, half_small, res, res_b, act, act_b, half_b, half_b, pay],
+        [half_b, half_small, res, res_b, act, act_b, half_b, shape((4 * rows, width), BF16), pay],
         [
             core_s,
             small1,
             dconv1,
             after1,
-            cw_all[1],
+            layer_of(cw_all, 1),
             dnz1,
             w_in(1, 0),
             x1,
@@ -1339,7 +1448,7 @@
             z[0],
             v[0],
             xd[0],
-            a2_all[0],
+            layer_of(a2_all, 0),
         ],
         [
             pltpu.VMEM((n_small, inner), F32),
@@ -1351,84 +1460,89 @@
         + [pltpu.VMEM((states, inner), F32), pltpu.VMEM((states, inner + EXTRA), F32)],
         cost=LONG,
     )
+    dxc_keep, small_keep, e1, de0, dy0, dz0, dz_keep, sends, payload = turn_back()
+    came = swap(sends)
     b_sum = summed(
         [
-            (n1_pair, (dxc_keep, swap(dxc_send))),
-            (gated0_pair, (de0, swap(de0))),
-            (n0_pair, (dz_keep, swap(dz_send))),
+            (n1_pair, (dxc_keep, piece(came, 0))),
+            (gated0_pair, (de0, piece(came, 2))),
+            (n0_pair, (dz_keep, piece(came, 1))),
         ],
-        (small_keep, swap(small_send)),
+        (small_keep, piece(came, 3)),
+        True,
+        (lambda: kept["last"], None, None),
     )
-    kept = {}
-
-    def first_shadow():
-        (kept["dnz0"],) = call(k_dnz, [res], [dz0, w_in(0, 1)])
-
-    def second_shadow():
+
+    def shadow_1():
+        kept["sum_a"] = next(a_sum)
+        (kept["dnz0"],) = call(k_dnz, [res], [dz0, w_in(0, 1)], cost=LONG)
+
+    def shadow_2():
         next(b_sum)
 
-    parts = exchange(payload, a2_all[0], "b", (first_shadow, second_shadow))
+    parts = exchange(payload, layer_of(a2_all, 0), "b", (shadow_1, shadow_2))
     dnz0 = kept["dnz0"]
-    next(a_sum)
+    sum_a = kept["sum_a"]
     scans = [scan(0, 0, dy0, parts, h0)]
-    next(a_sum)
     next(b_sum)
     scans.append(scan(0, 1, dy0, parts, h0))
     next(b_sum)
     dconv0, head0, small0 = post(0, scans, dy0)
     after0 = from_after(head0)
-    sum_a1 = next(a_sum)
-    dxc_keep, dxc_send, small_keep, small_send, e0 = call(
+    dxc_keep, small_keep, sends, e0_mine, e0_other = call(
         k_end,
-        [half_b, half_b, half_small, half_small, res_b],
-        [core_s, small0, dconv0, after0, cw_all[0], dnz0, w_in(0, 0), x0, row(norm_gain, 0), e1],
+        [half_b, half_small, shape((2 * rows, width), BF16)] + [shape((own, width), BF16)] * 2,
+        [
+            core_s,
+            small0,
+            dconv0,
+            after0,
+            layer_of(cw_all, 0),
+            dnz0,
+            w_in(0, 0),
+            x0,
+            row(norm_gain, 0),
+            e1,
+        ],
         [
             pltpu.VMEM((n_small, inner), F32),
             pltpu.VMEM((rows, inner), BF16),
             pltpu.VMEM((rows + HALO, inner), F32),
+            pltpu.VMEM((rows, width), F32),
         ],
         cost=LONG,
     )
-    c_sum = summed([(n0_pair, (dxc_keep, swap(dxc_send)))], (small_keep, swap(small_send)))
+    came = swap(sends)
+    c_sum = summed(
+        [(n0_pair, (dxc_keep, piece(came, 0)))], (small_keep, piece(came, 1))
+    )
+    sum_b = next(b_sum)
     next(c_sum)
-    g_out = placed(sum_a1, 0, g_out_shape, out_block, out_at(1), True, None)
-    next(b_sum)
-    next(c_sum)
-    g_in = placed(sum_a1, 1, g_in_shape, in_block, in_at(1, 1), False, None)
-    next(c_sum)
-    next(b_sum)
+    g_out = placed(sum_a, 0, g_out_shape, out_block, out_at(1), True, None)
+    input_grad = done_by_now(from_runs(e0_mine, e0_other))
     next(c_sum)
     next(c_sum)
-    sum_b = next(b_sum)
-    small1 = placed_small(sum_b, 3)
+    g_in = placed(sum_a, 1, g_in_shape, in_block, in_at(1, 1), False, None)
+    next(c_sum)
+    next(c_sum)
+    sum_c = next(c_sum)
     g_in = placed(sum_b, 0, g_in_shape, in_block, in_at(1, 0), False, g_in)
     g_out = placed(sum_b, 1, g_out_shape, out_block, out_at(0), True, g_out)
-    sum_c = next(c_sum)
     g_in = placed(sum_b, 2, g_in_shape, in_block, in_at(0, 1), False, g_in)
     g_in = placed(sum_c, 0, g_in_shape, in_block, in_at(0, 0), False, g_in)
-    small0 = placed_small(sum_c, 1)
-
-    smalls = jnp.stack([small0, small1])
-    n_x = rank + 2 * states
-    g_xw = jnp.swapaxes(smalls[:, 0:n_x], 1, 2)
-    g_dw = smalls[:, n_x : n_x + rank]
-    at = n_x + rank
-    g_al = jnp.swapaxes(smalls[:, at : at + states], 1, 2)
-    at += states
-    g_cw = jnp.swapaxes(smalls[:, at : at + taps], 1, 2)
-    at += taps
+    g_norm, g_cw, g_cb, g_xw, g_dw, g_db, g_al, g_sk = placed_small([(sum_c, 1), (sum_b, 3)])
     return (
-        from_runs(hidden_out),
-        from_runs(e0),
-        smalls[:, n_small - 1, 0:width],
+        hidden_out,
+        input_grad,
+        g_norm,
         g_in,
-        g_cw,
-        smalls[:, at],
-        g_xw,
+        jnp.swapaxes(g_cw, 1, 2),
+        g_cb,
+        jnp.swapaxes(g_xw, 1, 2),
         g_dw,
-        smalls[:, at + 1],
-        g_al,
-        smalls[:, at + 2],
+        g_db,
+        jnp.swapaxes(g_al, 1, 2),
+        g_sk,
         g_out.reshape(layers, inner, width),
     )
 

time: 581 us -> 495 us (0.85)
  waiting for transfers between devices: 96.3 us -> 63.9 us
  Pallas kernels: 320 us -> 289 us
  starting transfers between devices: 107 us -> 86.9 us
  between operations: 2.03 us -> 15.2 us
  local copies, waits for them, and re-layouts: 35.8 us -> 23.9 us
    pallas_call x41 -> x36, Pallas kernels: 293 us -> 262 us  [run(): pl.pallas_call(body, grid=(1,), in_specs=specs, out_specs=out_specs, out_...]
    ppermute x48 -> x30, waiting for transfers between devices: 70.7 us -> 45.3 us  [over(): return lax.ppermute(block, AXIS, [(i, i ^ flip << 1) for i in range(ndev)])]
    ppermute x48 -> x30, starting transfers between devices: 62.6 us -> 45 us  [over(): return lax.ppermute(block, AXIS, [(i, i ^ flip << 1) for i in range(ndev)])]
    unnamed x229 -> x142, local copies, waits for them, and re-layouts: 27.2 us -> 20.6 us
    ppermute x18, waiting for transfers between devices: 16.3 us -> 10.3 us  [send(): return lax.ppermute(block, AXIS, route)]
  transfers between devices with their start and end apart: 89 -> 65, of which waited for: 30 -> 22; matrix products, arithmetic and copies ran while one was open for 2% -> 1% of each run, Pallas kernels for 38% -> 46%
where the time goes in v2:
time: 495 us; the launch traced here: 485 us
  Pallas kernels  289 us (58%)
  starting transfers between devices  86.9 us (18%)
  waiting for transfers between devices  63.9 us (13%)
  local copies, waits for them, and re-layouts  23.9 us (5%)
  between operations  15.2 us (3%)
  other arithmetic  6.31 us (1%)
    pallas_call x36, Pallas kernels, run(): pl.pallas_call(body, grid=(1,), in_specs=specs, out_specs=out_specs, out_...  262 us
    ppermute x30, waiting for transfers between devices, over(): return lax.ppermute(block, AXIS, [(i, i ^ flip << 1) for i in range(ndev)])  45.3 us
    ppermute x30, starting transfers between devices, over(): return lax.ppermute(block, AXIS, [(i, i ^ flip << 1) for i in range(ndev)])  45 us
    ppermute x18, starting transfers between devices, send(): return lax.ppermute(block, AXIS, route)  28.3 us
    pallas_call x6, Pallas kernels, placed(): pl.pallas_call(functools.partial(k_place, len(arrays), split_rows), grid=...  26.3 us
    unnamed x142, local copies, waits for them, and re-layouts  20.6 us
    ppermute x18, waiting for transfers between devices, send(): return lax.ppermute(block, AXIS, route)  10.3 us
  transfers between devices with their start and end apart: 65, of which 22 were waited for; matrix products, arithmetic and copies ran while one was open for 1% of the time, Pallas kernels for 46%

profile of v2, /device:TPU:0, one launch (start us, length us, event | category | flops | bytes accessed | tf_op | source)
XLA Modules:
  0.0 484.8 jit_solution(18297458634400545535)
XLA Ops:
  15.4 4.8 collective-permute-start.1
  27.6 11.9 %shard_map.213 = (bf16[256,1536]{1,0:T(8,128)(2,1)}, bf16[256,128]{1,0:T(8,128)(2,1)}, f32[256,1536]{1,0:T(8,128)}, bf16[16,1792]{1,0:T(8,128)(2,1)}) custom-call(f32[8,1536]{1,0:T(8,128)} %copy-done.32, bf16[256,1536]{1,0:T(8,128)(2,1)} %get-tuple-element.161.refs_1_.refs_13_, f32[2,4,1536]{2,1,0:T(4,128)} %bitcast.38, f32[2,1536]{1,0:T(2,128)} %refs_15_.5, ...), custom_call_target="tpu_custom_call" | custom-call | flops 1 | bytes 100000000 | tf_op jit(solution)/shard_map/pallas_call | solution.py:66
  50.7 5.5 %collective-permute-start.8 = (bf16[16,1792]{1,0:T(8,128)(2,1)}, bf16[16,1792]{1,0:T(8,128)(2,1)S(1)}, u32[]{:S(2)}, u32[]{:S(2)}) collective-permute-start(bf16[16,1792]{1,0:T(8,128)(2,1)} %get-tuple-element.169), channel_id=1, source_target_pairs={{0,24},{1,25},{2,26},{3,27},{4,28},{5,29},{6,30},{7,31},{8,16},{9,... | collective-permute-start | bytes 172040 | tf_op jit(solution)/shard_map/ppermute | solution.py:1000
  62.7 18.9 %shard_map.216 = (f32[256,1536]{1,0:T(8,128)}, f32[256,768]{1,0:T(8,128)}, bf16[256,768]{1,0:T(8,128)(2,1)}, bf16[256,1536]{1,0:T(8,128)(2,1)}, f32[8,1536]{1,0:...) custom-call(s32[2]{0:T(128)} %pad_add_fusion.refs_0_, ...), custom_call_target="tpu_custom_call" | custom-call | flops 1 | bytes 100000000 | tf_op jit(solution)/shard_map/pallas_call | solution.py:66
  89.3 18.9 %shard_map.218 = (bf16[256,1536]{1,0:T(8,128)(2,1)}, bf16[256,128]{1,0:T(8,128)(2,1)}, f32[256,1536]{1,0:T(8,128)}, bf16[32,1792]{1,0:T(8,128)(2,1)}, f32[256,1536]{1,0:T(8,128)}) custom-call(f32[8,1536]{1,0:T(8,128)} %copy-done.31, bf16[256,1536]{1,0:T(8,128)(2,1)} %get-tuple-element.176.refs_1_.refs_13_, f32[2,4,1536]{2,1,0:T(4,128)} %bitcast.39, ...), custom_call_target="tpu_custom_call" | custom-call | flops 1 | bytes 100000000 | tf_op jit(solution)/shard_map/pallas_call | solution.py:66
  128.6 18.4 %shard_map.220 = (bf16[128,768]{1,0:T(8,128)(2,1)}, bf16[128,768]{1,0:T(8,128)(2,1)}, bf16[256,1536]{1,0:T(8,128)(2,1)}, bf16[256,768]{1,0:T(8,128)(2,1)}, bf16[...) custom-call(s32[2]{0:T(128)} %pad_add_fusion.refs_0_, s32[1]{0:T(128)} %bitcast.1.refs_1_.refs_0_.core, ...), custom_call_target="tpu_custom_call" | custom-call | flops 1 | bytes 100000000 | tf_op jit(solution)/shard_map/pallas_call | solution.py:66
  147.5 22.6 %shard_map.221 = (f32[256,1024]{1,0:T(8,128)}, f32[256,1024]{1,0:T(8,128)}, f32[16,1024]{1,0:T(8,128)}, f32[256,128]{1,0:T(8,128)}) custom-call(s32[2]{0:T(128)} %pad_add_fusion.refs_0_, bf16[16,1792]{1,0:T(8,128)(2,1)} %copy-done.12, bf16[16,1792]{1,0:T(8,128)(2,1)} %copy-done.13, bf16[16,1792]{1,0:T(8,128)(2,1)} %copy-done.14, ...), custom_call_target="tpu_custom_call" | custom-call | flops 1 | bytes 100000000 | tf_op jit(solution)/shard_map/pallas_call | solution.py:66
  171.4 5.8 %shard_map.222 = (f32[8,96,384]{2,1,0:T(8,128)}, f32[8,96,384]{2,1,0:T(8,128)}, bf16[8,96,384]{2,1,0:T(8,128)(2,1)}, bf16[8,96,384]{2,1,0:T(8,128)(2,1)}) custom-call(s32[1]{0:T(128)} %bitcast.11.refs_0_, bf16[256,768]{1,0:T(8,128)(2,1)} %get-tuple-element.195.refs_1_, bf16[512,768]{1,0:T(8,128)(2,1)} %copy-done.5, ...), custom_call_target="tpu_custom_call" | custom-call | flops 1 | bytes 100000000 | tf_op jit(solution)/shard_map/pallas_call | solution.py:66
  181.5 13.7 %shard_map.223 = (f32[256,512]{1,0:T(8,128)}, f32[256,512]{1,0:T(8,128)}, f32[16,512]{1,0:T(8,128)}, f32[256,128]{1,0:T(8,128)}) custom-call(s32[2]{0:T(128)} %pad_add_fusion.refs_0_, bf16[16,1792]{1,0:T(8,128)(2,1)} %copy-done.12, bf16[16,1792]{1,0:T(8,128)(2,1)} %copy-done.13, bf16[16,1792]{1,0:T(8,128)(2,1)} %copy-done.14, ...), custom_call_target="tpu_custom_call" | custom-call | flops 1 | bytes 100000000 | tf_op jit(solution)/shard_map/pallas_call | solution.py:66
  201.6 9.5 %shard_map.225 = (f32[256,1536]{1,0:T(8,128)}, f32[8,1536]{1,0:T(8,128)}, f32[152,1536]{1,0:T(8,128)}) custom-call(f32[256,1024]{1,0:T(8,128)} %get-tuple-element.203.refs_0_, f32[256,512]{1,0:T(8,128)} %get-tuple-element.204.refs_1_, f32[256,1024]{1,0:T(8,128)} %get-tuple-element.205.refs_2_, f32[256,512]{1,0:T(8,128)} %get-tuple-element.206.refs_3_, ...), custom_call_target="tpu_custom_call" | custom-call | flops 1 | bytes 100000000 | tf_op jit(solution)/shard_map/pallas_call | solution.py:66
  225.5 18.6 %shard_map.228 = (bf16[256,768]{1,0:T(8,128)(2,1)}, f32[160,768]{1,0:T(8,128)}, f32[256,768]{1,0:T(8,128)}, bf16[256,768]{1,0:T(8,128)(2,1)}, f32[256,1536]{1,0:...) custom-call(s32[1]{0:T(128)} %bitcast.1.refs_1_.refs_0_.core, ...), custom_call_target="tpu_custom_call" | custom-call | flops 1 | bytes 100000000 | tf_op jit(solution)/shard_map/pallas_call | solution.py:66
  262.8 8.6 %shard_map.232 = (f32[8,160,384]{2,1,0:T(8,128)}, f32[8,160,384]{2,1,0:T(8,128)}, bf16[8,160,384]{2,1,0:T(8,128)(2,1)}, bf16[8,160,384]{2,1,0:T(8,128)(2,1)}) custom-call(s32[1]{0:T(128)} %bitcast.11.refs_0_, bf16[256,768]{1,0:T(8,128)(2,1)} %get-tuple-element.177.refs_0_.refs_5_.refs_1_, bf16[512,768]{1,0:T(8,128)(2,1)} %copy-done.1, ...), custom_call_target="tpu_custom_call" | custom-call | flops 1 | bytes 100000000 | tf_op jit(solution)/shard_map/pallas_call | solution.py:66
  273.6 22.9 %shard_map.233 = (f32[256,1024]{1,0:T(8,128)}, f32[256,1024]{1,0:T(8,128)}, f32[16,1024]{1,0:T(8,128)}, f32[256,128]{1,0:T(8,128)}) custom-call(s32[2]{0:T(128)} %pad_add_fusion.refs_0_, bf16[16,1792]{1,0:T(8,128)(2,1)} %copy-done.30, bf16[16,1792]{1,0:T(8,128)(2,1)} %copy-done.29, bf16[16,1792]{1,0:T(8,128)(2,1)} %copy-done.28, ...), custom_call_target="tpu_custom_call" | custom-call | flops 1 | bytes 100000000 | tf_op jit(solution)/shard_map/pallas_call | solution.py:66
  301.4 4.7 shard_map.234
  308.3 13.7 %shard_map.235 = (f32[256,512]{1,0:T(8,128)}, f32[256,512]{1,0:T(8,128)}, f32[16,512]{1,0:T(8,128)}, f32[256,128]{1,0:T(8,128)}) custom-call(s32[2]{0:T(128)} %pad_add_fusion.refs_0_, bf16[16,1792]{1,0:T(8,128)(2,1)} %copy-done.30, bf16[16,1792]{1,0:T(8,128)(2,1)} %copy-done.29, bf16[16,1792]{1,0:T(8,128)(2,1)} %copy-done.28, ...), custom_call_target="tpu_custom_call" | custom-call | flops 1 | bytes 100000000 | tf_op jit(solution)/shard_map/pallas_call | solution.py:66
  334.0 9.5 %shard_map.237 = (f32[256,1536]{1,0:T(8,128)}, f32[8,1536]{1,0:T(8,128)}, f32[152,1536]{1,0:T(8,128)}) custom-call(f32[256,1024]{1,0:T(8,128)} %get-tuple-element.242.refs_0_, f32[256,512]{1,0:T(8,128)} %get-tuple-element.250.refs_1_, f32[256,1024]{1,0:T(8,128)} %get-tuple-element.251.refs_2_, f32[256,512]{1,0:T(8,128)} %get-tuple-element.252.refs_3_, ...), custom_call_target="tpu_custom_call" | custom-call | flops 1 | bytes 100000000 | tf_op jit(solution)/shard_map/pallas_call | solution.py:66
  345.1 4.6 collective-permute-done.40.refs_3_
  350.4 6.1 %shard_map.238 = (bf16[256,768]{1,0:T(8,128)(2,1)}, f32[160,768]{1,0:T(8,128)}, bf16[512,768]{1,0:T(8,128)(2,1)}, bf16[128,768]{1,0:T(8,128)(2,1)}, bf16[128,768]{1,0:T(8,128)(2,1)}) custom-call(s32[1]{0:T(128)} %bitcast.1.refs_1_.refs_0_.core, f32[152,1536]{1,0:T(8,128)} %get-tuple-element.260.refs_1_.refs_10_, f32[256,1536]{1,0:T(8,128)} %get-tuple-element.261.refs_2_, ...), custom_call_target="tpu_custom_call" | custom-call | flops 1 | bytes 100000000 | tf_op jit(solution)/shard_map/pallas_call | solution.py:66
  376.1 5.1 %collective-permute-done.46.refs_3_ = bf16[8,64,384]{2,1,0:T(8,128)(2,1)S(1)} collective-permute-done((bf16[8,64,384]{2,1,0:T(8,128)(2,1)}, bf16[8,64,384]{2,1,0:T(8,128)(2,1)S(1)}, u32[]{:S(2)}, u32[]{:S(2)}) %collective-permute-start.46) | collective-permute-done | bytes 393248 | tf_op jit(solution)/shard_map/ppermute | solution.py:1254
  387.6 8.3 %collective-permute-done.48.refs_3_ = bf16[4,64,384]{2,1,0:T(8,128)(2,1)S(1)} collective-permute-done((bf16[4,64,384]{2,1,0:T(8,128)(2,1)}, bf16[4,64,384]{2,1,0:T(8,128)(2,1)S(1)}, u32[]{:S(2)}, u32[]{:S(2)}) %collective-permute-start.48) | collective-permute-done | bytes 196640 | tf_op jit(solution)/shard_map/ppermute | solution.py:1254
  420.2 5.0 %collective-permute-done.55.refs_3_ = bf16[64,768]{1,0:T(8,128)(2,1)S(1)} collective-permute-done((bf16[64,768]{1,0:T(8,128)(2,1)}, bf16[64,768]{1,0:T(8,128)(2,1)S(1)}, u32[]{:S(2)}, u32[]{:S(2)}) %collective-permute-start.55) | collective-permute-done | bytes 98336 | tf_op jit(solution)/shard_map/ppermute | solution.py:1254
  425.2 9.3 %collective-permute-done.54.refs_2_ = bf16[64,768]{1,0:T(8,128)(2,1)S(1)} collective-permute-done((bf16[64,768]{1,0:T(8,128)(2,1)}, bf16[64,768]{1,0:T(8,128)(2,1)S(1)}, u32[]{:S(2)}, u32[]{:S(2)}) %collective-permute-start.54) | collective-permute-done | bytes 98336 | tf_op jit(solution)/shard_map/ppermute | solution.py:1254
  455.8 4.4 shard_map.248
  470.1 4.5 shard_map.251
  (308 shorter events, 214.4 us)
Async XLA Ops:
  7.2 364.6 %all-gather.5.cloned.1.call-start = ((), (), s32[]{:S(2)}) async-start(), calls=%async_computation | async-start | bytes 4866048 | tf_op jit(solution)/shard_map/all_gather | solution.py:1323
  20.2 22.8 %collective-permute-start.5 = (bf16[128,768]{1,0:T(8,128)(2,1)S(1)}, bf16[128,768]{1,0:T(8,128)(2,1)S(1)}, u32[]{:S(2)}, u32[]{:S(2)}) collective-permute-start(bf16[128,768]{1,0:T(8,128)(2,1)S(1)} %dynamic-slice_bitcast_fusion), channel_id=1, source_target_pairs={{0,1},{1,0},{2,3},{3,2},{4,5},{5,4},{6,7},{7,6},{8,9},{9,8},{10,11... | collective-permute-start | bytes 589832 | tf_op jit(solution)/shard_map/ppermute | solution.py:951
  123.8 46.4 %collective-permute-start.19 = (bf16[512,768]{1,0:T(8,128)(2,1)S(1)}, bf16[512,768]{1,0:T(8,128)(2,1)S(1)}, u32[]{:S(2)}, u32[]{:S(2)}) collective-permute-start(bf16[512,768]{1,0:T(8,128)(2,1)S(1)} %copy-done.68), channel_id=1, source_target_pairs={{0,1},{1,0},{2,3},{3,2},{4,5},{5,4},{6,7},{7,6},{8,9},{9,8},{10,11... | collective-permute-start | bytes 2359304 | tf_op jit(solution)/shard_map/ppermute | solution.py:1006
  147.0 23.2 %collective-permute-start.17 = (bf16[512,768]{1,0:T(8,128)(2,1)}, bf16[512,768]{1,0:T(8,128)(2,1)S(1)}, u32[]{:S(2)}, u32[]{:S(2)}) collective-permute-start(bf16[512,768]{1,0:T(8,128)(2,1)} %get-tuple-element.196), channel_id=1, source_target_pairs={{0,1},{1,0},{2,3},{3,2},{4,5},{5,4},{6,7},{7,6},{8,9},{9,8},{10,11... | collective-permute-start | bytes 2359304 | tf_op jit(solution)/shard_map/ppermute | solution.py:1006
  147.0 23.1 %collective-permute-start.18 = (bf16[256,768]{1,0:T(8,128)(2,1)S(1)}, bf16[256,768]{1,0:T(8,128)(2,1)S(1)}, u32[]{:S(2)}, u32[]{:S(2)}) collective-permute-start(bf16[256,768]{1,0:T(8,128)(2,1)S(1)} %copy-done.2), channel_id=1, source_target_pairs={{0,1},{1,0},{2,3},{3,2},{4,5},{5,4},{6,7},{7,6},{8,9},{9,8},{10,11... | collective-permute-start | bytes 1179656 | tf_op jit(solution)/shard_map/ppermute | solution.py:1006
  177.2 18.0 %collective-permute-start.20 = (bf16[8,96,384]{2,1,0:T(8,128)(2,1)}, bf16[8,96,384]{2,1,0:T(8,128)(2,1)S(1)}, u32[]{:S(2)}, u32[]{:S(2)}) collective-permute-start(bf16[8,96,384]{2,1,0:T(8,128)(2,1)} %get-tuple-element.211), channel_id=1, source_target_pairs={{0,2},{1,3},{2,0},{3,1},{4,6},{5,7},{6,4},{7,5},{8,10},{9,11},{10,... | collective-permute-start | bytes 1769480 | tf_op jit(solution)/shard_map/ppermute | solution.py:1254
  178.6 16.6 %collective-permute-start.21 = (bf16[8,96,384]{2,1,0:T(8,128)(2,1)}, bf16[8,96,384]{2,1,0:T(8,128)(2,1)S(1)}, u32[]{:S(2)}, u32[]{:S(2)}) collective-permute-start(bf16[8,96,384]{2,1,0:T(8,128)(2,1)} %get-tuple-element.200.refs_12_), channel_id=1, source_target_pairs={{0,4},{1,5},{2,6},{3,7},{4,0},{5,1},{6,2},{7,3},{8,12},{9,13},{10,... | collective-permute-start | bytes 1769480 | tf_op jit(solution)/shard_map/ppermute | solution.py:1254
  199.6 16.6 %collective-permute-start.23 = (bf16[4,96,384]{2,1,0:T(8,128)(2,1)}, bf16[4,96,384]{2,1,0:T(8,128)(2,1)S(1)}, u32[]{:S(2)}, u32[]{:S(2)}) collective-permute-start(bf16[4,96,384]{2,1,0:T(8,128)(2,1)} %get-tuple-element.221), channel_id=1, source_target_pairs={{0,4},{1,5},{2,6},{3,7},{4,0},{5,1},{6,2},{7,3},{8,12},{9,13},{10,... | collective-permute-start | bytes 884744 | tf_op jit(solution)/shard_map/ppermute | solution.py:1254
  201.0 15.3 %collective-permute-start.24 = (bf16[4,96,384]{2,1,0:T(8,128)(2,1)}, bf16[4,96,384]{2,1,0:T(8,128)(2,1)S(1)}, u32[]{:S(2)}, u32[]{:S(2)}) collective-permute-start(bf16[4,96,384]{2,1,0:T(8,128)(2,1)} %get-tuple-element.213.refs_19_), channel_id=1, source_target_pairs={{0,2},{1,3},{2,0},{3,1},{4,6},{5,7},{6,4},{7,5},{8,10},{9,11},{10,... | collective-permute-start | bytes 884744 | tf_op jit(solution)/shard_map/ppermute | solution.py:1254
  219.4 24.7 %collective-permute-start.28 = (bf16[96,768]{1,0:T(8,128)(2,1)}, bf16[96,768]{1,0:T(8,128)(2,1)S(1)}, u32[]{:S(2)}, u32[]{:S(2)}) collective-permute-start(bf16[96,768]{1,0:T(8,128)(2,1)} %get-tuple-element.228), channel_id=1, source_target_pairs={{0,8},{1,9},{2,10},{3,11},{4,12},{5,13},{6,14},{7,15},{8,0},{9,1},... | collective-permute-start | bytes 442376 | tf_op jit(solution)/shard_map/ppermute | solution.py:1254
  223.1 21.0 %collective-permute-start.29 = (bf16[96,768]{1,0:T(8,128)(2,1)}, bf16[96,768]{1,0:T(8,128)(2,1)S(1)}, u32[]{:S(2)}, u32[]{:S(2)}) collective-permute-start(bf16[96,768]{1,0:T(8,128)(2,1)} %get-tuple-element.229), channel_id=1, source_target_pairs={{0,16},{1,17},{2,18},{3,19},{4,20},{5,21},{6,22},{7,23},{8,24},{9,... | collective-permute-start | bytes 442376 | tf_op jit(solution)/shard_map/ppermute | solution.py:1254
  224.4 19.8 %collective-permute-start.30 = (bf16[96,768]{1,0:T(8,128)(2,1)}, bf16[96,768]{1,0:T(8,128)(2,1)S(1)}, u32[]{:S(2)}, u32[]{:S(2)}) collective-permute-start(bf16[96,768]{1,0:T(8,128)(2,1)} %get-tuple-element.230.refs_16_), channel_id=1, source_target_pairs={{0,24},{1,25},{2,26},{3,27},{4,28},{5,29},{6,30},{7,31},{8,16},{9,... | collective-permute-start | bytes 442376 | tf_op jit(solution)/shard_map/ppermute | solution.py:1254
  246.8 209.0 %all-gather.7.cloned.1.call-start = ((), (), s32[]{:S(2)}) async-start(), calls=%async_computation.1 | async-start | bytes 8110080 | tf_op jit(solution)/shard_map/all_gather | solution.py:1323
  246.8 14.7 %collective-permute-start.34 = (bf16[1024,768]{1,0:T(8,128)(2,1)}, bf16[1024,768]{1,0:T(8,128)(2,1)S(1)}, u32[]{:S(2)}, u32[]{:S(2)}) collective-permute-start(bf16[1024,768]{1,0:T(8,128)(2,1)} %get-tuple-element.236), channel_id=1, source_target_pairs={{0,1},{1,0},{2,3},{3,2},{4,5},{5,4},{6,7},{7,6},{8,9},{9,8},{10,11... | collective-permute-start | bytes 4718600 | tf_op jit(solution)/shard_map/ppermute | solution.py:1006
  246.9 14.6 %collective-permute-start.35 = (bf16[256,768]{1,0:T(8,128)(2,1)S(1)}, bf16[256,768]{1,0:T(8,128)(2,1)S(1)}, u32[]{:S(2)}, u32[]{:S(2)}) collective-permute-start(bf16[256,768]{1,0:T(8,128)(2,1)S(1)} %copy-done.4), channel_id=1, source_target_pairs={{0,1},{1,0},{2,3},{3,2},{4,5},{5,4},{6,7},{7,6},{8,9},{9,8},{10,11... | collective-permute-start | bytes 1179656 | tf_op jit(solution)/shard_map/ppermute | solution.py:1006
  271.5 28.5 %collective-permute-start.36 = (bf16[8,160,384]{2,1,0:T(8,128)(2,1)}, bf16[8,160,384]{2,1,0:T(8,128)(2,1)S(1)}, u32[]{:S(2)}, u32[]{:S(2)}) collective-permute-start(bf16[8,160,384]{2,1,0:T(8,128)(2,1)} %get-tuple-element.246), channel_id=1, source_target_pairs={{0,2},{1,3},{2,0},{3,1},{4,6},{5,7},{6,4},{7,5},{8,10},{9,11},{10,... | collective-permute-start | bytes 2949128 | tf_op jit(solution)/shard_map/ppermute | solution.py:1254
  272.6 27.5 %collective-permute-start.37 = (bf16[8,160,384]{2,1,0:T(8,128)(2,1)}, bf16[8,160,384]{2,1,0:T(8,128)(2,1)S(1)}, u32[]{:S(2)}, u32[]{:S(2)}) collective-permute-start(bf16[8,160,384]{2,1,0:T(8,128)(2,1)} %get-tuple-element.247.refs_12_), channel_id=1, source_target_pairs={{0,4},{1,5},{2,6},{3,7},{4,0},{5,1},{6,2},{7,3},{8,12},{9,13},{10,... | collective-permute-start | bytes 2949128 | tf_op jit(solution)/shard_map/ppermute | solution.py:1254
  306.1 15.9 %collective-permute-start.38 = (bf16[4,160,384]{2,1,0:T(8,128)(2,1)}, bf16[4,160,384]{2,1,0:T(8,128)(2,1)S(1)}, u32[]{:S(2)}, u32[]{:S(2)}) collective-permute-start(bf16[4,160,384]{2,1,0:T(8,128)(2,1)} %get-tuple-element.258), channel_id=1, source_target_pairs={{0,4},{1,5},{2,6},{3,7},{4,0},{5,1},{6,2},{7,3},{8,12},{9,13},{10,... | collective-permute-start | bytes 1474568 | tf_op jit(solution)/shard_map/ppermute | solution.py:1254
  325.9 30.6 %collective-permute-start.43 = (bf16[160,768]{1,0:T(8,128)(2,1)}, bf16[160,768]{1,0:T(8,128)(2,1)S(1)}, u32[]{:S(2)}, u32[]{:S(2)}) collective-permute-start(bf16[160,768]{1,0:T(8,128)(2,1)} %get-tuple-element.270), channel_id=1, source_target_pairs={{0,8},{1,9},{2,10},{3,11},{4,12},{5,13},{6,14},{7,15},{8,0},{9,1},... | collective-permute-start | bytes 737288 | tf_op jit(solution)/shard_map/ppermute | solution.py:1254
  330.0 26.5 %collective-permute-start.44 = (bf16[160,768]{1,0:T(8,128)(2,1)}, bf16[160,768]{1,0:T(8,128)(2,1)S(1)}, u32[]{:S(2)}, u32[]{:S(2)}) collective-permute-start(bf16[160,768]{1,0:T(8,128)(2,1)} %get-tuple-element.271), channel_id=1, source_target_pairs={{0,16},{1,17},{2,18},{3,19},{4,20},{5,21},{6,22},{7,23},{8,24},{9,... | collective-permute-start | bytes 737288 | tf_op jit(solution)/shard_map/ppermute | solution.py:1254
  334.0 22.5 %collective-permute-start.45 = (bf16[160,768]{1,0:T(8,128)(2,1)}, bf16[160,768]{1,0:T(8,128)(2,1)S(1)}, u32[]{:S(2)}, u32[]{:S(2)}) collective-permute-start(bf16[160,768]{1,0:T(8,128)(2,1)} %get-tuple-element.259.refs_19_), channel_id=1, source_target_pairs={{0,24},{1,25},{2,26},{3,27},{4,28},{5,29},{6,30},{7,31},{8,16},{9,... | collective-permute-start | bytes 737288 | tf_op jit(solution)/shard_map/ppermute | solution.py:1254
  367.0 14.2 %collective-permute-start.46 = (bf16[8,64,384]{2,1,0:T(8,128)(2,1)}, bf16[8,64,384]{2,1,0:T(8,128)(2,1)S(1)}, u32[]{:S(2)}, u32[]{:S(2)}) collective-permute-start(bf16[8,64,384]{2,1,0:T(8,128)(2,1)} %get-tuple-element.277), channel_id=1, source_target_pairs={{0,2},{1,3},{2,0},{3,1},{4,6},{5,7},{6,4},{7,5},{8,10},{9,11},{10,... | collective-permute-start | bytes 1179656 | tf_op jit(solution)/shard_map/ppermute | solution.py:1254
  417.5 17.0 %collective-permute-start.54 = (bf16[64,768]{1,0:T(8,128)(2,1)}, bf16[64,768]{1,0:T(8,128)(2,1)S(1)}, u32[]{:S(2)}, u32[]{:S(2)}) collective-permute-start(bf16[64,768]{1,0:T(8,128)(2,1)} %shard_map.245.refs_0_.refs_4_), channel_id=1, source_target_pairs={{0,16},{1,17},{2,18},{3,19},{4,20},{5,21},{6,22},{7,23},{8,24},{9,... | collective-permute-start | bytes 294920 | tf_op jit(solution)/shard_map/ppermute | solution.py:1254
  418.9 15.7 %collective-permute-start.53 = (bf16[64,768]{1,0:T(8,128)(2,1)}, bf16[64,768]{1,0:T(8,128)(2,1)S(1)}, u32[]{:S(2)}, u32[]{:S(2)}) collective-permute-start(bf16[64,768]{1,0:T(8,128)(2,1)} %shard_map.245.refs_0_.refs_4_), channel_id=1, source_target_pairs={{0,8},{1,9},{2,10},{3,11},{4,12},{5,13},{6,14},{7,15},{8,0},{9,1},... | collective-permute-start | bytes 294920 | tf_op jit(solution)/shard_map/ppermute | solution.py:1254
  (112 other events, 520.1 us)
Sparse Core Ops, SparseCore 0:
  246.9 70.9 all-gather.4
  359.6 89.3 all-gather.6
